TPU v7x, 32 devices: a whole 2x2x4 slice. The times are simulated.
32 devices in a mesh: group: 8 (over y, x, core), band: 4 (over z).
Axes of the slice: x: 2, y: 2, z: 4, core: 2. Of those that a mesh axis runs over, the one named last changes fastest.
Arguments:
- station_rows: int32 [8, 96, 128], P('group', 'band'), may hold values from 0 to 3
- station_lons: int32 [8, 96, 128], P('group', 'band'), may hold values from 0 to 1439
- station_obs: float32 [8, 96, 128], P('group', 'band'), may hold values from -6 to 6
- station_live: int32 [8, 96, 128], P('group', 'band'), may hold values 0 or 1
- block_band: int32 [8, 96, 1], P('group', 'band'), may hold values from 0 to 3; in each aligned block of 24 rows (0 to 23, 24 to 47, ..., all dimensions but the last counted through in order) at most 12 rows name the same one
- truth_field: float32 [8, 16, 1440], P('group', 'band'), may hold values from -6 to 6
- length_scales: float32 [4], replicated, may hold values from 1.5 to 6
- w_in: bfloat16 [3, 3, 32, 8], replicated, may hold values from -0.75 to 0.75
- w_down: bfloat16 [4, 4, 32, 32], replicated, may hold values from -0.25 to 0.25
- w_mid: bfloat16 [3, 3, 32, 32], replicated, may hold values from -0.375 to 0.375
- w_up: bfloat16 [3, 3, 32, 64], replicated, may hold values from -0.25 to 0.25
- w_head: bfloat16 [2, 32], replicated, may hold values from -1 to 1
Outputs:
- mean_field: float32 [8, 16, 1440], P('group', 'band')
- grad_in: float32 [3, 3, 32, 8], replicated
- grad_down: float32 [4, 4, 32, 32], replicated
- grad_mid: float32 [3, 3, 32, 32], replicated
- grad_up: float32 [3, 3, 32, 64], replicated
- grad_head: float32 [2, 32], replicated
Inputs may be any that keep to these rules, and one draw needn't show every extreme that they name: `block_band`: among the 24 blocks of one device no band is named by more than 12 blocks, and that number is reached.
All inputs are finite; a program needn't handle non-finite values. No bound on the sum of `station_live` on one device may be relied on, other than what follows from the above.
Results may differ from a plain program's by a relative error of at most 0.0025.
The roundings to bfloat16 on the way count: a program that leaves them out, or rounds other values in their place, can miss the bound.
Values may be sent and summed in bfloat16 or wider, within the bound.
No kernel may reach another device: no remote copies, remote signals or barrier semaphores. Data moves between devices by JAX's collectives and lax.ppermute only.
A program may use at most 64 MiB of HBM per device.

v0:
```python
import functools

import jax
import jax.numpy as jnp
import numpy as np
from jax import lax
from jax.experimental import pallas as pl
from jax.experimental.pallas import tpu as pltpu
from jax.sharding import PartitionSpec as P

LANES = 128
HALO = 64
REACH = 128
ROWS_BAND = 4
FAR = -1.0e6
F32 = jnp.float32
BF16 = jnp.bfloat16


def looped(count, step, body):
    step = min(step, count)
    if count == step:
        for index in range(count):
            body(index)
    else:

        def turn(outer, carry):
            for inner in range(step):
                body(outer * step + inner)
            return carry

        lax.fori_loop(0, count // step, turn, 0)


def dot(first, second):
    return jnp.dot(first, second, preferred_element_type=F32)


def dot_lanes(first, second):
    return lax.dot_general(first, second, (((1,), (1,)), ((), ())), preferred_element_type=F32)


def rolled(values, shift):
    width = values.shape[-1]
    return pltpu.roll(values, shift % width, values.ndim - 1)


def four_shifts(even, odd):
    return jnp.concatenate([rolled(odd, 1), even, odd, rolled(even, -1)], axis=0)


def three_shifts(values, width):
    return jnp.concatenate([rolled(values, width), values, rolled(values, -width)], axis=0)


def sigmoid(values):
    return 1.0 / (1.0 + jnp.exp(-values))


def silu(values):
    return values * sigmoid(values)


def silu_slope(values):
    squash = sigmoid(values)
    return squash * (1.0 + values * (1.0 - squash))


def split_three(values):
    high = values.astype(BF16).astype(F32)
    rest = values - high
    middle = rest.astype(BF16).astype(F32)
    return high, middle, rest - middle


def network_kernel(sizes, *refs):
    n_band, n_blocks, own, lon_count = sizes
    window = own + 2 * HALO
    half = window // 2
    rows = ROWS_BAND * n_band
    coarse = rows // 2
    hist_tiles = (window + 2 * REACH) // LANES
    own_tiles = own // LANES
    pays = refs[:n_band]
    (scales, w1, wd, wm, wu, wh, wht, wf, wmf, wbd) = refs[n_band : n_band + 10]
    grads_out, mean_out = refs[n_band + 10 : n_band + 12]
    (
        bands, hist, table, zf, p1, zj, p2, z2, p3, p4, h4, truth, mean_split,
        gs, gp4m, gj, gp3m, zg3, gp2m, zg2, gp1m, hi_pos, lo_pos,
        acc_up, acc_down, acc_mid, acc_in, acc_head,
    ) = refs[n_band + 12 :]

    me = lax.axis_index("band")
    cell_count = float(rows * lon_count)

    def iota(shape, dim):
        return lax.broadcasted_iota(jnp.int32, shape, dim)

    for source in range(n_band):
        pltpu.sync_copy(pays[source].at[pl.ds(3 * n_blocks, 8)], bands.at[source])

    hist[...] = jnp.zeros_like(hist)
    start = (me * own - HALO - REACH).astype(F32)
    for source in range(n_band):
        lon = pays[source][n_blocks : 2 * n_blocks]
        place = lon - start
        place = jnp.where(place < 0.0, place + lon_count, place)
        place = jnp.where(place < 0.0, place + lon_count, place)
        place = jnp.where(place >= lon_count, place - lon_count, place)
        tile = jnp.floor(place * (1.0 / LANES))
        hi_pos[source] = tile
        lo_pos[source] = place - tile * LANES

    m_index = iota((32, 1), 0)
    row_of = (m_index // 8).astype(F32)
    scale_of = (m_index % 8) // 2
    kind_of = m_index % 2
    spread = jnp.where(
        scale_of == 0, scales[0], jnp.where(scale_of == 1, scales[1], jnp.where(scale_of == 2, scales[2], scales[3]))
    )
    rate = -0.5 / (spread * spread)
    lane_iota = iota((LANES, LANES), 0).astype(F32)

    for source in range(n_band):

        def one_block(block, source=source):
            at_row = pays[source][pl.ds(block, 1), :]
            observed = pays[source][pl.ds(2 * n_blocks + block, 1), :]
            high = hi_pos[source, pl.ds(block, 1), :]
            low = lo_pos[source, pl.ds(block, 1), :]
            gap = row_of - at_row
            left = jnp.exp(gap * gap * rate) * jnp.where(kind_of == 0, 1.0, observed)
            spread_left = jnp.concatenate(
                [jnp.where(high == float(tile), left, 0.0) for tile in range(hist_tiles)], axis=0
            ).astype(BF16)
            one_hot = jnp.where(lane_iota == low, 1.0, 0.0).astype(BF16)
            band = bands[source, 0, block].astype(jnp.int32)
            hist[band] = hist[band] + dot_lanes(spread_left, one_hot)

        looped(n_blocks, 4, one_block)

    place_in = iota((4 * LANES, 2 * LANES), 0)
    place_out = iota((4 * LANES, 2 * LANES), 1)
    distance = (place_in - (REACH + 2 * (place_out % LANES) + place_out // LANES)).astype(F32)
    squared = distance * distance
    for scale in range(4):
        table[scale] = jnp.exp(squared * (-0.5 / (scales[scale] * scales[scale]))).astype(BF16)
    all_rows = 32 * n_band
    channel = iota((all_rows, 1), 0) % 8
    feats = []
    for chunk in range(half // LANES):
        tiles = [
            hist[:, (2 * chunk + t) * 32 : (2 * chunk + t + 1) * 32, :].reshape(all_rows, LANES)
            for t in range(4)
        ]
        cells = jnp.concatenate(tiles, axis=1)
        high = cells.astype(BF16)
        low = (cells - high.astype(F32)).astype(BF16)
        total = None
        for scale in range(4):
            keep = (channel // 2 == scale).astype(F32).astype(BF16)
            part = dot(high * keep, table[scale]) + dot(low * keep, table[scale])
            total = part if total is None else total + part
        below = pltpu.roll(total, 1, 0)
        density = jnp.where(channel % 2 == 0, total, below)
        feats.append(total / (1.0 + density))
    even = jnp.concatenate([f[:, :LANES] for f in feats], axis=1)
    odd = jnp.concatenate([f[:, LANES:] for f in feats], axis=1)
    odd_before = rolled(odd, 1)
    even_after = rolled(even, -1)
    for edge in (0, rows + 1):
        zf[edge] = jnp.zeros((32, half), BF16)
        zj[edge] = jnp.zeros((256, half), BF16)
        gs[edge] = jnp.zeros((128, half), BF16)
        gp4m[edge] = jnp.zeros((64, half), BF16)
        gp1m[edge] = jnp.zeros((64, half), BF16)
    for edge in (0, coarse + 1):
        zg2[edge] = jnp.zeros((96, half), BF16)
        gp2m[edge] = jnp.zeros((32, half), BF16)
    for edge in (0, coarse // 2 + 1):
        for par in range(2):
            z2[par, edge] = jnp.zeros((96, half), BF16)
            zg3[par, edge] = jnp.zeros((96, half), BF16)
            gp3m[par, edge] = jnp.zeros((32, half), BF16)
    for row in range(rows):
        pick = slice(row * 8, row * 8 + 8)
        zf[row + 1] = jnp.concatenate(
            [odd_before[pick], even[pick], odd[pick], even_after[pick]], axis=0
        ).astype(BF16)

    fine_iota = iota((2 * LANES, 2 * LANES), 0)
    part_iota = iota((2 * LANES, 2 * LANES), 1)
    parting = (fine_iota == 2 * (part_iota % LANES) + part_iota // LANES).astype(F32).astype(BF16)
    chunks = window // (2 * LANES)
    for source in range(n_band):
        at = lax.rem(me - source + n_band, n_band)
        pieces = []
        for chunk in range(2):
            if chunk < chunks:
                tiles = [
                    pays[source][pl.ds(3 * n_blocks + 8 + (me * own_tiles + 2 * chunk + t) * ROWS_BAND, ROWS_BAND), :]
                    for t in range(2)
                ]
                pieces.append(jnp.concatenate(tiles, axis=1))
            else:
                pieces.append(jnp.zeros((ROWS_BAND, 2 * LANES), F32))
        stacked = jnp.concatenate(split_three(jnp.concatenate(pieces, axis=0)) + (jnp.zeros((8, 2 * LANES), F32),), axis=0)
        parted = dot(stacked.astype(BF16), parting)
        parted = parted[0:8] + parted[8:16] + parted[16:24]
        for chunk in range(chunks):
            for phase in range(2):
                truth[at, phase * 4 : phase * 4 + 4, chunk * LANES : (chunk + 1) * LANES] = parted[
                    chunk * 4 : chunk * 4 + 4, phase * LANES : (phase + 1) * LANES
                ]

    def first(row):
        pre = dot(w1[...], zf[pl.ds(row, 3)].reshape(96, half))
        p1[row] = pre
        hidden = silu(pre)
        zj[row + 1, 128:256, :] = four_shifts(hidden[:32], hidden[32:]).astype(BF16)

    looped(rows, 4, first)

    def second(index):
        for par in range(2):
            row = 2 * index + par
            pre = dot(wd[...], zj[pl.ds(2 * row, 4), 128:256, :].reshape(512, half))
            p2[row] = pre
            z2[par, index + 1] = three_shifts(silu(pre), 2).astype(BF16)

    looped(coarse // 2, 4, second)

    def third(index):
        for par in range(2):
            row = 2 * index + par
            pre = dot(wm[...], z2[par, pl.ds(index, 3)].reshape(288, half))
            p3[row] = pre
            hidden = silu(pre)
            wide = four_shifts(hidden, hidden).astype(BF16)
            zj[2 * row + 1, 0:128, :] = wide
            zj[2 * row + 2, 0:128, :] = wide

    looped(coarse // 2, 4, third)

    def fourth(row):
        pre = dot(wu[...], zj[pl.ds(row, 3)].reshape(768, half))
        p4[row] = pre
        h4[row] = silu(pre).astype(BF16)

    looped(rows, 4, fourth)

    own_cells = jnp.clip(lon_count - me * own, 0, own) // 2
    place = iota((1, half), 1)
    mask = ((place >= HALO // 2) & (place < HALO // 2 + own_cells)).astype(F32)
    acc_head[...] = jnp.zeros_like(acc_head)

    def head(group):
        hidden = h4[pl.ds(4 * group, 4)].reshape(256, half)
        out = dot(wh[...], hidden)
        mean = out[:8]
        raw = out[8:]
        decay = jnp.exp(-jnp.abs(raw))
        noise = 0.1 + (jnp.maximum(raw, 0.0) + jnp.log1p(decay))
        error = (mean - truth[group]) / noise
        weight = 1.0 / (noise * cell_count)
        grad_mean = error * weight
        grad_raw = (1.0 - error * error) * weight * sigmoid(raw)
        grad_out = jnp.concatenate([grad_mean, grad_raw], axis=0)
        grad_bf = grad_out.astype(BF16)
        acc_head[...] += dot_lanes((grad_out * mask).astype(BF16), hidden)
        back = dot(wht[...], grad_bf)
        pre = p4[pl.ds(4 * group, 4)].reshape(256, half)
        grad = back * silu_slope(pre)
        for row in range(4):
            mine = grad[row * 64 : row * 64 + 64]
            gp4m[4 * group + row + 1] = (mine * mask).astype(BF16)
            gs[4 * group + row + 1] = four_shifts(mine[:32], mine[32:]).astype(BF16)
        parts = split_three(jnp.concatenate([mean[0:4], mean[4:8]], axis=1))
        mean_split[group] = jnp.concatenate(
            parts + (jnp.zeros((4, 2 * half), F32),), axis=0
        ).astype(BF16)

    looped(n_band, 1, head)

    target = iota((2 * half, own), 1) + HALO
    origin = iota((2 * half, own), 0)
    joining = (target == 2 * (origin % half) + origin // half).astype(F32).astype(BF16)
    joined = dot(mean_split[...].reshape(16 * n_band, 2 * half), joining)
    for band in range(n_band):
        four = joined[16 * band : 16 * band + 8] + joined[16 * band + 8 : 16 * band + 16]
        four = four[0:4] + four[4:8]
        for tile in range(own_tiles):
            mean_out[band, tile] = four[:, tile * LANES : (tile + 1) * LANES]

    def join_back(index):
        for par in range(2):
            row = 2 * index + par
            total = None
            for side in range(2):
                fine = 2 * row + side
                back = dot(wf[...], gs[pl.ds(fine, 3)].reshape(384, half)).astype(BF16)
                gj[fine] = back[64:]
                up = back[:64].astype(F32)
                part = up[:32] + up[32:]
                total = part if total is None else total + part
            grad = total * silu_slope(p3[row])
            gp3m[par, index + 1] = (grad * mask).astype(BF16)
            zg3[par, index + 1] = three_shifts(grad, 2).astype(BF16)

    looped(coarse // 2, 2, join_back)

    def mid_back(index):
        for par in range(2):
            row = 2 * index + par
            back = dot(wmf[...], zg3[par, pl.ds(index, 3)].reshape(288, half))
            grad = back * silu_slope(p2[row])
            gp2m[row + 1] = (grad * mask).astype(BF16)
            zg2[row + 1] = three_shifts(grad, 1).astype(BF16)

    looped(coarse // 2, 4, mid_back)

    def down_back(row):
        back = dot(wbd[...], zg2[pl.ds(row, 3)].reshape(288, half))
        for side in range(2):
            fine = 2 * row + side
            grad = (back[64 * side : 64 * side + 64] + gj[fine].astype(F32)) * silu_slope(p1[fine])
            gp1m[fine + 1] = (grad * mask).astype(BF16)

    looped(coarse, 4, down_back)

    acc_up[...] = jnp.zeros_like(acc_up)
    acc_down[...] = jnp.zeros_like(acc_down)
    acc_mid[...] = jnp.zeros_like(acc_mid)
    acc_in[...] = jnp.zeros_like(acc_in)

    def weights_fine(row):
        acc_up[...] += dot_lanes(gp4m[pl.ds(row, 3)].reshape(192, half), zj[row + 1])
        acc_in[...] += dot_lanes(gp1m[pl.ds(row, 3)].reshape(192, half), zf[row + 1])

    looped(rows, 4, weights_fine)

    def weights_coarse(index):
        for par in range(2):
            row = 2 * index + par
            acc_mid[...] += dot_lanes(gp3m[par, pl.ds(index, 3)].reshape(96, half), z2[par, index + 1])
            acc_down[...] += dot_lanes(
                gp2m[pl.ds(row, 3)].reshape(96, half),
                zj[pl.ds(2 * row + 1, 2), 128:256, :].reshape(256, half),
            )

    looped(coarse // 2, 4, weights_coarse)

    up = acc_up[...]
    inner = acc_in[...]
    for step in range(3):
        first_up, second_up = up[64 * step : 64 * step + 32], up[64 * step + 32 : 64 * step + 64]
        first_in, second_in = inner[64 * step : 64 * step + 32], inner[64 * step + 32 : 64 * step + 64]
        at = slice(32 * step, 32 * step + 32)
        for part in range(2):
            cols = slice(128 * part, 128 * part + 128)
            grads_out[96 * part + 32 * step : 96 * part + 32 * step + 32, :] = first_up[:, cols] + rolled(
                second_up[:, cols], -32
            )
        grads_out[at, 96:120] = first_in[:, 0:24] + second_in[:, 8:32]
    down = acc_down[...]
    for tap, (step, side) in enumerate(((2, 1), (1, 0), (1, 1), (0, 0))):
        grads_out[192 + 32 * tap : 224 + 32 * tap, :] = down[
            32 * step : 32 * step + 32, 128 * side : 128 * side + 128
        ]
    grads_out[320:416, 0:96] = acc_mid[...]
    k_index = iota((16, 256), 0) % 8
    c_index = iota((16, 256), 1) // 32
    same = (k_index % 4 == c_index // 2) & (k_index // 4 == c_index % 2)
    heads = jnp.where(same, acc_head[...], 0.0)
    for kind in range(2):
        line = jnp.sum(heads[8 * kind : 8 * kind + 8], axis=0, keepdims=True)
        line = line[:, :128] + line[:, 128:]
        line = line + rolled(line, 64)
        line = line + rolled(line, 32)
        grads_out[320 + kind : 321 + kind, 96:128] = line[:, 96:128]


def unpack_kernel(sizes, *refs):
    n_band, own, lon_count = sizes
    low, high = refs[0], refs[1]
    means = refs[2 : 2 + n_band]
    mean_out, grad_in, grad_down, grad_mid, grad_up, grad_head, wide = refs[2 + n_band :]
    me = lax.axis_index("band")
    core = lax.rem(lax.axis_index("group"), 2)
    own_tiles = own // LANES
    first = jnp.where(core == 0, low[...], high[...])
    second = jnp.where(core == 0, high[...], low[...])
    both = jnp.concatenate([first, second], axis=0)
    lane = lax.broadcasted_iota(jnp.int32, (96, LANES), 1)
    part_a, part_b = both[0:96], both[96:192]
    mid = both[320:416]
    for tap_col in range(3):
        ups = jnp.where(lane < 32, rolled(part_a, -32 * tap_col), rolled(part_b, 32 - 32 * tap_col))
        ins = rolled(part_a, -96 - 8 * tap_col)
        mids = rolled(mid, -32 * tap_col)
        for tap_row in range(3):
            at = slice(32 * (2 - tap_row), 32 * (2 - tap_row) + 32)
            grad_up[tap_row, tap_col] = ups[at, 0:64]
            grad_in[tap_row, tap_col] = ins[at, 0:8]
            grad_mid[tap_row, tap_col] = mids[at, 0:32]
    down = both[192:320]
    for tap_col in range(4):
        downs = rolled(down, -32 * tap_col)
        for tap_row in range(4):
            grad_down[tap_row, tap_col] = downs[32 * tap_row : 32 * tap_row + 32, 0:32]
    grad_head[...] = rolled(mid[0:8], -96)[0:2, 0:32]
    for shift in range(n_band):
        origin = lax.rem(me - shift + n_band, n_band)
        for tile in range(own_tiles):
            at = pl.multiple_of((origin * own_tiles + tile) * LANES, LANES)
            wide[:, pl.ds(at, LANES)] = means[shift][tile]
    mean_out[0] = wide[:, 0:lon_count]


def phased(taps):
    before = jnp.pad(taps, ((0, 0), (0, 0), (0, 1), (0, 0)))
    after = jnp.pad(taps, ((0, 0), (0, 0), (1, 0), (0, 0)))
    return jnp.stack([before, after])


def parted(taps, axis):
    first = lax.rev(lax.slice_in_dim(taps, 1, 4, 2, axis), (axis,))
    second = lax.rev(lax.slice_in_dim(taps, 0, 3, 2, axis), (axis,))
    at_end = [(0, 0)] * taps.ndim
    at_start = [(0, 0)] * taps.ndim
    at_end[axis] = (0, 1)
    at_start[axis] = (1, 0)
    return jnp.stack([jnp.pad(first, at_end), jnp.pad(second, at_start)])


def matrices(w_in, w_down, w_mid, w_up, w_head):
    w1 = phased(jnp.transpose(w_in, (2, 0, 1, 3))).reshape(64, 96)
    wd = jnp.transpose(w_down, (2, 0, 1, 3)).reshape(32, 512)
    wm = jnp.transpose(w_mid, (2, 0, 1, 3)).reshape(32, 288)
    up = jnp.transpose(w_up.reshape(3, 3, 32, 2, 32), (2, 0, 3, 1, 4)).reshape(32, 6, 3, 32)
    wu = phased(up).reshape(64, 768)
    sel = np.zeros((8, 8), np.float32)
    for phase in range(2):
        for row in range(4):
            sel[phase * 4 + row, row * 2 + phase] = 1.0
    wh = (jnp.asarray(sel, BF16)[None, :, :, None] * w_head[:, None, None, :]).reshape(16, 256)
    back = phased(jnp.transpose(w_up[::-1, ::-1], (3, 0, 1, 2)))
    wf = jnp.transpose(back.reshape(2, 2, 32, 384), (1, 0, 2, 3)).reshape(128, 384)
    wmf = jnp.transpose(w_mid[::-1, ::-1], (3, 0, 1, 2)).reshape(32, 288)
    taps = jnp.transpose(w_down, (3, 0, 1, 2))
    taps = parted(parted(taps, 1), 3)
    wbd = jnp.transpose(taps, (1, 0, 2, 3, 4, 5)).reshape(128, 288)
    return w1, wd, wm, wu, wh, wh.T, wf, wmf, wbd


def swapped(values, axis, count, bits):
    return lax.ppermute(values, axis, [(i, i ^ bits) for i in range(count)])


def shifted(values, axis, count, shift):
    return lax.ppermute(values, axis, [(i, (i + shift) % count) for i in range(count)])


def reduced(grads, mean_tiles, n_band, n_group):
    group = lax.axis_index("group")
    band = lax.axis_index("band")
    core, chip = group % 2, group // 2
    chips = n_group // 2
    tile_rows = mean_tiles.shape[1]
    half = grads.shape[0] // 2
    mine = lax.dynamic_slice_in_dim(grads, core * half, half, 0)
    theirs = lax.dynamic_slice_in_dim(grads, (1 - core) * half, half, 0)
    total = mine + swapped(theirs, "group", n_group, 1)
    share = half // chips
    kept = lax.dynamic_slice_in_dim(total, chip * share, share, 0)
    got = [
        swapped(lax.dynamic_slice_in_dim(total, (chip ^ k) * share, share, 0), "group", n_group, 2 * k)
        for k in range(1, chips)
    ]
    for piece in got:
        kept = kept + piece
    means = [lax.dynamic_index_in_dim(mean_tiles, band, 0, keepdims=False)]
    arrived = []
    for k in range(1, n_band):
        target = lax.rem(band + k, n_band)
        sent = jnp.concatenate([kept, lax.dynamic_index_in_dim(mean_tiles, target, 0, keepdims=False)])
        arrived.append(shifted(sent, "band", n_band, k))
    for piece in arrived:
        kept = kept + piece[:share]
        means.append(piece[share:])
    pieces = [(chip, kept)] + [
        (chip ^ k, swapped(kept, "group", n_group, 2 * k)) for k in range(1, chips)
    ]
    whole = jnp.zeros((chips, share, LANES), F32)
    for at, piece in pieces:
        whole = lax.dynamic_update_slice(whole, piece[None], (at, 0, 0))
    whole = whole.reshape(half, LANES)
    return whole, swapped(whole, "group", n_group, 1), means


def vmem(*shape, dtype=BF16):
    return pltpu.VMEM(shape, dtype)


def local(
    station_rows,
    station_lons,
    station_obs,
    station_live,
    block_band,
    truth_field,
    length_scales,
    w_in,
    w_down,
    w_mid,
    w_up,
    w_head,
):
    n_band = lax.axis_size("band")
    n_group = lax.axis_size("group")
    n_blocks = station_rows.shape[1]
    lon_count = truth_field.shape[2]
    own_tiles = -(-(-(-lon_count // LANES)) // n_band)
    own = own_tiles * LANES
    window = own + 2 * HALO
    half = window // 2
    rows = ROWS_BAND * n_band
    coarse = rows // 2
    hist_tiles = (window + 2 * REACH) // LANES

    field = truth_field[0]
    total_tiles = n_band * own_tiles + 1
    extended = jnp.concatenate(
        [field[:, lon_count - HALO :], field, field[:, : total_tiles * LANES - HALO - lon_count]], axis=1
    )
    truth_rows = jnp.transpose(extended.reshape(ROWS_BAND, total_tiles, LANES), (1, 0, 2)).reshape(-1, LANES)
    fill = -truth_rows.shape[0] % 8
    band_rows = jnp.zeros((8, LANES), F32).at[0, :n_blocks].set(block_band[0, :, 0].astype(F32))
    pay = jnp.concatenate(
        [
            station_rows[0].astype(F32),
            jnp.where(station_live[0] > 0, station_lons[0].astype(F32), FAR),
            station_obs[0],
            band_rows,
            jnp.pad(truth_rows, ((0, fill), (0, 0))),
        ]
    )
    pays = [pay] + [shifted(pay, "band", n_band, k) for k in range(1, n_band)]
    mats = matrices(w_in, w_down, w_mid, w_up, w_head)

    in_vmem = pl.BlockSpec(memory_space=pltpu.VMEM)
    in_smem = pl.BlockSpec(memory_space=pltpu.SMEM)
    grads, mean_tiles = pl.pallas_call(
        functools.partial(network_kernel, (n_band, n_blocks, own, lon_count)),
        out_shape=(
            jax.ShapeDtypeStruct((416, LANES), F32),
            jax.ShapeDtypeStruct((n_band, own_tiles, ROWS_BAND, LANES), F32),
        ),
        in_specs=[in_vmem] * n_band + [in_smem] + [in_vmem] * len(mats),
        out_specs=(in_vmem, in_vmem),
        scratch_shapes=[
            pltpu.SMEM((n_band, 8, LANES), F32),
            vmem(n_band, hist_tiles * 32, LANES, dtype=F32),
            vmem(4, 4 * LANES, 2 * LANES),
            vmem(rows + 2, 32, half),
            vmem(rows, 64, half, dtype=F32),
            vmem(rows + 2, 256, half),
            vmem(coarse, 32, half, dtype=F32),
            vmem(2, coarse // 2 + 2, 96, half),
            vmem(coarse, 32, half, dtype=F32),
            vmem(rows, 64, half, dtype=F32),
            vmem(rows, 64, half),
            vmem(n_band, 8, half, dtype=F32),
            vmem(n_band, 16, 2 * half),
            vmem(rows + 2, 128, half),
            vmem(rows + 2, 64, half),
            vmem(rows, 64, half),
            vmem(2, coarse // 2 + 2, 32, half),
            vmem(2, coarse // 2 + 2, 96, half),
            vmem(coarse + 2, 32, half),
            vmem(coarse + 2, 96, half),
            vmem(rows + 2, 64, half),
            vmem(n_band, n_blocks, LANES, dtype=F32),
            vmem(n_band, n_blocks, LANES, dtype=F32),
            vmem(192, 256, dtype=F32),
            vmem(96, 256, dtype=F32),
            vmem(96, 96, dtype=F32),
            vmem(192, 32, dtype=F32),
            vmem(16, 256, dtype=F32),
        ],
        compiler_params=pltpu.CompilerParams(vmem_limit_bytes=40 * 1024 * 1024),
    )(*pays, length_scales, *mats)

    low, high, means = reduced(grads, mean_tiles.reshape(n_band, own_tiles * ROWS_BAND, LANES), n_band, n_group)
    means = [piece.reshape(own_tiles, ROWS_BAND, LANES) for piece in means]
    return pl.pallas_call(
        functools.partial(unpack_kernel, (n_band, own, lon_count)),
        out_shape=(
            jax.ShapeDtypeStruct((1, ROWS_BAND, lon_count), F32),
            jax.ShapeDtypeStruct((3, 3, 32, 8), F32),
            jax.ShapeDtypeStruct((4, 4, 32, 32), F32),
            jax.ShapeDtypeStruct((3, 3, 32, 32), F32),
            jax.ShapeDtypeStruct((3, 3, 32, 64), F32),
            jax.ShapeDtypeStruct((2, 32), F32),
        ),
        in_specs=[in_vmem] * (2 + n_band),
        out_specs=(in_vmem,) * 6,
        scratch_shapes=[vmem(ROWS_BAND, n_band * own, dtype=F32)],
        compiler_params=pltpu.CompilerParams(vmem_limit_bytes=16 * 1024 * 1024),
    )(low, high, *means)


def solution(mesh):
    return jax.shard_map(
        local,
        mesh=mesh,
        in_specs=(
            P("group", "band", None),
            P("group", "band", None),
            P("group", "band", None),
            P("group", "band", None),
            P("group", "band", None),
            P("group", "band", None),
            P(),
            P(),
            P(),
            P(),
            P(),
            P(),
        ),
        out_specs=(P("group", "band", None), P(), P(), P(), P(), P()),
        check_vma=False,
    )
```

profile of v0, /device:TPU:0, one launch (start us, length us, event | category | flops | bytes accessed | tf_op | source)
XLA Modules:
  0.0 63.3 jit_solution(6396288620192802886)
XLA Ops:
  0.6 0.7 %slice.65 = f32[4,160]{1,0:T(4,128)S(1)} slice(f32[4,1440]{1,0:T(4,128)} %bitcast.87), slice={[0:4], [0:160]} | slice | bytes 5120 | tf_op jit(solution)/shard_map/slice | solution.py:534
  1.3 0.8 %slice.64 = f32[4,64]{1,0:T(4,128)S(1)} slice(f32[4,1440]{1,0:T(4,128)} %bitcast.88), slice={[0:4], [1376:1440]} | slice | bytes 2048 | tf_op jit(solution)/shard_map/slice | solution.py:534
  2.1 0.8 %concatenate.18 = f32[4,1664]{1,0:T(4,128)S(1)} concatenate(f32[4,64]{1,0:T(4,128)S(1)} %slice.64, f32[4,1440]{1,0:T(4,128)} %bitcast.89, f32[4,160]{1,0:T(4,128)S(1)} %slice.65), dimensions={1} | concatenate | bytes 53248 | tf_op jit(solution)/shard_map/concatenate | solution.py:533
  3.7 0.7 %copy-done.7 = s32[1,24,128]{2,1,0:T(8,128)S(1)} copy-done((s32[1,24,128]{2,1,0:T(8,128)S(1)}, s32[1,24,128]{2,1,0:T(8,128)}, u32[]{:S(2)}) %copy-start.7) | copy-done | bytes 12312
  4.4 3.1 %collective-permute-start = (f32[136,128]{1,0:T(8,128)S(1)}, f32[136,128]{1,0:T(8,128)S(1)}, u32[]{:S(2)}, u32[]{:S(2)}) collective-permute-start(f32[136,128]{1,0:T(8,128)S(1)} %pad_dynamic-update-slice_fusion.refs_0_), channel_id=1, source_target_pairs={{0,1},{1,2},{2,3},{3,0},{4,5},{5,6},{6,7},{7,4},{8,9},{9,10},{10,1... | collective-permute-start | bytes 208904 | tf_op jit(solution)/shard_map/ppermute | solution.py:461
  7.5 2.6 %collective-permute-start.1 = (f32[136,128]{1,0:T(8,128)S(1)}, f32[136,128]{1,0:T(8,128)S(1)}, u32[]{:S(2)}, u32[]{:S(2)}) collective-permute-start(f32[136,128]{1,0:T(8,128)S(1)} %pad_dynamic-update-slice_fusion.refs_0_), channel_id=1, source_target_pairs={{0,2},{1,3},{2,0},{3,1},{4,6},{5,7},{6,4},{7,5},{8,10},{9,11},{10,... | collective-permute-start | bytes 208904 | tf_op jit(solution)/shard_map/ppermute | solution.py:461
  10.1 1.3 %collective-permute-start.2 = (f32[136,128]{1,0:T(8,128)S(1)}, f32[136,128]{1,0:T(8,128)S(1)}, u32[]{:S(2)}, u32[]{:S(2)}) collective-permute-start(f32[136,128]{1,0:T(8,128)S(1)} %pad_dynamic-update-slice_fusion.refs_0_), channel_id=1, source_target_pairs={{0,3},{1,0},{2,1},{3,2},{4,7},{5,4},{6,5},{7,6},{8,11},{9,8},{10,9... | collective-permute-start | bytes 208904 | tf_op jit(solution)/shard_map/ppermute | solution.py:461
  11.6 0.9 %copy-done.1 = bf16[4,4,32,32]{3,2,1,0:T(8,128)(2,1)S(1)} copy-done((bf16[4,4,32,32]{3,2,1,0:T(8,128)(2,1)S(1)}, bf16[4,4,32,32]{3,2,1,0:T(8,128)(2,1)}, u32[]{:S(2)}) %copy-start.1) | copy-done | bytes 32792
  14.9 0.7 %copy-done.4 = bf16[3,3,32,8]{2,3,1,0:T(8,128)(2,1)S(1)} copy-done((bf16[3,3,32,8]{2,3,1,0:T(8,128)(2,1)S(1)}, bf16[3,3,32,8]{2,3,1,0:T(8,128)(2,1)}, u32[]{:S(2)}) %copy-start.4) | copy-done | bytes 4632
  17.1 0.7 %copy-done.3 = bf16[3,3,32,32]{3,2,1,0:T(8,128)(2,1)S(1)} copy-done((bf16[3,3,32,32]{3,2,1,0:T(8,128)(2,1)S(1)}, bf16[3,3,32,32]{3,2,1,0:T(8,128)(2,1)}, u32[]{:S(2)}) %copy-start.3) | copy-done | bytes 18456
  18.8 19.8 %shard_map.172 = (f32[416,128]{1,0:T(8,128)S(1)}, f32[4,3,4,128]{3,2,1,0:T(4,128)S(1)}) custom-call(f32[136,128]{1,0:T(8,128)S(1)} %pad_dynamic-update-slice_fusion.refs_0_, f32[136,128]{1,0:T(8,128)S(1)} %collective-permute-done.refs_1_, f32[136,128]{1,0:T(8,128)S(1)} %collective-permute-done.1.refs_2_, f32[136,128]{1,0:T(8,128)S(1)} %collective-permute-done.2.refs_3_, ...), custom_call_target="tpu_custom_call" | custom-call | tf_op jit(solution)/shard_map/pallas_call | solution.py:553
  38.7 1.2 %collective-permute-done.3 = f32[208,128]{1,0:T(8,128)S(1)} collective-permute-done((f32[208,128]{1,0:T(8,128)S(1)}, f32[208,128]{1,0:T(8,128)S(1)}, u32[]{:S(2)}, u32[]{:S(2)}) %collective-permute-start.3) | collective-permute-done | bytes 106528 | tf_op jit(solution)/shard_map/ppermute | solution.py:457
  40.0 1.6 %collective-permute-start.4 = (f32[52,128]{1,0:T(8,128)S(1)}, f32[52,128]{1,0:T(8,128)S(1)}, u32[]{:S(2)}, u32[]{:S(2)}) collective-permute-start(f32[52,128]{1,0:T(8,128)S(1)} %get-tuple-element.42), channel_id=1, source_target_pairs={{0,8},{4,12},{8,0},{12,4},{16,24},{20,28},{24,16},{28,20},{1,9},{5... | collective-permute-start | bytes 79880 | tf_op jit(solution)/shard_map/ppermute | solution.py:457
  41.5 1.5 %collective-permute-start.5 = (f32[52,128]{1,0:T(8,128)S(1)}, f32[52,128]{1,0:T(8,128)S(1)}, u32[]{:S(2)}, u32[]{:S(2)}) collective-permute-start(f32[52,128]{1,0:T(8,128)S(1)} %get-tuple-element.44), channel_id=1, source_target_pairs={{0,16},{4,20},{8,24},{12,28},{16,0},{20,4},{24,8},{28,12},{1,17},{... | collective-permute-start | bytes 79880 | tf_op jit(solution)/shard_map/ppermute | solution.py:457
  43.9 1.5 %collective-permute-done.5 = f32[52,128]{1,0:T(8,128)S(1)} collective-permute-done((f32[52,128]{1,0:T(8,128)S(1)}, f32[52,128]{1,0:T(8,128)S(1)}, u32[]{:S(2)}, u32[]{:S(2)}) %collective-permute-start.5) | collective-permute-done | bytes 26656 | tf_op jit(solution)/shard_map/ppermute | solution.py:457
  45.4 2.4 %collective-permute-done.6 = f32[52,128]{1,0:T(8,128)S(1)} collective-permute-done((f32[52,128]{1,0:T(8,128)S(1)}, f32[52,128]{1,0:T(8,128)S(1)}, u32[]{:S(2)}, u32[]{:S(2)}) %collective-permute-start.6) | collective-permute-done | bytes 26656 | tf_op jit(solution)/shard_map/ppermute | solution.py:457
  47.9 0.7 %collective-permute-start.7 = (f32[64,128]{1,0:T(8,128)S(1)}, f32[64,128]{1,0:T(8,128)S(1)}, u32[]{:S(2)}, u32[]{:S(2)}) collective-permute-start(f32[64,128]{1,0:T(8,128)S(1)} %get-tuple-element.47), channel_id=1, source_target_pairs={{0,1},{1,2},{2,3},{3,0},{4,5},{5,6},{6,7},{7,4},{8,9},{9,10},{10,1... | collective-permute-start | bytes 98312 | tf_op jit(solution)/shard_map/ppermute | solution.py:461
  48.9 2.8 %collective-permute-start.9 = (f32[64,128]{1,0:T(8,128)S(1)}, f32[64,128]{1,0:T(8,128)S(1)}, u32[]{:S(2)}, u32[]{:S(2)}) collective-permute-start(f32[64,128]{1,0:T(8,128)S(1)} %get-tuple-element.49), channel_id=1, source_target_pairs={{0,3},{1,0},{2,1},{3,2},{4,7},{5,4},{6,5},{7,6},{8,11},{9,8},{10,9... | collective-permute-start | bytes 98312 | tf_op jit(solution)/shard_map/ppermute | solution.py:461
  51.8 2.0 %collective-permute-done.7 = f32[64,128]{1,0:T(8,128)S(1)} collective-permute-done((f32[64,128]{1,0:T(8,128)S(1)}, f32[64,128]{1,0:T(8,128)S(1)}, u32[]{:S(2)}, u32[]{:S(2)}) %collective-permute-start.7) | collective-permute-done | bytes 32800 | tf_op jit(solution)/shard_map/ppermute | solution.py:461
  55.4 2.4 %collective-permute-start.12 = (f32[52,128]{1,0:T(8,128)S(1)}, f32[52,128]{1,0:T(8,128)S(1)}, u32[]{:S(2)}, u32[]{:S(2)}) collective-permute-start(f32[52,128]{1,0:T(8,128)S(1)} %get-tuple-element.35), channel_id=1, source_target_pairs={{0,24},{4,28},{8,16},{12,20},{16,8},{20,12},{24,0},{28,4},{1,25},{... | collective-permute-start | bytes 79880 | tf_op jit(solution)/shard_map/ppermute | solution.py:457
  58.7 1.4 %collective-permute-done.12 = f32[52,128]{1,0:T(8,128)S(1)} collective-permute-done((f32[52,128]{1,0:T(8,128)S(1)}, f32[52,128]{1,0:T(8,128)S(1)}, u32[]{:S(2)}, u32[]{:S(2)}) %collective-permute-start.12) | collective-permute-done | bytes 26656 | tf_op jit(solution)/shard_map/ppermute | solution.py:457
  60.3 1.2 %collective-permute-done.13.refs_1_ = f32[208,128]{1,0:T(8,128)S(1)} collective-permute-done((f32[208,128]{1,0:T(8,128)S(1)}, f32[208,128]{1,0:T(8,128)S(1)}, u32[]{:S(2)}, u32[]{:S(2)}) %collective-permute-start.13) | collective-permute-done | bytes 106528 | tf_op jit(solution)/shard_map/ppermute | solution.py:457
  61.5 1.0 %shard_map.173 = (f32[1,4,1440]{2,1,0:T(4,128)}, f32[3,3,32,8]{3,2,1,0:T(8,128)S(1)}, f32[4,4,32,32]{3,2,1,0:T(8,128)}, f32[3,3,32,32]{3,2,1,0:T(8,128)}, f32[3,3,32,64]{3,2,1,0:T(8,128)}, /*index=5*/f32[2,32]{1,0:T(2,128)}) custom-call(f32[208,128]{1,0:T(8,128)S(1)} %reshape.129.refs_0_, f32[208,128]{1,0:T(8,128)S(1)} %collective-permute-done.13.refs_1_, ...), custom_call_target="tpu_custom_call" | custom-call | tf_op jit(solution)/shard_map/pallas_call | solution.py:596
  62.5 0.7 %copy.45 = f32[3,3,32,8]{2,3,1,0:T(8,128)} copy(f32[3,3,32,8]{3,2,1,0:T(8,128)S(1)} %get-tuple-element.29) | data formatting | bytes 18432 | tf_op jit(solution)/shard_map/pallas_call | solution.py:596
  (105 shorter events, 9.5 us)
Async XLA Ops:
  3.0 0.7 %copy-start.5 = (s32[1,24,128]{2,1,0:T(8,128)S(1)}, s32[1,24,128]{2,1,0:T(8,128)}, u32[]{:S(2)}) copy-start(s32[1,24,128]{2,1,0:T(8,128)} %param.15) | copy-start | bytes 36868
  3.0 0.7 %copy-start.11 = (s32[1,24,1]{1,2,0:T(1,128)S(1)}, s32[1,24,1]{1,2,0:T(1,128)}, u32[]{:S(2)}) copy-start(s32[1,24,1]{1,2,0:T(1,128)} %param.19) | copy-start | bytes 292
  3.0 0.7 %copy-start.8 = (s32[1,24,128]{2,1,0:T(8,128)S(1)}, s32[1,24,128]{2,1,0:T(8,128)}, u32[]{:S(2)}) copy-start(s32[1,24,128]{2,1,0:T(8,128)} %param.18) | copy-start | bytes 36868
  3.7 0.7 %copy-start.7 = (s32[1,24,128]{2,1,0:T(8,128)S(1)}, s32[1,24,128]{2,1,0:T(8,128)}, u32[]{:S(2)}) copy-start(s32[1,24,128]{2,1,0:T(8,128)} %param.16) | copy-start | bytes 36868
  3.7 0.7 %copy-start.6 = (f32[1,24,128]{2,1,0:T(8,128)S(1)}, f32[1,24,128]{2,1,0:T(8,128)}, u32[]{:S(2)}) copy-start(f32[1,24,128]{2,1,0:T(8,128)} %param.17) | copy-start | bytes 36868
  4.4 7.1 %copy-start.2 = (bf16[3,3,32,64]{3,2,1,0:T(8,128)(2,1)S(1)}, bf16[3,3,32,64]{3,2,1,0:T(8,128)(2,1)}, u32[]{:S(2)}) copy-start(bf16[3,3,32,64]{3,2,1,0:T(8,128)(2,1)} %param.25) | copy-start | bytes 110596
  4.4 13.7 %collective-permute-start = (f32[136,128]{1,0:T(8,128)S(1)}, f32[136,128]{1,0:T(8,128)S(1)}, u32[]{:S(2)}, u32[]{:S(2)}) collective-permute-start(f32[136,128]{1,0:T(8,128)S(1)} %pad_dynamic-update-slice_fusion.refs_0_), channel_id=1, source_target_pairs={{0,1},{1,2},{2,3},{3,0},{4,5},{5,6},{6,7},{7,4},{8,9},{9,10},{10,1... | collective-permute-start | bytes 208904 | tf_op jit(solution)/shard_map/ppermute | solution.py:461
  7.5 10.6 %collective-permute-start.1 = (f32[136,128]{1,0:T(8,128)S(1)}, f32[136,128]{1,0:T(8,128)S(1)}, u32[]{:S(2)}, u32[]{:S(2)}) collective-permute-start(f32[136,128]{1,0:T(8,128)S(1)} %pad_dynamic-update-slice_fusion.refs_0_), channel_id=1, source_target_pairs={{0,2},{1,3},{2,0},{3,1},{4,6},{5,7},{6,4},{7,5},{8,10},{9,11},{10,... | collective-permute-start | bytes 208904 | tf_op jit(solution)/shard_map/ppermute | solution.py:461
  10.1 8.0 %collective-permute-start.2 = (f32[136,128]{1,0:T(8,128)S(1)}, f32[136,128]{1,0:T(8,128)S(1)}, u32[]{:S(2)}, u32[]{:S(2)}) collective-permute-start(f32[136,128]{1,0:T(8,128)S(1)} %pad_dynamic-update-slice_fusion.refs_0_), channel_id=1, source_target_pairs={{0,3},{1,0},{2,1},{3,2},{4,7},{5,4},{6,5},{7,6},{8,11},{9,8},{10,9... | collective-permute-start | bytes 208904 | tf_op jit(solution)/shard_map/ppermute | solution.py:461
  11.6 0.9 %copy-start.1 = (bf16[4,4,32,32]{3,2,1,0:T(8,128)(2,1)S(1)}, bf16[4,4,32,32]{3,2,1,0:T(8,128)(2,1)}, u32[]{:S(2)}) copy-start(bf16[4,4,32,32]{3,2,1,0:T(8,128)(2,1)} %param.23) | copy-start | bytes 98308
  14.9 0.7 %copy-start.4 = (bf16[3,3,32,8]{2,3,1,0:T(8,128)(2,1)S(1)}, bf16[3,3,32,8]{2,3,1,0:T(8,128)(2,1)}, u32[]{:S(2)}) copy-start(bf16[3,3,32,8]{2,3,1,0:T(8,128)(2,1)} %param.22) | copy-start | bytes 13828
  15.6 0.7 %copy-start.10 = (bf16[2,32]{1,0:T(2,128)(2,1)S(1)}, bf16[2,32]{1,0:T(2,128)(2,1)}, u32[]{:S(2)}) copy-start(bf16[2,32]{1,0:T(2,128)(2,1)} %param.26) | copy-start | bytes 388
  16.9 0.9 %copy-start.3 = (bf16[3,3,32,32]{3,2,1,0:T(8,128)(2,1)S(1)}, bf16[3,3,32,32]{3,2,1,0:T(8,128)(2,1)}, u32[]{:S(2)}) copy-start(bf16[3,3,32,32]{3,2,1,0:T(8,128)(2,1)} %param.24) | copy-start | bytes 55300
  38.6 1.4 %collective-permute-start.3 = (f32[208,128]{1,0:T(8,128)S(1)}, f32[208,128]{1,0:T(8,128)S(1)}, u32[]{:S(2)}, u32[]{:S(2)}) collective-permute-start(f32[208,128]{1,0:T(8,128)S(1)} %constant_dynamic-slice_fusion.7), channel_id=1, source_target_pairs={{0,4},{4,0},{8,12},{12,8},{16,20},{20,16},{24,28},{28,24},{1,5},{5... | collective-permute-start | bytes 319496 | tf_op jit(solution)/shard_map/ppermute | solution.py:457
  40.0 3.9 %collective-permute-start.4 = (f32[52,128]{1,0:T(8,128)S(1)}, f32[52,128]{1,0:T(8,128)S(1)}, u32[]{:S(2)}, u32[]{:S(2)}) collective-permute-start(f32[52,128]{1,0:T(8,128)S(1)} %get-tuple-element.42), channel_id=1, source_target_pairs={{0,8},{4,12},{8,0},{12,4},{16,24},{20,28},{24,16},{28,20},{1,9},{5... | collective-permute-start | bytes 79880 | tf_op jit(solution)/shard_map/ppermute | solution.py:457
  41.5 3.9 %collective-permute-start.5 = (f32[52,128]{1,0:T(8,128)S(1)}, f32[52,128]{1,0:T(8,128)S(1)}, u32[]{:S(2)}, u32[]{:S(2)}) collective-permute-start(f32[52,128]{1,0:T(8,128)S(1)} %get-tuple-element.44), channel_id=1, source_target_pairs={{0,16},{4,20},{8,24},{12,28},{16,0},{20,4},{24,8},{28,12},{1,17},{... | collective-permute-start | bytes 79880 | tf_op jit(solution)/shard_map/ppermute | solution.py:457
  43.1 4.8 %collective-permute-start.6 = (f32[52,128]{1,0:T(8,128)S(1)}, f32[52,128]{1,0:T(8,128)S(1)}, u32[]{:S(2)}, u32[]{:S(2)}) collective-permute-start(f32[52,128]{1,0:T(8,128)S(1)} %get-tuple-element.43), channel_id=1, source_target_pairs={{0,24},{4,28},{8,16},{12,20},{16,8},{20,12},{24,0},{28,4},{1,25},{... | collective-permute-start | bytes 79880 | tf_op jit(solution)/shard_map/ppermute | solution.py:457
  47.9 5.9 %collective-permute-start.7 = (f32[64,128]{1,0:T(8,128)S(1)}, f32[64,128]{1,0:T(8,128)S(1)}, u32[]{:S(2)}, u32[]{:S(2)}) collective-permute-start(f32[64,128]{1,0:T(8,128)S(1)} %get-tuple-element.47), channel_id=1, source_target_pairs={{0,1},{1,2},{2,3},{3,0},{4,5},{5,6},{6,7},{7,4},{8,9},{9,10},{10,1... | collective-permute-start | bytes 98312 | tf_op jit(solution)/shard_map/ppermute | solution.py:461
  48.6 5.6 %collective-permute-start.8 = (f32[64,128]{1,0:T(8,128)S(1)}, f32[64,128]{1,0:T(8,128)S(1)}, u32[]{:S(2)}, u32[]{:S(2)}) collective-permute-start(f32[64,128]{1,0:T(8,128)S(1)} %get-tuple-element.48), channel_id=1, source_target_pairs={{0,2},{1,3},{2,0},{3,1},{4,6},{5,7},{6,4},{7,5},{8,10},{9,11},{10,... | collective-permute-start | bytes 98312 | tf_op jit(solution)/shard_map/ppermute | solution.py:461
  48.9 5.3 %collective-permute-start.9 = (f32[64,128]{1,0:T(8,128)S(1)}, f32[64,128]{1,0:T(8,128)S(1)}, u32[]{:S(2)}, u32[]{:S(2)}) collective-permute-start(f32[64,128]{1,0:T(8,128)S(1)} %get-tuple-element.49), channel_id=1, source_target_pairs={{0,3},{1,0},{2,1},{3,2},{4,7},{5,4},{6,5},{7,6},{8,11},{9,8},{10,9... | collective-permute-start | bytes 98312 | tf_op jit(solution)/shard_map/ppermute | solution.py:461
  54.3 3.9 %collective-permute-start.10 = (f32[52,128]{1,0:T(8,128)S(1)}, f32[52,128]{1,0:T(8,128)S(1)}, u32[]{:S(2)}, u32[]{:S(2)}) collective-permute-start(f32[52,128]{1,0:T(8,128)S(1)} %get-tuple-element.35), channel_id=1, source_target_pairs={{0,8},{4,12},{8,0},{12,4},{16,24},{20,28},{24,16},{28,20},{1,9},{5... | collective-permute-start | bytes 79880 | tf_op jit(solution)/shard_map/ppermute | solution.py:457
  54.9 3.9 %collective-permute-start.11 = (f32[52,128]{1,0:T(8,128)S(1)}, f32[52,128]{1,0:T(8,128)S(1)}, u32[]{:S(2)}, u32[]{:S(2)}) collective-permute-start(f32[52,128]{1,0:T(8,128)S(1)} %get-tuple-element.35), channel_id=1, source_target_pairs={{0,16},{4,20},{8,24},{12,28},{16,0},{20,4},{24,8},{28,12},{1,17},{... | collective-permute-start | bytes 79880 | tf_op jit(solution)/shard_map/ppermute | solution.py:457
  55.4 4.8 %collective-permute-start.12 = (f32[52,128]{1,0:T(8,128)S(1)}, f32[52,128]{1,0:T(8,128)S(1)}, u32[]{:S(2)}, u32[]{:S(2)}) collective-permute-start(f32[52,128]{1,0:T(8,128)S(1)} %get-tuple-element.35), channel_id=1, source_target_pairs={{0,24},{4,28},{8,16},{12,20},{16,8},{20,12},{24,0},{28,4},{1,25},{... | collective-permute-start | bytes 79880 | tf_op jit(solution)/shard_map/ppermute | solution.py:457
  60.2 1.4 %collective-permute-start.13 = (f32[208,128]{1,0:T(8,128)S(1)}, f32[208,128]{1,0:T(8,128)S(1)}, u32[]{:S(2)}, u32[]{:S(2)}) collective-permute-start(f32[208,128]{1,0:T(8,128)S(1)} %reshape.129.refs_0_), channel_id=1, source_target_pairs={{0,4},{4,0},{8,12},{12,8},{16,20},{20,16},{24,28},{28,24},{1,5},{5... | collective-permute-start | bytes 319496 | tf_op jit(solution)/shard_map/ppermute | solution.py:457
  (2 other events, 1.3 us)
where the time goes:
time: 63.7 us; the launch traced here: 63.3 us
  Pallas kernels  20.7 us (32%)
  starting transfers between devices  18.1 us (28%)
  waiting for transfers between devices  11.5 us (18%)
  local copies, waits for them, and re-layouts  11 us (17%)
  between operations  1.27 us (2%)
    pallas_call x1, Pallas kernels, local(): pl.pallas_call(functools.partial(network_kernel, (n_band, n_blocks, own,...  19.8 us
    ppermute x6, starting transfers between devices, shifted(): lax.ppermute(values, axis, [(i, (i + shift) % count) for i in range(count)])  10.9 us
    ppermute x8, waiting for transfers between devices, swapped(): return lax.ppermute(values, axis, [(i, i ^ bits) for i in range(count)])  8.98 us
    ppermute x8, starting transfers between devices, swapped(): return lax.ppermute(values, axis, [(i, i ^ bits) for i in range(count)])  7.25 us
    unnamed x29, local copies, waits for them, and re-layouts  4.99 us
    ppermute x6, waiting for transfers between devices, shifted(): lax.ppermute(values, axis, [(i, (i + shift) % count) for i in range(count)])  2.49 us
  transfers between devices with their start and end apart: 14, of which 10 were waited for; matrix products, arithmetic and copies ran while one was open for 5% of the time, Pallas kernels for 0%

commit v1 on v0

--- a/solution.py
+++ b/solution.py
@@ -2,7 +2,6 @@
 
 import jax
 import jax.numpy as jnp
-import numpy as np
 from jax import lax
 from jax.experimental import pallas as pl
 from jax.experimental.pallas import tpu as pltpu
@@ -40,6 +39,10 @@
     return lax.dot_general(first, second, (((1,), (1,)), ((), ())), preferred_element_type=F32)
 
 
+def iota(shape, dim):
+    return lax.broadcasted_iota(jnp.int32, shape, dim)
+
+
 def rolled(values, shift):
     width = values.shape[-1]
     return pltpu.roll(values, shift % width, values.ndim - 1)
@@ -73,43 +76,16 @@
     return high, middle, rest - middle
 
 
-def network_kernel(sizes, *refs):
-    n_band, n_blocks, own, lon_count = sizes
-    window = own + 2 * HALO
-    half = window // 2
-    rows = ROWS_BAND * n_band
-    coarse = rows // 2
-    hist_tiles = (window + 2 * REACH) // LANES
-    own_tiles = own // LANES
-    pays = refs[:n_band]
-    (scales, w1, wd, wm, wu, wh, wht, wf, wmf, wbd) = refs[n_band : n_band + 10]
-    grads_out, mean_out = refs[n_band + 10 : n_band + 12]
-    (
-        bands, hist, table, zf, p1, zj, p2, z2, p3, p4, h4, truth, mean_split,
-        gs, gp4m, gj, gp3m, zg3, gp2m, zg2, gp1m, hi_pos, lo_pos,
-        acc_up, acc_down, acc_mid, acc_in, acc_head,
-    ) = refs[n_band + 12 :]
-
-    me = lax.axis_index("band")
-    cell_count = float(rows * lon_count)
-
-    def iota(shape, dim):
-        return lax.broadcasted_iota(jnp.int32, shape, dim)
-
-    for source in range(n_band):
-        pltpu.sync_copy(pays[source].at[pl.ds(3 * n_blocks, 8)], bands.at[source])
-
-    hist[...] = jnp.zeros_like(hist)
+def station_sums(own, lon_count, n_blocks, step, me, pay, bands, scales, hist, hi_pos, lo_pos):
+    hist_tiles = hist.shape[1] // 32
     start = (me * own - HALO - REACH).astype(F32)
-    for source in range(n_band):
-        lon = pays[source][n_blocks : 2 * n_blocks]
-        place = lon - start
-        place = jnp.where(place < 0.0, place + lon_count, place)
-        place = jnp.where(place < 0.0, place + lon_count, place)
-        place = jnp.where(place >= lon_count, place - lon_count, place)
-        tile = jnp.floor(place * (1.0 / LANES))
-        hi_pos[source] = tile
-        lo_pos[source] = place - tile * LANES
+    place = pay[n_blocks : 2 * n_blocks] - start
+    place = jnp.where(place < 0.0, place + lon_count, place)
+    place = jnp.where(place < 0.0, place + lon_count, place)
+    place = jnp.where(place >= lon_count, place - lon_count, place)
+    tile_of = jnp.floor(place * (1.0 / LANES))
+    hi_pos[...] = tile_of
+    lo_pos[...] = place - tile_of * LANES
 
     m_index = iota((32, 1), 0)
     row_of = (m_index // 8).astype(F32)
@@ -121,23 +97,64 @@
     rate = -0.5 / (spread * spread)
     lane_iota = iota((LANES, LANES), 0).astype(F32)
 
-    for source in range(n_band):
-
-        def one_block(block, source=source):
-            at_row = pays[source][pl.ds(block, 1), :]
-            observed = pays[source][pl.ds(2 * n_blocks + block, 1), :]
-            high = hi_pos[source, pl.ds(block, 1), :]
-            low = lo_pos[source, pl.ds(block, 1), :]
-            gap = row_of - at_row
-            left = jnp.exp(gap * gap * rate) * jnp.where(kind_of == 0, 1.0, observed)
-            spread_left = jnp.concatenate(
-                [jnp.where(high == float(tile), left, 0.0) for tile in range(hist_tiles)], axis=0
-            ).astype(BF16)
-            one_hot = jnp.where(lane_iota == low, 1.0, 0.0).astype(BF16)
-            band = bands[source, 0, block].astype(jnp.int32)
-            hist[band] = hist[band] + dot_lanes(spread_left, one_hot)
-
-        looped(n_blocks, 4, one_block)
+    def one_block(block):
+        at_row = pay[pl.ds(block, 1), :]
+        observed = pay[pl.ds(2 * n_blocks + block, 1), :]
+        high = hi_pos[pl.ds(block, 1), :]
+        low = lo_pos[pl.ds(block, 1), :]
+        gap = row_of - at_row
+        left = jnp.exp(gap * gap * rate) * jnp.where(kind_of == 0, 1.0, observed)
+        spread_left = jnp.concatenate(
+            [jnp.where(high == float(tile), left, 0.0) for tile in range(hist_tiles)], axis=0
+        ).astype(BF16)
+        one_hot = jnp.where(lane_iota == low, 1.0, 0.0).astype(BF16)
+        band = bands[0, block].astype(jnp.int32)
+        hist[band] = hist[band] + dot_lanes(spread_left, one_hot)
+
+    looped(n_blocks, step, one_block)
+
+
+def pack_kernel(sizes, *refs):
+    n_band, n_blocks, own, lon_count = sizes
+    pays = refs[6 : 6 + n_band]
+    wide = refs[6 + n_band]
+    held, sems = refs[7 + n_band : 13 + n_band], refs[13 + n_band]
+    copies = [pltpu.make_async_copy(refs[k], held[k], sems.at[k]) for k in range(6)]
+    for copy in copies:
+        copy.start()
+    for copy in copies:
+        copy.wait()
+    rows, lons, obs, live, block_band, field = held
+    me = lax.axis_index("band")
+    at_row = rows[0].astype(F32)
+    lon = jnp.where(live[0] > 0, lons[0].astype(F32), FAR)
+    total = wide.shape[1]
+    wide[:, 0:HALO] = field[0, :, lon_count - HALO : lon_count]
+    wide[:, HALO : HALO + lon_count] = field[0]
+    wide[:, HALO + lon_count : total] = field[0, :, 0 : total - HALO - lon_count]
+    for shift in range(n_band):
+        pay = pays[shift]
+        pay[0:n_blocks] = at_row
+        pay[n_blocks : 2 * n_blocks] = lon
+        pay[2 * n_blocks : 3 * n_blocks] = obs[0]
+        pay[3 * n_blocks : 3 * n_blocks + 8] = jnp.zeros((8, LANES), F32)
+        pay[3 * n_blocks : 3 * n_blocks + 1, 0:n_blocks] = block_band[...].astype(F32)
+        target = lax.rem(me + shift, n_band)
+        for tile in range((own + 2 * HALO) // LANES):
+            at = pl.multiple_of(target * own + tile * LANES, LANES)
+            first = 3 * n_blocks + 8 + ROWS_BAND * tile
+            pay[first : first + ROWS_BAND] = wide[:, pl.ds(at, LANES)]
+
+
+def early_kernel(sizes, *refs):
+    n_band, n_blocks, own, lon_count = sizes
+    pay, scales, hist, table, token, bands, hi_pos, lo_pos = refs
+    me = lax.axis_index("band")
+    token[...] = jnp.zeros_like(token)
+    pltpu.sync_copy(pay.at[pl.ds(3 * n_blocks, 8)], bands)
+    hist[...] = jnp.zeros_like(hist)
+    step = n_blocks if n_band <= 4 else 4
+    station_sums(own, lon_count, n_blocks, step, me, pay, bands, scales, hist, hi_pos, lo_pos)
 
     place_in = iota((4 * LANES, 2 * LANES), 0)
     place_out = iota((4 * LANES, 2 * LANES), 1)
@@ -145,6 +162,99 @@
     squared = distance * distance
     for scale in range(4):
         table[scale] = jnp.exp(squared * (-0.5 / (scales[scale] * scales[scale]))).astype(BF16)
+
+
+def matrix_kernel(*refs):
+    w_in, w_down, w_mid, w_up, w_head, _ = refs[:6]
+    w1, wd, wm, wu, wh, wht, wf, wmf, wbd = refs[6:15]
+    t1, td, tm, tu, tf, tmf, tbd = refs[15:]
+    t1[...] = jnp.zeros_like(t1)
+    tu[...] = jnp.zeros_like(tu)
+    tf[...] = jnp.zeros_like(tf)
+    tbd[...] = jnp.zeros_like(tbd)
+    for row in range(3):
+        for col in range(3):
+            inner = w_in[row, col].astype(F32)
+            mid = w_mid[row, col].astype(F32)
+            up = w_up[row, col].astype(F32)
+            tm[:, (row * 3 + col) * 32 : (row * 3 + col) * 32 + 32] = mid
+            back = (2 - row) * 3 + 2 - col
+            tmf[back * 32 : back * 32 + 32, 0:32] = mid
+            for phase in range(2):
+                at = row * 32 + (phase + col) * 8
+                t1[at : at + 8, phase * 32 : phase * 32 + 32] = inner
+                for part in range(2):
+                    cols = slice(part * 32, part * 32 + 32)
+                    at = (row * 2 + part) * 128 + (phase + col) * 32
+                    tu[phase * 32 : phase * 32 + 32, at : at + 32] = up[:, cols]
+                    at = (2 - row) * 128 + (phase + 2 - col) * 32
+                    to = part * 64 + phase * 32
+                    tf[at : at + 32, to : to + 32] = up[:, cols]
+    sides = (((1, 0), (3, -1)), ((0, 1), (2, 0)))
+    for row in range(4):
+        for col in range(4):
+            td[:, (row * 4 + col) * 32 : (row * 4 + col) * 32 + 32] = w_down[row, col].astype(F32)
+    for side in range(2):
+        for phase in range(2):
+            for row, row_shift in sides[side]:
+                for col, col_shift in sides[phase]:
+                    at = (row_shift + 1) * 96 + (col_shift + 1) * 32
+                    to = (side * 2 + phase) * 32
+                    tbd[at : at + 32, to : to + 32] = w_down[row, col].astype(F32)
+    w1[...] = t1[...].T[0:64, 0:96].astype(BF16)
+    wd[...] = td[...].astype(BF16)
+    wm[...] = tm[...].astype(BF16)
+    wu[...] = tu[...].astype(BF16)
+    wf[...] = tf[...].T.astype(BF16)
+    wmf[...] = tmf[...].T[0:32, 0:288].astype(BF16)
+    wbd[...] = tbd[...].T[:, 0:288].astype(BF16)
+    heads = w_head[...].astype(F32)
+    heads = jnp.concatenate([heads, jnp.zeros((6, 32), F32)], axis=0)
+    heads = jnp.concatenate([heads, jnp.zeros((8, 96), F32)], axis=1)
+    heads = heads + rolled(heads, 32)
+    heads = heads + rolled(heads, 64)
+    heads = jnp.concatenate([heads, heads], axis=1)
+    k_index = iota((128, 256), 0)
+    c_index = iota((128, 256), 1) // 32
+    same = (k_index % 4 == c_index // 2) & ((k_index // 4) % 2 == c_index % 2) & (k_index < 16)
+    full = jnp.where(same, jnp.where(k_index < 8, heads[0:1], heads[1:2]), 0.0)
+    wh[...] = full[0:16].astype(BF16)
+    wht[...] = full.T[:, 0:16].astype(BF16)
+
+
+def network_kernel(sizes, *refs):
+    n_band, n_blocks, own, lon_count = sizes
+    window = own + 2 * HALO
+    half = window // 2
+    rows = ROWS_BAND * n_band
+    coarse = rows // 2
+    own_tiles = own // LANES
+    pays = refs[:n_band]
+    (scales, hist_own, table, w1, wd, wm, wu, wh, wht, wf, wmf, wbd) = refs[n_band : n_band + 12]
+    hist, grads_out, mean_out = refs[n_band + 12 : n_band + 15]
+    (
+        bands, band_sems, zf, p1, zj, p2, z2, p3, p4, h4, truth, mean_split,
+        gs, gp4m, gj, gp3m, zg3, gp2m, zg2, gp1m, hi_pos, lo_pos,
+        acc_up, acc_down, acc_mid, acc_in, acc_head,
+    ) = refs[n_band + 15 :]
+    many = n_band > 4
+    me = lax.axis_index("band")
+    cell_count = float(rows * lon_count)
+
+    copies = [
+        pltpu.make_async_copy(pays[k].at[pl.ds(3 * n_blocks, 8)], bands.at[k], band_sems.at[k])
+        for k in range(1, n_band)
+    ]
+    for copy in copies:
+        copy.start()
+    for copy in copies:
+        copy.wait()
+    for source in range(1, n_band):
+        station_sums(
+            own, lon_count, n_blocks, 4 if many else n_blocks, me, pays[source], bands.at[source], scales,
+            hist, hi_pos.at[source], lo_pos.at[source],
+        )
+
     all_rows = 32 * n_band
     channel = iota((all_rows, 1), 0) % 8
     feats = []
@@ -198,7 +308,9 @@
         for chunk in range(2):
             if chunk < chunks:
                 tiles = [
-                    pays[source][pl.ds(3 * n_blocks + 8 + (me * own_tiles + 2 * chunk + t) * ROWS_BAND, ROWS_BAND), :]
+                    pays[source][
+                        3 * n_blocks + 8 + (2 * chunk + t) * ROWS_BAND : 3 * n_blocks + 8 + (2 * chunk + t + 1) * ROWS_BAND
+                    ]
                     for t in range(2)
                 ]
                 pieces.append(jnp.concatenate(tiles, axis=1))
@@ -219,7 +331,7 @@
         hidden = silu(pre)
         zj[row + 1, 128:256, :] = four_shifts(hidden[:32], hidden[32:]).astype(BF16)
 
-    looped(rows, 4, first)
+    looped(rows, 4 if many else rows, first)
 
     def second(index):
         for par in range(2):
@@ -228,7 +340,7 @@
             p2[row] = pre
             z2[par, index + 1] = three_shifts(silu(pre), 2).astype(BF16)
 
-    looped(coarse // 2, 4, second)
+    looped(coarse // 2, 4 if many else coarse // 2, second)
 
     def third(index):
         for par in range(2):
@@ -240,14 +352,14 @@
             zj[2 * row + 1, 0:128, :] = wide
             zj[2 * row + 2, 0:128, :] = wide
 
-    looped(coarse // 2, 4, third)
+    looped(coarse // 2, 4 if many else coarse // 2, third)
 
     def fourth(row):
         pre = dot(wu[...], zj[pl.ds(row, 3)].reshape(768, half))
         p4[row] = pre
         h4[row] = silu(pre).astype(BF16)
 
-    looped(rows, 4, fourth)
+    looped(rows, 4 if many else rows, fourth)
 
     own_cells = jnp.clip(lon_count - me * own, 0, own) // 2
     place = iota((1, half), 1)
@@ -280,7 +392,7 @@
             parts + (jnp.zeros((4, 2 * half), F32),), axis=0
         ).astype(BF16)
 
-    looped(n_band, 1, head)
+    looped(n_band, 1 if many else n_band, head)
 
     target = iota((2 * half, own), 1) + HALO
     origin = iota((2 * half, own), 0)
@@ -307,7 +419,7 @@
             gp3m[par, index + 1] = (grad * mask).astype(BF16)
             zg3[par, index + 1] = three_shifts(grad, 2).astype(BF16)
 
-    looped(coarse // 2, 2, join_back)
+    looped(coarse // 2, 2 if many else coarse // 2, join_back)
 
     def mid_back(index):
         for par in range(2):
@@ -317,7 +429,7 @@
             gp2m[row + 1] = (grad * mask).astype(BF16)
             zg2[row + 1] = three_shifts(grad, 1).astype(BF16)
 
-    looped(coarse // 2, 4, mid_back)
+    looped(coarse // 2, 4 if many else coarse // 2, mid_back)
 
     def down_back(row):
         back = dot(wbd[...], zg2[pl.ds(row, 3)].reshape(288, half))
@@ -326,7 +438,7 @@
             grad = (back[64 * side : 64 * side + 64] + gj[fine].astype(F32)) * silu_slope(p1[fine])
             gp1m[fine + 1] = (grad * mask).astype(BF16)
 
-    looped(coarse, 4, down_back)
+    looped(coarse, 4 if many else coarse, down_back)
 
     acc_up[...] = jnp.zeros_like(acc_up)
     acc_down[...] = jnp.zeros_like(acc_down)
@@ -335,9 +447,9 @@
 
     def weights_fine(row):
         acc_up[...] += dot_lanes(gp4m[pl.ds(row, 3)].reshape(192, half), zj[row + 1])
-        acc_in[...] += dot_lanes(gp1m[pl.ds(row, 3)].reshape(192, half), zf[row + 1])
-
-    looped(rows, 4, weights_fine)
+        acc_in[...] += dot_lanes(zf[row + 1], gp1m[pl.ds(row, 3)].reshape(192, half))
+
+    looped(rows, 4 if many else rows, weights_fine)
 
     def weights_coarse(index):
         for par in range(2):
@@ -348,26 +460,33 @@
                 zj[pl.ds(2 * row + 1, 2), 128:256, :].reshape(256, half),
             )
 
-    looped(coarse // 2, 4, weights_coarse)
+    looped(coarse // 2, 4 if many else coarse // 2, weights_coarse)
 
     up = acc_up[...]
-    inner = acc_in[...]
     for step in range(3):
         first_up, second_up = up[64 * step : 64 * step + 32], up[64 * step + 32 : 64 * step + 64]
-        first_in, second_in = inner[64 * step : 64 * step + 32], inner[64 * step + 32 : 64 * step + 64]
-        at = slice(32 * step, 32 * step + 32)
         for part in range(2):
             cols = slice(128 * part, 128 * part + 128)
             grads_out[96 * part + 32 * step : 96 * part + 32 * step + 32, :] = first_up[:, cols] + rolled(
                 second_up[:, cols], -32
             )
-        grads_out[at, 96:120] = first_in[:, 0:24] + second_in[:, 8:32]
+    mid = acc_mid[...]
+    grads_out[0:96, 96:128] = mid[:, 0:32]
+    grads_out[96:192, 96:128] = mid[:, 32:64]
     down = acc_down[...]
     for tap, (step, side) in enumerate(((2, 1), (1, 0), (1, 1), (0, 0))):
         grads_out[192 + 32 * tap : 224 + 32 * tap, :] = down[
             32 * step : 32 * step + 32, 128 * side : 128 * side + 128
         ]
-    grads_out[320:416, 0:96] = acc_mid[...]
+    inner = acc_in[...]
+    for step in range(3):
+        grads_out[320:344, 32 * step : 32 * step + 32] = (
+            inner[0:24, 64 * step : 64 * step + 32] + inner[8:32, 64 * step + 32 : 64 * step + 64]
+        )
+    for part in range(4):
+        grads_out[344:368, 32 * part : 32 * part + 32] = mid[24 * part : 24 * part + 24, 64:96]
+    grads_out[320:344, 96:128] = jnp.zeros((24, 32), F32)
+    grads_out[368:384] = jnp.zeros((16, LANES), F32)
     k_index = iota((16, 256), 0) % 8
     c_index = iota((16, 256), 1) // 32
     same = (k_index % 4 == c_index // 2) & (k_index // 4 == c_index % 2)
@@ -390,25 +509,26 @@
     own_tiles = own // LANES
     first = jnp.where(core == 0, low[...], high[...])
     second = jnp.where(core == 0, high[...], low[...])
-    both = jnp.concatenate([first, second], axis=0)
-    lane = lax.broadcasted_iota(jnp.int32, (96, LANES), 1)
-    part_a, part_b = both[0:96], both[96:192]
-    mid = both[320:416]
+    part_a, part_b = first[0:96], first[96:192]
+    down, inner, folded = second[0:128], second[128:152], second[152:176]
+    last = jnp.concatenate([rolled(folded, -32 * part) for part in range(4)], axis=0)
+    lane = iota((96, LANES), 1)
+    mids = (rolled(part_a, -96), rolled(part_b, -96), last)
     for tap_col in range(3):
         ups = jnp.where(lane < 32, rolled(part_a, -32 * tap_col), rolled(part_b, 32 - 32 * tap_col))
-        ins = rolled(part_a, -96 - 8 * tap_col)
-        mids = rolled(mid, -32 * tap_col)
         for tap_row in range(3):
             at = slice(32 * (2 - tap_row), 32 * (2 - tap_row) + 32)
             grad_up[tap_row, tap_col] = ups[at, 0:64]
-            grad_in[tap_row, tap_col] = ins[at, 0:8]
-            grad_mid[tap_row, tap_col] = mids[at, 0:32]
-    down = both[192:320]
+            grad_mid[tap_row, tap_col] = mids[tap_col][at, 0:32]
+    for tap_row in range(3):
+        ins = rolled(inner, -32 * (2 - tap_row))
+        for tap_col in range(3):
+            grad_in[tap_row, tap_col] = ins[8 * tap_col : 8 * tap_col + 8, 0:32]
     for tap_col in range(4):
         downs = rolled(down, -32 * tap_col)
         for tap_row in range(4):
             grad_down[tap_row, tap_col] = downs[32 * tap_row : 32 * tap_row + 32, 0:32]
-    grad_head[...] = rolled(mid[0:8], -96)[0:2, 0:32]
+    grad_head[...] = rolled(inner[0:8], -96)[0:2, 0:32]
     for shift in range(n_band):
         origin = lax.rem(me - shift + n_band, n_band)
         for tile in range(own_tiles):
@@ -417,42 +537,6 @@
     mean_out[0] = wide[:, 0:lon_count]
 
 
-def phased(taps):
-    before = jnp.pad(taps, ((0, 0), (0, 0), (0, 1), (0, 0)))
-    after = jnp.pad(taps, ((0, 0), (0, 0), (1, 0), (0, 0)))
-    return jnp.stack([before, after])
-
-
-def parted(taps, axis):
-    first = lax.rev(lax.slice_in_dim(taps, 1, 4, 2, axis), (axis,))
-    second = lax.rev(lax.slice_in_dim(taps, 0, 3, 2, axis), (axis,))
-    at_end = [(0, 0)] * taps.ndim
-    at_start = [(0, 0)] * taps.ndim
-    at_end[axis] = (0, 1)
-    at_start[axis] = (1, 0)
-    return jnp.stack([jnp.pad(first, at_end), jnp.pad(second, at_start)])
-
-
-def matrices(w_in, w_down, w_mid, w_up, w_head):
-    w1 = phased(jnp.transpose(w_in, (2, 0, 1, 3))).reshape(64, 96)
-    wd = jnp.transpose(w_down, (2, 0, 1, 3)).reshape(32, 512)
-    wm = jnp.transpose(w_mid, (2, 0, 1, 3)).reshape(32, 288)
-    up = jnp.transpose(w_up.reshape(3, 3, 32, 2, 32), (2, 0, 3, 1, 4)).reshape(32, 6, 3, 32)
-    wu = phased(up).reshape(64, 768)
-    sel = np.zeros((8, 8), np.float32)
-    for phase in range(2):
-        for row in range(4):
-            sel[phase * 4 + row, row * 2 + phase] = 1.0
-    wh = (jnp.asarray(sel, BF16)[None, :, :, None] * w_head[:, None, None, :]).reshape(16, 256)
-    back = phased(jnp.transpose(w_up[::-1, ::-1], (3, 0, 1, 2)))
-    wf = jnp.transpose(back.reshape(2, 2, 32, 384), (1, 0, 2, 3)).reshape(128, 384)
-    wmf = jnp.transpose(w_mid[::-1, ::-1], (3, 0, 1, 2)).reshape(32, 288)
-    taps = jnp.transpose(w_down, (3, 0, 1, 2))
-    taps = parted(parted(taps, 1), 3)
-    wbd = jnp.transpose(taps, (1, 0, 2, 3, 4, 5)).reshape(128, 288)
-    return w1, wd, wm, wu, wh, wh.T, wf, wmf, wbd
-
-
 def swapped(values, axis, count, bits):
     return lax.ppermute(values, axis, [(i, i ^ bits) for i in range(count)])
 
@@ -464,19 +548,15 @@
 def reduced(grads, mean_tiles, n_band, n_group):
     group = lax.axis_index("group")
     band = lax.axis_index("band")
-    core, chip = group % 2, group // 2
-    chips = n_group // 2
-    tile_rows = mean_tiles.shape[1]
+    core, side = group % 2, (group // 2) % 2
     half = grads.shape[0] // 2
     mine = lax.dynamic_slice_in_dim(grads, core * half, half, 0)
     theirs = lax.dynamic_slice_in_dim(grads, (1 - core) * half, half, 0)
     total = mine + swapped(theirs, "group", n_group, 1)
-    share = half // chips
-    kept = lax.dynamic_slice_in_dim(total, chip * share, share, 0)
-    got = [
-        swapped(lax.dynamic_slice_in_dim(total, (chip ^ k) * share, share, 0), "group", n_group, 2 * k)
-        for k in range(1, chips)
-    ]
+    share = half // 2
+    kept = lax.dynamic_slice_in_dim(total, side * share, share, 0)
+    other = lax.dynamic_slice_in_dim(total, (1 - side) * share, share, 0)
+    got = [swapped(other if k % 2 else kept, "group", n_group, 2 * k) for k in range(1, n_group // 2)]
     for piece in got:
         kept = kept + piece
     means = [lax.dynamic_index_in_dim(mean_tiles, band, 0, keepdims=False)]
@@ -488,13 +568,8 @@
     for piece in arrived:
         kept = kept + piece[:share]
         means.append(piece[share:])
-    pieces = [(chip, kept)] + [
-        (chip ^ k, swapped(kept, "group", n_group, 2 * k)) for k in range(1, chips)
-    ]
-    whole = jnp.zeros((chips, share, LANES), F32)
-    for at, piece in pieces:
-        whole = lax.dynamic_update_slice(whole, piece[None], (at, 0, 0))
-    whole = whole.reshape(half, LANES)
+    other = swapped(kept, "group", n_group, 2)
+    whole = jnp.where(side == 0, jnp.concatenate([kept, other]), jnp.concatenate([other, kept]))
     return whole, swapped(whole, "group", n_group, 1), means
 
 
@@ -528,40 +603,91 @@
     coarse = rows // 2
     hist_tiles = (window + 2 * REACH) // LANES
 
-    field = truth_field[0]
-    total_tiles = n_band * own_tiles + 1
-    extended = jnp.concatenate(
-        [field[:, lon_count - HALO :], field, field[:, : total_tiles * LANES - HALO - lon_count]], axis=1
-    )
-    truth_rows = jnp.transpose(extended.reshape(ROWS_BAND, total_tiles, LANES), (1, 0, 2)).reshape(-1, LANES)
-    fill = -truth_rows.shape[0] % 8
-    band_rows = jnp.zeros((8, LANES), F32).at[0, :n_blocks].set(block_band[0, :, 0].astype(F32))
-    pay = jnp.concatenate(
-        [
-            station_rows[0].astype(F32),
-            jnp.where(station_live[0] > 0, station_lons[0].astype(F32), FAR),
-            station_obs[0],
-            band_rows,
-            jnp.pad(truth_rows, ((0, fill), (0, 0))),
-        ]
-    )
-    pays = [pay] + [shifted(pay, "band", n_band, k) for k in range(1, n_band)]
-    mats = matrices(w_in, w_down, w_mid, w_up, w_head)
-
+    sizes = (n_band, n_blocks, own, lon_count)
+    pay_rows = 3 * n_blocks + 8 + -(-(window // LANES) * ROWS_BAND // 8) * 8
+    wide_lanes = (n_band * own_tiles + 1) * LANES
     in_vmem = pl.BlockSpec(memory_space=pltpu.VMEM)
     in_smem = pl.BlockSpec(memory_space=pltpu.SMEM)
-    grads, mean_tiles = pl.pallas_call(
-        functools.partial(network_kernel, (n_band, n_blocks, own, lon_count)),
+    in_hbm = pl.BlockSpec(memory_space=pltpu.HBM)
+
+    def shaped(*shape, dtype=BF16):
+        return jax.ShapeDtypeStruct(shape, dtype)
+
+    arrays = (
+        station_rows, station_lons, station_obs, station_live, block_band.reshape(1, n_blocks), truth_field
+    )
+    packed = pl.pallas_call(
+        functools.partial(pack_kernel, sizes),
+        out_shape=(shaped(pay_rows, LANES, dtype=F32),) * n_band,
+        in_specs=[in_hbm] * 6,
+        out_specs=(in_vmem,) * n_band,
+        scratch_shapes=[vmem(ROWS_BAND, wide_lanes, dtype=F32)]
+        + [vmem(*arg.shape, dtype=arg.dtype) for arg in arrays]
+        + [pltpu.SemaphoreType.DMA((6,))],
+        compiler_params=pltpu.CompilerParams(vmem_limit_bytes=56 * 1024 * 1024),
+    )(*arrays)
+    pays = [packed[0]] + [shifted(packed[k], "band", n_band, k) for k in range(1, n_band)]
+
+    hist_shape = (n_band, hist_tiles * 32, LANES)
+    hist, table, token = pl.pallas_call(
+        functools.partial(early_kernel, sizes),
         out_shape=(
-            jax.ShapeDtypeStruct((416, LANES), F32),
-            jax.ShapeDtypeStruct((n_band, own_tiles, ROWS_BAND, LANES), F32),
+            shaped(*hist_shape, dtype=F32),
+            shaped(4, 4 * LANES, 2 * LANES),
+            shaped(8, LANES, dtype=F32),
         ),
-        in_specs=[in_vmem] * n_band + [in_smem] + [in_vmem] * len(mats),
-        out_specs=(in_vmem, in_vmem),
+        in_specs=[in_vmem, in_smem],
+        out_specs=(in_vmem,) * 3,
+        scratch_shapes=[
+            pltpu.SMEM((8, LANES), F32),
+            vmem(n_blocks, LANES, dtype=F32),
+            vmem(n_blocks, LANES, dtype=F32),
+        ],
+        compiler_params=pltpu.CompilerParams(vmem_limit_bytes=16 * 1024 * 1024),
+        cost_estimate=pl.CostEstimate(flops=200_000_000, bytes_accessed=2_000_000, transcendentals=700_000),
+    )(packed[0], length_scales)
+    mats = pl.pallas_call(
+        matrix_kernel,
+        out_shape=(
+            shaped(64, 96),
+            shaped(32, 512),
+            shaped(32, 288),
+            shaped(64, 768),
+            shaped(16, 256),
+            shaped(256, 16),
+            shaped(128, 384),
+            shaped(32, 288),
+            shaped(128, 288),
+        ),
+        in_specs=[in_vmem] * 6,
+        out_specs=(in_vmem,) * 9,
+        scratch_shapes=[
+            vmem(128, 128, dtype=F32),
+            vmem(32, 512, dtype=F32),
+            vmem(32, 288, dtype=F32),
+            vmem(64, 768, dtype=F32),
+            vmem(384, 128, dtype=F32),
+            vmem(384, 128, dtype=F32),
+            vmem(384, 128, dtype=F32),
+        ],
+        compiler_params=pltpu.CompilerParams(vmem_limit_bytes=16 * 1024 * 1024),
+        cost_estimate=pl.CostEstimate(flops=10_000_000, bytes_accessed=1_000_000, transcendentals=0),
+    )(jnp.transpose(w_in, (0, 1, 3, 2)), w_down, w_mid, w_up, w_head, token)
+    early = (hist, table) + tuple(mats)
+
+    _, grads, mean_tiles = pl.pallas_call(
+        functools.partial(network_kernel, sizes),
+        out_shape=(
+            shaped(*hist_shape, dtype=F32),
+            shaped(384, LANES, dtype=F32),
+            shaped(n_band, own_tiles, ROWS_BAND, LANES, dtype=F32),
+        ),
+        in_specs=[in_vmem] * n_band + [in_smem] + [in_vmem] * 11,
+        out_specs=(in_vmem, in_vmem, in_vmem),
+        input_output_aliases={n_band + 1: 0},
         scratch_shapes=[
             pltpu.SMEM((n_band, 8, LANES), F32),
-            vmem(n_band, hist_tiles * 32, LANES, dtype=F32),
-            vmem(4, 4 * LANES, 2 * LANES),
+            pltpu.SemaphoreType.DMA((n_band,)),
             vmem(rows + 2, 32, half),
             vmem(rows, 64, half, dtype=F32),
             vmem(rows + 2, 256, half),
@@ -585,19 +711,20 @@
             vmem(192, 256, dtype=F32),
             vmem(96, 256, dtype=F32),
             vmem(96, 96, dtype=F32),
-            vmem(192, 32, dtype=F32),
+            vmem(32, 192, dtype=F32),
             vmem(16, 256, dtype=F32),
         ],
         compiler_params=pltpu.CompilerParams(vmem_limit_bytes=40 * 1024 * 1024),
-    )(*pays, length_scales, *mats)
+        cost_estimate=pl.CostEstimate(flops=4_000_000_000, bytes_accessed=4_000_000, transcendentals=2_000_000),
+    )(*pays, length_scales, *early)
 
     low, high, means = reduced(grads, mean_tiles.reshape(n_band, own_tiles * ROWS_BAND, LANES), n_band, n_group)
     means = [piece.reshape(own_tiles, ROWS_BAND, LANES) for piece in means]
-    return pl.pallas_call(
+    outs = pl.pallas_call(
         functools.partial(unpack_kernel, (n_band, own, lon_count)),
         out_shape=(
             jax.ShapeDtypeStruct((1, ROWS_BAND, lon_count), F32),
-            jax.ShapeDtypeStruct((3, 3, 32, 8), F32),
+            jax.ShapeDtypeStruct((3, 3, 8, 32), F32),
             jax.ShapeDtypeStruct((4, 4, 32, 32), F32),
             jax.ShapeDtypeStruct((3, 3, 32, 32), F32),
             jax.ShapeDtypeStruct((3, 3, 32, 64), F32),
@@ -608,6 +735,7 @@
         scratch_shapes=[vmem(ROWS_BAND, n_band * own, dtype=F32)],
         compiler_params=pltpu.CompilerParams(vmem_limit_bytes=16 * 1024 * 1024),
     )(low, high, *means)
+    return (outs[0], jnp.transpose(outs[1], (0, 1, 3, 2))) + tuple(outs[2:])
 
 
 def solution(mesh):

time: 63.7 us -> 46 us (0.72)
  local copies, waits for them, and re-layouts: 11 us -> 1.54 us
  Pallas kernels: 20.7 us -> 14.2 us
  starting transfers between devices: 18.1 us -> 15 us
  waiting for transfers between devices: 11.5 us -> 14.1 us
    pallas_call x1 -> x4, Pallas kernels: 19.8 us -> 13.3 us  [the longest x1 9.11 us: local(): pl.pallas_call(functools.partial(network_kernel, sizes), out_shape=(shape...]
    unnamed x29 -> x16, local copies, waits for them, and re-layouts: 4.99 us -> 1.43 us
    ppermute x6, waiting for transfers between devices: 2.49 us -> 5.46 us  [shifted(): lax.ppermute(values, axis, [(i, (i + shift) % count) for i in range(count)])]
    ppermute x8 -> x6, starting transfers between devices: 7.25 us -> 5.25 us  [swapped(): return lax.ppermute(values, axis, [(i, i ^ bits) for i in range(count)])]
    slice x4 -> x0, local copies, waits for them, and re-layouts: 1.47 us -> none  [the longest x1 0.76 us: local(): field[:, lon_count - HALO:]]
    reshape x12 -> x0, local copies, waits for them, and re-layouts: 1.37 us -> none  [the longest x2 0.45 us: matrices(): wbd = jnp.transpose(taps, (1, 0, 2, 3, 4, 5)).reshape(128, 288)]
    ppermute x6, starting transfers between devices: 10.9 us -> 9.73 us  [shifted(): lax.ppermute(values, axis, [(i, (i + shift) % count) for i in range(count)])]
    another operation x10 -> x0, local copies, waits for them, and re-layouts: 0.85 us -> none  [the longest x7 0.77 us: phased(): return jnp.stack([before, after])]
  transfers between devices with their start and end apart: 14 -> 12, of which waited for: 10 -> 8; matrix products, arithmetic and copies ran while one was open for 5% -> 0% of each run, Pallas kernels for 0% -> 6%
where the time goes in v1:
time: 46 us; the launch traced here: 45.8 us
  starting transfers between devices  15 us (33%)
  Pallas kernels  14.2 us (31%)
  waiting for transfers between devices  14.1 us (31%)
  local copies, waits for them, and re-layouts  1.54 us (3%)
  between operations  0.85 us (2%)
    ppermute x6, starting transfers between devices, shifted(): lax.ppermute(values, axis, [(i, (i + shift) % count) for i in range(count)])  9.73 us
    pallas_call x1, Pallas kernels, local(): pl.pallas_call(functools.partial(network_kernel, sizes), out_shape=(shape...  9.11 us
    ppermute x6, waiting for transfers between devices, swapped(): return lax.ppermute(values, axis, [(i, i ^ bits) for i in range(count)])  8.64 us
    ppermute x6, waiting for transfers between devices, shifted(): lax.ppermute(values, axis, [(i, (i + shift) % count) for i in range(count)])  5.46 us
    ppermute x6, starting transfers between devices, swapped(): return lax.ppermute(values, axis, [(i, i ^ bits) for i in range(count)])  5.25 us
    pallas_call x1, Pallas kernels, local(): pl.pallas_call(functools.partial(early_kernel, sizes), out_shape=(shaped(...  2.11 us
    pallas_call x1, Pallas kernels, local(): pl.pallas_call(functools.partial(pack_kernel, sizes), out_shape=(shaped(p...  1.62 us
    unnamed x16, local copies, waits for them, and re-layouts  1.43 us
  transfers between devices with their start and end apart: 12, of which 8 were waited for; matrix products, arithmetic and copies ran while one was open for 0% of the time, Pallas kernels for 6%

profile of v1, /device:TPU:0, one launch (start us, length us, event | category | flops | bytes accessed | tf_op | source)
XLA Modules:
  0.0 45.8 jit_solution(818658920686867712)
XLA Ops:
  0.6 1.6 %shard_map.163 = (f32[96,128]{1,0:T(8,128)}, f32[96,128]{1,0:T(8,128)}, f32[96,128]{1,0:T(8,128)}, f32[96,128]{1,0:T(8,128)}) custom-call(s32[1,24,128]{2,1,0:T(8,128)} %refs_0_.1, s32[1,24,128]{2,1,0:T(8,128)} %refs_1_.3, f32[1,24,128]{2,1,0:T(8,128)} %refs_2_.2, s32[1,24,128]{2,1,0:T(8,128)} %refs_3_.2, s32[1,24]{1,0:T(1,128)} %bitcast.16, ...), custom_call_target="tpu_custom_call" | custom-call | tf_op jit(solution)/shard_map/pallas_call | solution.py:619
  2.3 3.1 %collective-permute-start = (f32[96,128]{1,0:T(8,128)}, f32[96,128]{1,0:T(8,128)S(1)}, u32[]{:S(2)}, u32[]{:S(2)}) collective-permute-start(f32[96,128]{1,0:T(8,128)} %get-tuple-element.31), channel_id=1, source_target_pairs={{0,1},{1,2},{2,3},{3,0},{4,5},{5,6},{6,7},{7,4},{8,9},{9,10},{10,1... | collective-permute-start | bytes 147464 | tf_op jit(solution)/shard_map/ppermute | solution.py:545
  5.3 2.6 %collective-permute-start.1 = (f32[96,128]{1,0:T(8,128)}, f32[96,128]{1,0:T(8,128)S(1)}, u32[]{:S(2)}, u32[]{:S(2)}) collective-permute-start(f32[96,128]{1,0:T(8,128)} %get-tuple-element.32), channel_id=1, source_target_pairs={{0,2},{1,3},{2,0},{3,1},{4,6},{5,7},{6,4},{7,5},{8,10},{9,11},{10,... | collective-permute-start | bytes 147464 | tf_op jit(solution)/shard_map/ppermute | solution.py:545
  7.9 1.3 %collective-permute-start.2 = (f32[96,128]{1,0:T(8,128)}, f32[96,128]{1,0:T(8,128)S(1)}, u32[]{:S(2)}, u32[]{:S(2)}) collective-permute-start(f32[96,128]{1,0:T(8,128)} %get-tuple-element.33), channel_id=1, source_target_pairs={{0,3},{1,0},{2,1},{3,2},{4,7},{5,4},{6,5},{7,6},{8,11},{9,8},{10,9... | collective-permute-start | bytes 147464 | tf_op jit(solution)/shard_map/ppermute | solution.py:545
  9.3 0.8 %copy-done.5 = f32[96,128]{1,0:T(8,128)S(1)} copy-done((f32[96,128]{1,0:T(8,128)S(1)}, f32[96,128]{1,0:T(8,128)}, u32[]{:S(2)}) %copy-start.5) | copy-done | bytes 49176
  10.1 2.1 %shard_map.164 = (f32[4,192,128]{2,1,0:T(8,128)S(1)}, bf16[4,512,256]{2,1,0:T(8,128)(2,1)S(1)}, f32[8,128]{1,0:T(8,128)S(1)}) custom-call(f32[96,128]{1,0:T(8,128)S(1)} %copy-done.5, f32[4]{0:T(128)S(1)} %copy-done.6), custom_call_target="tpu_custom_call" | custom-call | flops 200000000 | bytes 2000000 | tf_op jit(solution)/shard_map/pallas_call | solution.py:632
  12.3 0.6 %copy-done.4 = bf16[2,32]{1,0:T(2,128)(2,1)S(1)} copy-done((bf16[2,32]{1,0:T(2,128)(2,1)S(1)}, bf16[2,32]{1,0:T(2,128)(2,1)}, u32[]{:S(2)}) %copy-start.4) | copy-done | bytes 152
  12.9 0.4 shard_map.165
  13.3 9.1 %shard_map.166 = (f32[4,192,128]{2,1,0:T(8,128)S(1)}, f32[384,128]{1,0:T(8,128)S(1)}, f32[4,3,4,128]{3,2,1,0:T(4,128)S(1)}) custom-call(f32[96,128]{1,0:T(8,128)S(1)} %copy-done.5, f32[96,128]{1,0:T(8,128)S(1)} %collective-permute-done.refs_1_, f32[96,128]{1,0:T(8,128)S(1)} %collective-permute-done.1.refs_2_, ...), custom_call_target="tpu_custom_call", output_to_operand_aliasing={{0}: (5, {})} | custom-call | flops 4000000000 | bytes 4000000 | tf_op jit(solution)/shard_map/pallas_call | solution.py:678
  22.6 1.2 %collective-permute-done.3 = f32[192,128]{1,0:T(8,128)S(1)} collective-permute-done((f32[192,128]{1,0:T(8,128)S(1)}, f32[192,128]{1,0:T(8,128)S(1)}, u32[]{:S(2)}, u32[]{:S(2)}) %collective-permute-start.3) | collective-permute-done | bytes 98336 | tf_op jit(solution)/shard_map/ppermute | solution.py:541
  23.9 2.5 %collective-permute-start.6 = (f32[96,128]{1,0:T(8,128)S(1)}, f32[96,128]{1,0:T(8,128)S(1)}, u32[]{:S(2)}, u32[]{:S(2)}) collective-permute-start(f32[96,128]{1,0:T(8,128)S(1)} %get-tuple-element.55), channel_id=1, source_target_pairs={{0,24},{4,28},{8,16},{12,20},{16,8},{20,12},{24,0},{28,4},{1,25},{... | collective-permute-start | bytes 147464 | tf_op jit(solution)/shard_map/ppermute | solution.py:541
  26.4 0.5 %collective-permute-start.4 = (f32[96,128]{1,0:T(8,128)S(1)}, f32[96,128]{1,0:T(8,128)S(1)}, u32[]{:S(2)}, u32[]{:S(2)}) collective-permute-start(f32[96,128]{1,0:T(8,128)S(1)} %get-tuple-element.55), channel_id=1, source_target_pairs={{0,8},{4,12},{8,0},{12,4},{16,24},{20,28},{24,16},{28,20},{1,9},{5... | collective-permute-start | bytes 147464 | tf_op jit(solution)/shard_map/ppermute | solution.py:541
  26.9 0.5 %collective-permute-start.5 = (f32[96,128]{1,0:T(8,128)S(1)}, f32[96,128]{1,0:T(8,128)S(1)}, u32[]{:S(2)}, u32[]{:S(2)}) collective-permute-start(f32[96,128]{1,0:T(8,128)S(1)} %get-tuple-element.54), channel_id=1, source_target_pairs={{0,16},{4,20},{8,24},{12,28},{16,0},{20,4},{24,8},{28,12},{1,17},{... | collective-permute-start | bytes 147464 | tf_op jit(solution)/shard_map/ppermute | solution.py:541
  27.5 1.7 %collective-permute-done.6 = f32[96,128]{1,0:T(8,128)S(1)} collective-permute-done((f32[96,128]{1,0:T(8,128)S(1)}, f32[96,128]{1,0:T(8,128)S(1)}, u32[]{:S(2)}, u32[]{:S(2)}) %collective-permute-start.6) | collective-permute-done | bytes 49184 | tf_op jit(solution)/shard_map/ppermute | solution.py:541
  29.2 1.9 %collective-permute-done.5 = f32[96,128]{1,0:T(8,128)S(1)} collective-permute-done((f32[96,128]{1,0:T(8,128)S(1)}, f32[96,128]{1,0:T(8,128)S(1)}, u32[]{:S(2)}, u32[]{:S(2)}) %collective-permute-start.5) | collective-permute-done | bytes 49184 | tf_op jit(solution)/shard_map/ppermute | solution.py:541
  31.1 2.1 %collective-permute-start.9 = (f32[108,128]{1,0:T(8,128)S(1)}, f32[108,128]{1,0:T(8,128)S(1)}, u32[]{:S(2)}, u32[]{:S(2)}) collective-permute-start(f32[108,128]{1,0:T(8,128)S(1)} %get-tuple-element.58), channel_id=1, source_target_pairs={{0,3},{1,0},{2,1},{3,2},{4,7},{5,4},{6,5},{7,6},{8,11},{9,8},{10,9... | collective-permute-start | bytes 165896 | tf_op jit(solution)/shard_map/ppermute | solution.py:545
  33.3 0.5 %collective-permute-start.7 = (f32[108,128]{1,0:T(8,128)S(1)}, f32[108,128]{1,0:T(8,128)S(1)}, u32[]{:S(2)}, u32[]{:S(2)}) collective-permute-start(f32[108,128]{1,0:T(8,128)S(1)} %get-tuple-element.56), channel_id=1, source_target_pairs={{0,1},{1,2},{2,3},{3,0},{4,5},{5,6},{6,7},{7,4},{8,9},{9,10},{10,1... | collective-permute-start | bytes 165896 | tf_op jit(solution)/shard_map/ppermute | solution.py:545
  33.8 1.8 %collective-permute-done.9 = f32[108,128]{1,0:T(8,128)S(1)} collective-permute-done((f32[108,128]{1,0:T(8,128)S(1)}, f32[108,128]{1,0:T(8,128)S(1)}, u32[]{:S(2)}, u32[]{:S(2)}) %collective-permute-start.9) | collective-permute-done | bytes 55328 | tf_op jit(solution)/shard_map/ppermute | solution.py:545
  35.6 2.7 %collective-permute-done.8 = f32[108,128]{1,0:T(8,128)S(1)} collective-permute-done((f32[108,128]{1,0:T(8,128)S(1)}, f32[108,128]{1,0:T(8,128)S(1)}, u32[]{:S(2)}, u32[]{:S(2)}) %collective-permute-start.8) | collective-permute-done | bytes 55328 | tf_op jit(solution)/shard_map/ppermute | solution.py:545
  38.3 1.0 %collective-permute-done.7 = f32[108,128]{1,0:T(8,128)S(1)} collective-permute-done((f32[108,128]{1,0:T(8,128)S(1)}, f32[108,128]{1,0:T(8,128)S(1)}, u32[]{:S(2)}, u32[]{:S(2)}) %collective-permute-start.7) | collective-permute-done | bytes 55328 | tf_op jit(solution)/shard_map/ppermute | solution.py:545
  39.3 1.6 %collective-permute-start.10 = (f32[96,128]{1,0:T(8,128)S(1)}, f32[96,128]{1,0:T(8,128)S(1)}, u32[]{:S(2)}, u32[]{:S(2)}) collective-permute-start(f32[96,128]{1,0:T(8,128)S(1)} %slice_add_fusion), channel_id=1, source_target_pairs={{0,8},{4,12},{8,0},{12,4},{16,24},{20,28},{24,16},{28,20},{1,9},{5... | collective-permute-start | bytes 147464 | tf_op jit(solution)/shard_map/ppermute | solution.py:541
  40.8 2.6 %collective-permute-done.10 = f32[96,128]{1,0:T(8,128)S(1)} collective-permute-done((f32[96,128]{1,0:T(8,128)S(1)}, f32[96,128]{1,0:T(8,128)S(1)}, u32[]{:S(2)}, u32[]{:S(2)}) %collective-permute-start.10) | collective-permute-done | bytes 49184 | tf_op jit(solution)/shard_map/ppermute | solution.py:541
  43.6 1.2 %collective-permute-done.11.refs_1_ = f32[192,128]{1,0:T(8,128)S(1)} collective-permute-done((f32[192,128]{1,0:T(8,128)S(1)}, f32[192,128]{1,0:T(8,128)S(1)}, u32[]{:S(2)}, u32[]{:S(2)}) %collective-permute-start.11) | collective-permute-done | bytes 98336 | tf_op jit(solution)/shard_map/ppermute | solution.py:541
  44.8 1.0 %shard_map.167 = (f32[1,4,1440]{2,1,0:T(4,128)}, f32[3,3,8,32]{3,2,1,0:T(8,128)}, f32[4,4,32,32]{3,2,1,0:T(8,128)}, f32[3,3,32,32]{3,2,1,0:T(8,128)}, f32[3,3,32,64]{3,2,1,0:T(8,128)}, /*index=5*/f32[2,32]{1,0:T(2,128)}) custom-call(f32[192,128]{1,0:T(8,128)S(1)} %maximum_select_fusion.refs_0_, f32[192,128]{1,0:T(8,128)S(1)} %collective-permute-done.11.refs_1_, ...), custom_call_target="tpu_custom_call" | custom-call | tf_op jit(solution)/shard_map/pallas_call | solution.py:723
  (36 shorter events, 0.5 us)
Async XLA Ops:
  2.3 11.1 %collective-permute-start = (f32[96,128]{1,0:T(8,128)}, f32[96,128]{1,0:T(8,128)S(1)}, u32[]{:S(2)}, u32[]{:S(2)}) collective-permute-start(f32[96,128]{1,0:T(8,128)} %get-tuple-element.31), channel_id=1, source_target_pairs={{0,1},{1,2},{2,3},{3,0},{4,5},{5,6},{6,7},{7,4},{8,9},{9,10},{10,1... | collective-permute-start | bytes 147464 | tf_op jit(solution)/shard_map/ppermute | solution.py:545
  5.3 8.0 %collective-permute-start.1 = (f32[96,128]{1,0:T(8,128)}, f32[96,128]{1,0:T(8,128)S(1)}, u32[]{:S(2)}, u32[]{:S(2)}) collective-permute-start(f32[96,128]{1,0:T(8,128)} %get-tuple-element.32), channel_id=1, source_target_pairs={{0,2},{1,3},{2,0},{3,1},{4,6},{5,7},{6,4},{7,5},{8,10},{9,11},{10,... | collective-permute-start | bytes 147464 | tf_op jit(solution)/shard_map/ppermute | solution.py:545
  7.9 5.4 %collective-permute-start.2 = (f32[96,128]{1,0:T(8,128)}, f32[96,128]{1,0:T(8,128)S(1)}, u32[]{:S(2)}, u32[]{:S(2)}) collective-permute-start(f32[96,128]{1,0:T(8,128)} %get-tuple-element.33), channel_id=1, source_target_pairs={{0,3},{1,0},{2,1},{3,2},{4,7},{5,4},{6,5},{7,6},{8,11},{9,8},{10,9... | collective-permute-start | bytes 147464 | tf_op jit(solution)/shard_map/ppermute | solution.py:545
  9.3 0.8 %copy-start.5 = (f32[96,128]{1,0:T(8,128)S(1)}, f32[96,128]{1,0:T(8,128)}, u32[]{:S(2)}) copy-start(f32[96,128]{1,0:T(8,128)} %get-tuple-element.30.refs_0_) | copy-start | bytes 147460
  9.3 0.8 %copy-start.6 = (f32[4]{0:T(128)S(1)}, f32[4]{0:T(128)}, u32[]{:S(2)}) copy-start(f32[4]{0:T(128)} %refs_4_.3) | copy-start | bytes 52
  10.1 2.1 %copy-start = (bf16[4,4,32,32]{3,2,1,0:T(8,128)(2,1)S(1)}, bf16[4,4,32,32]{3,2,1,0:T(8,128)(2,1)}, u32[]{:S(2)}) copy-start(bf16[4,4,32,32]{3,2,1,0:T(8,128)(2,1)} %refs_1_.5) | copy-start | bytes 98308
  10.1 2.2 %copy-start.1 = (bf16[3,3,32,32]{3,2,1,0:T(8,128)(2,1)S(1)}, bf16[3,3,32,32]{3,2,1,0:T(8,128)(2,1)}, u32[]{:S(2)}) copy-start(bf16[3,3,32,32]{3,2,1,0:T(8,128)(2,1)} %refs_2_.3) | copy-start | bytes 55300
  10.1 2.2 %copy-start.2 = (bf16[3,3,32,64]{3,2,1,0:T(8,128)(2,1)S(1)}, bf16[3,3,32,64]{3,2,1,0:T(8,128)(2,1)}, u32[]{:S(2)}) copy-start(bf16[3,3,32,64]{3,2,1,0:T(8,128)(2,1)} %refs_3_.3) | copy-start | bytes 110596
  10.1 2.2 %copy-start.3 = (bf16[3,3,32,8]{2,3,1,0:T(8,128)(2,1)S(1)}, bf16[3,3,32,8]{2,3,1,0:T(8,128)(2,1)}, u32[]{:S(2)}) copy-start(bf16[3,3,32,8]{2,3,1,0:T(8,128)(2,1)} %param.19) | copy-start | bytes 13828
  12.2 0.7 %copy-start.4 = (bf16[2,32]{1,0:T(2,128)(2,1)S(1)}, bf16[2,32]{1,0:T(2,128)(2,1)}, u32[]{:S(2)}) copy-start(bf16[2,32]{1,0:T(2,128)(2,1)} %refs_4_.2) | copy-start | bytes 388
  22.5 1.4 %collective-permute-start.3 = (f32[192,128]{1,0:T(8,128)S(1)}, f32[192,128]{1,0:T(8,128)S(1)}, u32[]{:S(2)}, u32[]{:S(2)}) collective-permute-start(f32[192,128]{1,0:T(8,128)S(1)} %constant_dynamic-slice_fusion.6), channel_id=1, source_target_pairs={{0,4},{4,0},{8,12},{12,8},{16,20},{20,16},{24,28},{28,24},{1,5},{5... | collective-permute-start | bytes 294920 | tf_op jit(solution)/shard_map/ppermute | solution.py:541
  23.9 5.3 %collective-permute-start.6 = (f32[96,128]{1,0:T(8,128)S(1)}, f32[96,128]{1,0:T(8,128)S(1)}, u32[]{:S(2)}, u32[]{:S(2)}) collective-permute-start(f32[96,128]{1,0:T(8,128)S(1)} %get-tuple-element.55), channel_id=1, source_target_pairs={{0,24},{4,28},{8,16},{12,20},{16,8},{20,12},{24,0},{28,4},{1,25},{... | collective-permute-start | bytes 147464 | tf_op jit(solution)/shard_map/ppermute | solution.py:541
  26.4 4.6 %collective-permute-start.4 = (f32[96,128]{1,0:T(8,128)S(1)}, f32[96,128]{1,0:T(8,128)S(1)}, u32[]{:S(2)}, u32[]{:S(2)}) collective-permute-start(f32[96,128]{1,0:T(8,128)S(1)} %get-tuple-element.55), channel_id=1, source_target_pairs={{0,8},{4,12},{8,0},{12,4},{16,24},{20,28},{24,16},{28,20},{1,9},{5... | collective-permute-start | bytes 147464 | tf_op jit(solution)/shard_map/ppermute | solution.py:541
  26.9 4.1 %collective-permute-start.5 = (f32[96,128]{1,0:T(8,128)S(1)}, f32[96,128]{1,0:T(8,128)S(1)}, u32[]{:S(2)}, u32[]{:S(2)}) collective-permute-start(f32[96,128]{1,0:T(8,128)S(1)} %get-tuple-element.54), channel_id=1, source_target_pairs={{0,16},{4,20},{8,24},{12,28},{16,0},{20,4},{24,8},{28,12},{1,17},{... | collective-permute-start | bytes 147464 | tf_op jit(solution)/shard_map/ppermute | solution.py:541
  31.1 4.5 %collective-permute-start.9 = (f32[108,128]{1,0:T(8,128)S(1)}, f32[108,128]{1,0:T(8,128)S(1)}, u32[]{:S(2)}, u32[]{:S(2)}) collective-permute-start(f32[108,128]{1,0:T(8,128)S(1)} %get-tuple-element.58), channel_id=1, source_target_pairs={{0,3},{1,0},{2,1},{3,2},{4,7},{5,4},{6,5},{7,6},{8,11},{9,8},{10,9... | collective-permute-start | bytes 165896 | tf_op jit(solution)/shard_map/ppermute | solution.py:545
  33.2 5.1 %collective-permute-start.8 = (f32[108,128]{1,0:T(8,128)S(1)}, f32[108,128]{1,0:T(8,128)S(1)}, u32[]{:S(2)}, u32[]{:S(2)}) collective-permute-start(f32[108,128]{1,0:T(8,128)S(1)} %get-tuple-element.57), channel_id=1, source_target_pairs={{0,2},{1,3},{2,0},{3,1},{4,6},{5,7},{6,4},{7,5},{8,10},{9,11},{10,... | collective-permute-start | bytes 165896 | tf_op jit(solution)/shard_map/ppermute | solution.py:545
  33.3 6.0 %collective-permute-start.7 = (f32[108,128]{1,0:T(8,128)S(1)}, f32[108,128]{1,0:T(8,128)S(1)}, u32[]{:S(2)}, u32[]{:S(2)}) collective-permute-start(f32[108,128]{1,0:T(8,128)S(1)} %get-tuple-element.56), channel_id=1, source_target_pairs={{0,1},{1,2},{2,3},{3,0},{4,5},{5,6},{6,7},{7,4},{8,9},{9,10},{10,1... | collective-permute-start | bytes 165896 | tf_op jit(solution)/shard_map/ppermute | solution.py:545
  39.3 4.2 %collective-permute-start.10 = (f32[96,128]{1,0:T(8,128)S(1)}, f32[96,128]{1,0:T(8,128)S(1)}, u32[]{:S(2)}, u32[]{:S(2)}) collective-permute-start(f32[96,128]{1,0:T(8,128)S(1)} %slice_add_fusion), channel_id=1, source_target_pairs={{0,8},{4,12},{8,0},{12,4},{16,24},{20,28},{24,16},{28,20},{1,9},{5... | collective-permute-start | bytes 147464 | tf_op jit(solution)/shard_map/ppermute | solution.py:541
  43.4 1.4 %collective-permute-start.11 = (f32[192,128]{1,0:T(8,128)S(1)}, f32[192,128]{1,0:T(8,128)S(1)}, u32[]{:S(2)}, u32[]{:S(2)}) collective-permute-start(f32[192,128]{1,0:T(8,128)S(1)} %maximum_select_fusion.refs_0_), channel_id=1, source_target_pairs={{0,4},{4,0},{8,12},{12,8},{16,20},{20,16},{24,28},{28,24},{1,5},{5... | collective-permute-start | bytes 294920 | tf_op jit(solution)/shard_map/ppermute | solution.py:541

commit v2 on v1

--- a/solution.py
+++ b/solution.py
@@ -57,16 +57,13 @@
 
 
 def sigmoid(values):
-    return 1.0 / (1.0 + jnp.exp(-values))
-
-
-def silu(values):
-    return values * sigmoid(values)
-
-
-def silu_slope(values):
+    return 0.5 + 0.5 * jnp.tanh(0.5 * values)
+
+
+def silu_and_slope(values):
     squash = sigmoid(values)
-    return squash * (1.0 + values * (1.0 - squash))
+    hidden = values * squash
+    return hidden, squash + hidden * (1.0 - squash)
 
 
 def split_three(values):
@@ -88,8 +85,8 @@
     lo_pos[...] = place - tile_of * LANES
 
     m_index = iota((32, 1), 0)
-    row_of = (m_index // 8).astype(F32)
-    scale_of = (m_index % 8) // 2
+    row_of = ((m_index % 8) // 2).astype(F32)
+    scale_of = m_index // 8
     kind_of = m_index % 2
     spread = jnp.where(
         scale_of == 0, scales[0], jnp.where(scale_of == 1, scales[1], jnp.where(scale_of == 2, scales[2], scales[3]))
@@ -116,15 +113,15 @@
 
 def pack_kernel(sizes, *refs):
     n_band, n_blocks, own, lon_count = sizes
-    pays = refs[6 : 6 + n_band]
-    wide = refs[6 + n_band]
-    held, sems = refs[7 + n_band : 13 + n_band], refs[13 + n_band]
-    copies = [pltpu.make_async_copy(refs[k], held[k], sems.at[k]) for k in range(6)]
+    pays = refs[7 : 7 + n_band]
+    wide = refs[7 + n_band]
+    held, sems = refs[8 + n_band : 15 + n_band], refs[15 + n_band]
+    copies = [pltpu.make_async_copy(refs[k], held[k], sems.at[k]) for k in range(7)]
     for copy in copies:
         copy.start()
     for copy in copies:
         copy.wait()
-    rows, lons, obs, live, block_band, field = held
+    rows, lons, obs, live, block_band, field, scales = held
     me = lax.axis_index("band")
     at_row = rows[0].astype(F32)
     lon = jnp.where(live[0] > 0, lons[0].astype(F32), FAR)
@@ -139,7 +136,8 @@
         pay[2 * n_blocks : 3 * n_blocks] = obs[0]
         pay[3 * n_blocks : 3 * n_blocks + 8] = jnp.zeros((8, LANES), F32)
         pay[3 * n_blocks : 3 * n_blocks + 1, 0:n_blocks] = block_band[...].astype(F32)
-        target = lax.rem(me + shift, n_band)
+        pay[3 * n_blocks + 1 : 3 * n_blocks + 2, 0:4] = scales[...]
+        target = me ^ shift
         for tile in range((own + 2 * HALO) // LANES):
             at = pl.multiple_of(target * own + tile * LANES, LANES)
             first = 3 * n_blocks + 8 + ROWS_BAND * tile
@@ -148,41 +146,49 @@
 
 def early_kernel(sizes, *refs):
     n_band, n_blocks, own, lon_count = sizes
-    pay, scales, hist, table, token, bands, hi_pos, lo_pos = refs
+    pay = refs[0]
+    hist, table, w1, wd, wm, wu, wh, wht, wf, wmf, wbd = refs[6:17]
+    bands, hi_pos, lo_pos, t1, td, tm, tu, tf, tmf, tbd = refs[17:27]
+    held, sems = refs[27:32], refs[32]
     me = lax.axis_index("band")
-    token[...] = jnp.zeros_like(token)
-    pltpu.sync_copy(pay.at[pl.ds(3 * n_blocks, 8)], bands)
-    hist[...] = jnp.zeros_like(hist)
-    step = n_blocks if n_band <= 4 else 4
-    station_sums(own, lon_count, n_blocks, step, me, pay, bands, scales, hist, hi_pos, lo_pos)
-
+    band_copy = pltpu.make_async_copy(pay.at[pl.ds(3 * n_blocks, 8)], bands, sems.at[5])
+    band_copy.start()
+    copies = [pltpu.make_async_copy(refs[1 + k], held[k], sems.at[k]) for k in range(5)]
+    for copy in copies:
+        copy.start()
     place_in = iota((4 * LANES, 2 * LANES), 0)
     place_out = iota((4 * LANES, 2 * LANES), 1)
     distance = (place_in - (REACH + 2 * (place_out % LANES) + place_out // LANES)).astype(F32)
     squared = distance * distance
+    band_copy.wait()
+    scales = [bands[1, k] for k in range(4)]
+    hist[...] = jnp.zeros_like(hist)
+    step = n_blocks if n_band <= 4 else 4
+    station_sums(own, lon_count, n_blocks, step, me, pay, bands, scales, hist, hi_pos, lo_pos)
     for scale in range(4):
         table[scale] = jnp.exp(squared * (-0.5 / (scales[scale] * scales[scale]))).astype(BF16)
 
-
-def matrix_kernel(*refs):
-    w_in, w_down, w_mid, w_up, w_head, _ = refs[:6]
-    w1, wd, wm, wu, wh, wht, wf, wmf, wbd = refs[6:15]
-    t1, td, tm, tu, tf, tmf, tbd = refs[15:]
-    t1[...] = jnp.zeros_like(t1)
-    tu[...] = jnp.zeros_like(tu)
-    tf[...] = jnp.zeros_like(tf)
-    tbd[...] = jnp.zeros_like(tbd)
+    for copy in copies:
+        copy.wait()
+    w_in, w_down, w_mid, w_up, w_head = held
+    for held in (t1, tm, tu, tf, tmf, tbd):
+        held[...] = jnp.zeros_like(held)
     for row in range(3):
         for col in range(3):
             inner = w_in[row, col].astype(F32)
             mid = w_mid[row, col].astype(F32)
             up = w_up[row, col].astype(F32)
-            tm[:, (row * 3 + col) * 32 : (row * 3 + col) * 32 + 32] = mid
             back = (2 - row) * 3 + 2 - col
-            tmf[back * 32 : back * 32 + 32, 0:32] = mid
+            for out in range(4):
+                at = out * 96 + (row * 3 + col) * 32
+                tm[out * 32 : out * 32 + 32, at : at + 32] = mid
+                at = out * 96 + back * 32
+                tmf[at : at + 32, out * 32 : out * 32 + 32] = mid
             for phase in range(2):
-                at = row * 32 + (phase + col) * 8
-                t1[at : at + 8, phase * 32 : phase * 32 + 32] = inner
+                for out in range(4):
+                    at = (out + row) * 32 + (phase + col) * 8
+                    to = out * 64 + phase * 32
+                    t1[at : at + 8, to : to + 32] = inner
                 for part in range(2):
                     cols = slice(part * 32, part * 32 + 32)
                     at = (row * 2 + part) * 128 + (phase + col) * 32
@@ -198,16 +204,24 @@
         for phase in range(2):
             for row, row_shift in sides[side]:
                 for col, col_shift in sides[phase]:
-                    at = (row_shift + 1) * 96 + (col_shift + 1) * 32
-                    to = (side * 2 + phase) * 32
-                    tbd[at : at + 32, to : to + 32] = w_down[row, col].astype(F32)
-    w1[...] = t1[...].T[0:64, 0:96].astype(BF16)
-    wd[...] = td[...].astype(BF16)
+                    for out in range(2):
+                        at = (out + row_shift + 1) * 96 + (col_shift + 1) * 32
+                        to = out * 128 + (side * 2 + phase) * 32
+                        tbd[at : at + 32, to : to + 32] = w_down[row, col].astype(F32)
+
+    def two_rows(one, shift):
+        empty = jnp.zeros((one.shape[0], shift), F32)
+        return jnp.concatenate(
+            [jnp.concatenate([one, empty], axis=1), jnp.concatenate([empty, one], axis=1)], axis=0
+        ).astype(BF16)
+
+    w1[...] = t1[...].T[:, 0:192].astype(BF16)
+    wd[...] = two_rows(td[...], 256)
     wm[...] = tm[...].astype(BF16)
-    wu[...] = tu[...].astype(BF16)
-    wf[...] = tf[...].T.astype(BF16)
-    wmf[...] = tmf[...].T[0:32, 0:288].astype(BF16)
-    wbd[...] = tbd[...].T[:, 0:288].astype(BF16)
+    wu[...] = two_rows(tu[...], 256)
+    wf[...] = two_rows(tf[...].T, 128)
+    wmf[...] = tmf[...].T[:, 0:576].astype(BF16)
+    wbd[...] = tbd[...].T.astype(BF16)
     heads = w_head[...].astype(F32)
     heads = jnp.concatenate([heads, jnp.zeros((6, 32), F32)], axis=0)
     heads = jnp.concatenate([heads, jnp.zeros((8, 96), F32)], axis=1)
@@ -230,13 +244,13 @@
     coarse = rows // 2
     own_tiles = own // LANES
     pays = refs[:n_band]
-    (scales, hist_own, table, w1, wd, wm, wu, wh, wht, wf, wmf, wbd) = refs[n_band : n_band + 12]
-    hist, grads_out, mean_out = refs[n_band + 12 : n_band + 15]
+    (hist_own, table, w1, wd, wm, wu, wh, wht, wf, wmf, wbd) = refs[n_band : n_band + 11]
+    hist, grads_out, mean_out = refs[n_band + 11 : n_band + 14]
     (
         bands, band_sems, zf, p1, zj, p2, z2, p3, p4, h4, truth, mean_split,
         gs, gp4m, gj, gp3m, zg3, gp2m, zg2, gp1m, hi_pos, lo_pos,
         acc_up, acc_down, acc_mid, acc_in, acc_head,
-    ) = refs[n_band + 15 :]
+    ) = refs[n_band + 14 :]
     many = n_band > 4
     me = lax.axis_index("band")
     cell_count = float(rows * lon_count)
@@ -247,37 +261,6 @@
     ]
     for copy in copies:
         copy.start()
-    for copy in copies:
-        copy.wait()
-    for source in range(1, n_band):
-        station_sums(
-            own, lon_count, n_blocks, 4 if many else n_blocks, me, pays[source], bands.at[source], scales,
-            hist, hi_pos.at[source], lo_pos.at[source],
-        )
-
-    all_rows = 32 * n_band
-    channel = iota((all_rows, 1), 0) % 8
-    feats = []
-    for chunk in range(half // LANES):
-        tiles = [
-            hist[:, (2 * chunk + t) * 32 : (2 * chunk + t + 1) * 32, :].reshape(all_rows, LANES)
-            for t in range(4)
-        ]
-        cells = jnp.concatenate(tiles, axis=1)
-        high = cells.astype(BF16)
-        low = (cells - high.astype(F32)).astype(BF16)
-        total = None
-        for scale in range(4):
-            keep = (channel // 2 == scale).astype(F32).astype(BF16)
-            part = dot(high * keep, table[scale]) + dot(low * keep, table[scale])
-            total = part if total is None else total + part
-        below = pltpu.roll(total, 1, 0)
-        density = jnp.where(channel % 2 == 0, total, below)
-        feats.append(total / (1.0 + density))
-    even = jnp.concatenate([f[:, :LANES] for f in feats], axis=1)
-    odd = jnp.concatenate([f[:, LANES:] for f in feats], axis=1)
-    odd_before = rolled(odd, 1)
-    even_after = rolled(even, -1)
     for edge in (0, rows + 1):
         zf[edge] = jnp.zeros((32, half), BF16)
         zj[edge] = jnp.zeros((256, half), BF16)
@@ -292,18 +275,12 @@
             z2[par, edge] = jnp.zeros((96, half), BF16)
             zg3[par, edge] = jnp.zeros((96, half), BF16)
             gp3m[par, edge] = jnp.zeros((32, half), BF16)
-    for row in range(rows):
-        pick = slice(row * 8, row * 8 + 8)
-        zf[row + 1] = jnp.concatenate(
-            [odd_before[pick], even[pick], odd[pick], even_after[pick]], axis=0
-        ).astype(BF16)
-
     fine_iota = iota((2 * LANES, 2 * LANES), 0)
     part_iota = iota((2 * LANES, 2 * LANES), 1)
     parting = (fine_iota == 2 * (part_iota % LANES) + part_iota // LANES).astype(F32).astype(BF16)
     chunks = window // (2 * LANES)
     for source in range(n_band):
-        at = lax.rem(me - source + n_band, n_band)
+        at = me ^ source
         pieces = []
         for chunk in range(2):
             if chunk < chunks:
@@ -325,41 +302,108 @@
                     chunk * 4 : chunk * 4 + 4, phase * LANES : (phase + 1) * LANES
                 ]
 
-    def first(row):
-        pre = dot(w1[...], zf[pl.ds(row, 3)].reshape(96, half))
-        p1[row] = pre
-        hidden = silu(pre)
-        zj[row + 1, 128:256, :] = four_shifts(hidden[:32], hidden[32:]).astype(BF16)
-
-    looped(rows, 4 if many else rows, first)
+    for copy in copies:
+        copy.wait()
+    scales = [bands[1, 1, k] for k in range(4)]
+    for source in range(1, n_band):
+        station_sums(
+            own, lon_count, n_blocks, 4 if many else n_blocks, me, pays[source], bands.at[source], scales,
+            hist, hi_pos.at[source], lo_pos.at[source],
+        )
+
+    eight = 8 * n_band
+    chunks = half // LANES
+    sub = iota((8, 1), 0)
+    per_scale = []
+    for scale in range(4):
+        stacked = []
+        for chunk in range(chunks):
+            tiles = [
+                hist[:, (2 * chunk + t) * 32 + 8 * scale : (2 * chunk + t) * 32 + 8 * scale + 8, :].reshape(eight, LANES)
+                for t in range(4)
+            ]
+            stacked.append(jnp.concatenate(tiles, axis=1))
+        cells = jnp.concatenate(stacked, axis=0)
+        high = cells.astype(BF16)
+        low = (cells - high.astype(F32)).astype(BF16)
+        both = dot(jnp.concatenate([high, low], axis=0), table[scale])
+        total = both[: chunks * eight] + both[chunks * eight :]
+        below = pltpu.roll(total, 1, 0)
+        density = jnp.where(iota((chunks * eight, 1), 0) % 2 == 0, total, below)
+        per_scale.append(total / (1.0 + density))
+
+    def phase_rows(phase):
+        lines = []
+        for band in range(n_band):
+            parts = [
+                jnp.concatenate(
+                    [
+                        per_scale[scale][
+                            chunk * eight + 8 * band : chunk * eight + 8 * band + 8,
+                            phase * LANES : (phase + 1) * LANES,
+                        ]
+                        for chunk in range(chunks)
+                    ],
+                    axis=1,
+                )
+                for scale in range(4)
+            ]
+            for row in range(ROWS_BAND):
+                line = None
+                for scale in range(4):
+                    turn = (2 * scale - 2 * row) % 8
+                    moved = pltpu.roll(parts[scale], turn, 0) if turn else parts[scale]
+                    line = moved if line is None else jnp.where(sub // 2 == scale, moved, line)
+                lines.append(line)
+        return jnp.concatenate(lines, axis=0)
+
+    even, odd = phase_rows(0), phase_rows(1)
+    odd_before = rolled(odd, 1)
+    even_after = rolled(even, -1)
+    for row in range(rows):
+        pick = slice(row * 8, row * 8 + 8)
+        zf[row + 1] = jnp.concatenate(
+            [odd_before[pick], even[pick], odd[pick], even_after[pick]], axis=0
+        ).astype(BF16)
+
+    def first(group):
+        pre = dot(w1[...], zf[pl.ds(4 * group, 6)].reshape(192, half))
+        for out in range(4):
+            row = 4 * group + out
+            hidden, p1[row] = silu_and_slope(pre[64 * out : 64 * out + 64])
+            zj[row + 1, 128:256, :] = four_shifts(hidden[:32], hidden[32:]).astype(BF16)
+
+    looped(n_band, 1 if many else n_band, first)
 
     def second(index):
+        pre = dot(wd[...], zj[pl.ds(4 * index, 6), 128:256, :].reshape(768, half))
         for par in range(2):
             row = 2 * index + par
-            pre = dot(wd[...], zj[pl.ds(2 * row, 4), 128:256, :].reshape(512, half))
-            p2[row] = pre
-            z2[par, index + 1] = three_shifts(silu(pre), 2).astype(BF16)
+            hidden, p2[row] = silu_and_slope(pre[32 * par : 32 * par + 32])
+            z2[par, index + 1] = three_shifts(hidden, 2).astype(BF16)
 
     looped(coarse // 2, 4 if many else coarse // 2, second)
 
-    def third(index):
+    def third(group):
         for par in range(2):
-            row = 2 * index + par
-            pre = dot(wm[...], z2[par, pl.ds(index, 3)].reshape(288, half))
-            p3[row] = pre
-            hidden = silu(pre)
-            wide = four_shifts(hidden, hidden).astype(BF16)
-            zj[2 * row + 1, 0:128, :] = wide
-            zj[2 * row + 2, 0:128, :] = wide
-
-    looped(coarse // 2, 4 if many else coarse // 2, third)
-
-    def fourth(row):
-        pre = dot(wu[...], zj[pl.ds(row, 3)].reshape(768, half))
-        p4[row] = pre
-        h4[row] = silu(pre).astype(BF16)
-
-    looped(rows, 4 if many else rows, fourth)
+            pre = dot(wm[...], z2[par, pl.ds(4 * group, 6)].reshape(576, half))
+            for out in range(4):
+                row = 2 * (4 * group + out) + par
+                hidden, p3[row] = silu_and_slope(pre[32 * out : 32 * out + 32])
+                wide = four_shifts(hidden, hidden).astype(BF16)
+                zj[2 * row + 1, 0:128, :] = wide
+                zj[2 * row + 2, 0:128, :] = wide
+
+    looped(coarse // 8, 1, third)
+
+    def fourth(pair):
+        pre = dot(wu[...], zj[pl.ds(2 * pair, 4)].reshape(1024, half))
+        for out in range(2):
+            row = 2 * pair + out
+            hidden, p4[row] = silu_and_slope(pre[64 * out : 64 * out + 64])
+            h4[row] = hidden.astype(BF16)
+
+    looped(rows // 2, 2 if many else rows // 2, fourth)
 
     own_cells = jnp.clip(lon_count - me * own, 0, own) // 2
     place = iota((1, half), 1)
@@ -381,8 +425,7 @@
         grad_bf = grad_out.astype(BF16)
         acc_head[...] += dot_lanes((grad_out * mask).astype(BF16), hidden)
         back = dot(wht[...], grad_bf)
-        pre = p4[pl.ds(4 * group, 4)].reshape(256, half)
-        grad = back * silu_slope(pre)
+        grad = back * p4[pl.ds(4 * group, 4)].reshape(256, half)
         for row in range(4):
             mine = grad[row * 64 : row * 64 + 64]
             gp4m[4 * group + row + 1] = (mine * mask).astype(BF16)
@@ -407,38 +450,39 @@
     def join_back(index):
         for par in range(2):
             row = 2 * index + par
+            back = dot(wf[...], gs[pl.ds(2 * row, 4)].reshape(512, half)).astype(BF16)
             total = None
             for side in range(2):
-                fine = 2 * row + side
-                back = dot(wf[...], gs[pl.ds(fine, 3)].reshape(384, half)).astype(BF16)
-                gj[fine] = back[64:]
-                up = back[:64].astype(F32)
+                mine = back[128 * side : 128 * side + 128]
+                gj[2 * row + side] = mine[64:]
+                up = mine[:64].astype(F32)
                 part = up[:32] + up[32:]
                 total = part if total is None else total + part
-            grad = total * silu_slope(p3[row])
+            grad = total * p3[row]
             gp3m[par, index + 1] = (grad * mask).astype(BF16)
             zg3[par, index + 1] = three_shifts(grad, 2).astype(BF16)
 
     looped(coarse // 2, 2 if many else coarse // 2, join_back)
 
-    def mid_back(index):
+    def mid_back(group):
         for par in range(2):
-            row = 2 * index + par
-            back = dot(wmf[...], zg3[par, pl.ds(index, 3)].reshape(288, half))
-            grad = back * silu_slope(p2[row])
-            gp2m[row + 1] = (grad * mask).astype(BF16)
-            zg2[row + 1] = three_shifts(grad, 1).astype(BF16)
-
-    looped(coarse // 2, 4 if many else coarse // 2, mid_back)
-
-    def down_back(row):
-        back = dot(wbd[...], zg2[pl.ds(row, 3)].reshape(288, half))
-        for side in range(2):
-            fine = 2 * row + side
-            grad = (back[64 * side : 64 * side + 64] + gj[fine].astype(F32)) * silu_slope(p1[fine])
+            back = dot(wmf[...], zg3[par, pl.ds(4 * group, 6)].reshape(576, half))
+            for out in range(4):
+                row = 2 * (4 * group + out) + par
+                grad = back[32 * out : 32 * out + 32] * p2[row]
+                gp2m[row + 1] = (grad * mask).astype(BF16)
+                zg2[row + 1] = three_shifts(grad, 1).astype(BF16)
+
+    looped(coarse // 8, 1, mid_back)
+
+    def down_back(pair):
+        back = dot(wbd[...], zg2[pl.ds(2 * pair, 4)].reshape(384, half))
+        for out in range(4):
+            fine = 4 * pair + out
+            grad = (back[64 * out : 64 * out + 64] + gj[fine].astype(F32)) * p1[fine]
             gp1m[fine + 1] = (grad * mask).astype(BF16)
 
-    looped(coarse, 4 if many else coarse, down_back)
+    looped(coarse // 2, 2 if many else coarse // 2, down_back)
 
     acc_up[...] = jnp.zeros_like(acc_up)
     acc_down[...] = jnp.zeros_like(acc_down)
@@ -607,73 +651,66 @@
     pay_rows = 3 * n_blocks + 8 + -(-(window // LANES) * ROWS_BAND // 8) * 8
     wide_lanes = (n_band * own_tiles + 1) * LANES
     in_vmem = pl.BlockSpec(memory_space=pltpu.VMEM)
-    in_smem = pl.BlockSpec(memory_space=pltpu.SMEM)
     in_hbm = pl.BlockSpec(memory_space=pltpu.HBM)
+
+    def in_place(arg):
+        return pltpu.with_memory_space_constraint(arg, pltpu.HBM)
 
     def shaped(*shape, dtype=BF16):
         return jax.ShapeDtypeStruct(shape, dtype)
 
     arrays = (
-        station_rows, station_lons, station_obs, station_live, block_band.reshape(1, n_blocks), truth_field
+        station_rows, station_lons, station_obs, station_live, block_band.reshape(1, n_blocks), truth_field,
+        length_scales.reshape(1, 4),
     )
     packed = pl.pallas_call(
         functools.partial(pack_kernel, sizes),
         out_shape=(shaped(pay_rows, LANES, dtype=F32),) * n_band,
-        in_specs=[in_hbm] * 6,
+        in_specs=[in_hbm] * 7,
         out_specs=(in_vmem,) * n_band,
         scratch_shapes=[vmem(ROWS_BAND, wide_lanes, dtype=F32)]
         + [vmem(*arg.shape, dtype=arg.dtype) for arg in arrays]
-        + [pltpu.SemaphoreType.DMA((6,))],
-        compiler_params=pltpu.CompilerParams(vmem_limit_bytes=56 * 1024 * 1024),
-    )(*arrays)
-    pays = [packed[0]] + [shifted(packed[k], "band", n_band, k) for k in range(1, n_band)]
+        + [pltpu.SemaphoreType.DMA((7,))],
+        compiler_params=pltpu.CompilerParams(vmem_limit_bytes=8 * 1024 * 1024),
+    )(*[in_place(arg) for arg in arrays])
+    pays = [packed[0]] + [swapped(packed[k], "band", n_band, k) for k in range(1, n_band)]
 
     hist_shape = (n_band, hist_tiles * 32, LANES)
-    hist, table, token = pl.pallas_call(
+    weights = (jnp.transpose(w_in, (0, 1, 3, 2)), w_down, w_mid, w_up, w_head)
+    early = pl.pallas_call(
         functools.partial(early_kernel, sizes),
         out_shape=(
             shaped(*hist_shape, dtype=F32),
             shaped(4, 4 * LANES, 2 * LANES),
-            shaped(8, LANES, dtype=F32),
+            shaped(256, 192),
+            shaped(64, 768),
+            shaped(128, 576),
+            shaped(128, 1024),
+            shaped(16, 256),
+            shaped(256, 16),
+            shaped(256, 512),
+            shaped(128, 576),
+            shaped(256, 384),
         ),
-        in_specs=[in_vmem, in_smem],
-        out_specs=(in_vmem,) * 3,
+        in_specs=[in_vmem] + [in_hbm] * 5,
+        out_specs=(in_vmem,) * 11,
         scratch_shapes=[
             pltpu.SMEM((8, LANES), F32),
             vmem(n_blocks, LANES, dtype=F32),
             vmem(n_blocks, LANES, dtype=F32),
-        ],
+            vmem(256, 256, dtype=F32),
+            vmem(32, 512, dtype=F32),
+            vmem(128, 576, dtype=F32),
+            vmem(64, 768, dtype=F32),
+            vmem(384, 128, dtype=F32),
+            vmem(640, 128, dtype=F32),
+            vmem(384, 256, dtype=F32),
+        ]
+        + [vmem(*arg.shape) for arg in weights]
+        + [pltpu.SemaphoreType.DMA((6,))],
         compiler_params=pltpu.CompilerParams(vmem_limit_bytes=16 * 1024 * 1024),
         cost_estimate=pl.CostEstimate(flops=200_000_000, bytes_accessed=2_000_000, transcendentals=700_000),
-    )(packed[0], length_scales)
-    mats = pl.pallas_call(
-        matrix_kernel,
-        out_shape=(
-            shaped(64, 96),
-            shaped(32, 512),
-            shaped(32, 288),
-            shaped(64, 768),
-            shaped(16, 256),
-            shaped(256, 16),
-            shaped(128, 384),
-            shaped(32, 288),
-            shaped(128, 288),
-        ),
-        in_specs=[in_vmem] * 6,
-        out_specs=(in_vmem,) * 9,
-        scratch_shapes=[
-            vmem(128, 128, dtype=F32),
-            vmem(32, 512, dtype=F32),
-            vmem(32, 288, dtype=F32),
-            vmem(64, 768, dtype=F32),
-            vmem(384, 128, dtype=F32),
-            vmem(384, 128, dtype=F32),
-            vmem(384, 128, dtype=F32),
-        ],
-        compiler_params=pltpu.CompilerParams(vmem_limit_bytes=16 * 1024 * 1024),
-        cost_estimate=pl.CostEstimate(flops=10_000_000, bytes_accessed=1_000_000, transcendentals=0),
-    )(jnp.transpose(w_in, (0, 1, 3, 2)), w_down, w_mid, w_up, w_head, token)
-    early = (hist, table) + tuple(mats)
+    )(packed[0], *[in_place(arg) for arg in weights])
 
     _, grads, mean_tiles = pl.pallas_call(
         functools.partial(network_kernel, sizes),
@@ -682,9 +719,9 @@
             shaped(384, LANES, dtype=F32),
             shaped(n_band, own_tiles, ROWS_BAND, LANES, dtype=F32),
         ),
-        in_specs=[in_vmem] * n_band + [in_smem] + [in_vmem] * 11,
+        in_specs=[in_vmem] * (n_band + 11),
         out_specs=(in_vmem, in_vmem, in_vmem),
-        input_output_aliases={n_band + 1: 0},
+        input_output_aliases={n_band: 0},
         scratch_shapes=[
             pltpu.SMEM((n_band, 8, LANES), F32),
             pltpu.SemaphoreType.DMA((n_band,)),
@@ -716,7 +753,7 @@
         ],
         compiler_params=pltpu.CompilerParams(vmem_limit_bytes=40 * 1024 * 1024),
         cost_estimate=pl.CostEstimate(flops=4_000_000_000, bytes_accessed=4_000_000, transcendentals=2_000_000),
-    )(*pays, length_scales, *early)
+    )(*pays, *early)
 
     low, high, means = reduced(grads, mean_tiles.reshape(n_band, own_tiles * ROWS_BAND, LANES), n_band, n_group)
     means = [piece.reshape(own_tiles, ROWS_BAND, LANES) for piece in means]

time: 46 us -> 43.6 us (0.948)
  waiting for transfers between devices: 14.1 us -> 17.1 us
  Pallas kernels: 14.2 us -> 12 us
  starting transfers between devices: 15 us -> 13.4 us
  local copies, waits for them, and re-layouts: 1.54 us -> 0.11 us
    ppermute x6 -> x3, starting transfers between devices: 9.73 us -> 2.44 us  [shifted(): lax.ppermute(values, axis, [(i, (i + shift) % count) for i in range(count)])]
    ppermute x6 -> x9, starting transfers between devices: 5.25 us -> 10.9 us  [swapped(): return lax.ppermute(values, axis, [(i, i ^ bits) for i in range(count)])]
    ppermute x6 -> x9, waiting for transfers between devices: 8.64 us -> 12.3 us  [swapped(): return lax.ppermute(values, axis, [(i, i ^ bits) for i in range(count)])]
    unnamed x16 -> x2, local copies, waits for them, and re-layouts: 1.43 us -> 0.01 us
    pallas_call x1, Pallas kernels: 9.11 us -> 7.81 us  [local(): pl.pallas_call(functools.partial(network_kernel, sizes), out_shape=(shape...]
    ppermute x6 -> x3, waiting for transfers between devices: 5.46 us -> 4.77 us  [shifted(): lax.ppermute(values, axis, [(i, (i + shift) % count) for i in range(count)])]
    pallas_call x1, Pallas kernels: 1.62 us -> 0.98 us  [local(): pl.pallas_call(functools.partial(pack_kernel, sizes), out_shape=(shaped(p...]
  transfers between devices with their start and end apart: 12 -> 12, of which waited for: 8 -> 10; matrix products, arithmetic and copies ran while one was open for 0% -> 0% of each run, Pallas kernels for 6% -> 5%
where the time goes in v2:
time: 43.6 us; the launch traced here: 43.3 us
  waiting for transfers between devices  17.1 us (39%)
  starting transfers between devices  13.4 us (31%)
  Pallas kernels  12 us (28%)
  between operations  0.78 us (2%)
    ppermute x9, waiting for transfers between devices, swapped(): return lax.ppermute(values, axis, [(i, i ^ bits) for i in range(count)])  12.3 us
    ppermute x9, starting transfers between devices, swapped(): return lax.ppermute(values, axis, [(i, i ^ bits) for i in range(count)])  10.9 us
    pallas_call x1, Pallas kernels, local(): pl.pallas_call(functools.partial(network_kernel, sizes), out_shape=(shape...  7.81 us
    ppermute x3, waiting for transfers between devices, shifted(): lax.ppermute(values, axis, [(i, (i + shift) % count) for i in range(count)])  4.77 us
    ppermute x3, starting transfers between devices, shifted(): lax.ppermute(values, axis, [(i, (i + shift) % count) for i in range(count)])  2.44 us
    pallas_call x1, Pallas kernels, local(): pl.pallas_call(functools.partial(early_kernel, sizes), out_shape=(shaped(...  2.21 us
    pallas_call x1, Pallas kernels, local(): pl.pallas_call(functools.partial(pack_kernel, sizes), out_shape=(shaped(p...  0.98 us
    pallas_call x1, Pallas kernels, local(): pl.pallas_call(functools.partial(unpack_kernel, (n_band, own, lon_count))...  0.95 us
  transfers between devices with their start and end apart: 12, of which 10 were waited for; matrix products, arithmetic and copies ran while one was open for 0% of the time, Pallas kernels for 5%

profile of v2, /device:TPU:0, one launch (start us, length us, event | category | flops | bytes accessed | tf_op | source)
XLA Modules:
  0.0 43.3 jit_solution(17460230945451702915)
XLA Ops:
  0.6 1.0 %shard_map.163 = (f32[96,128]{1,0:T(8,128)S(1)}, f32[96,128]{1,0:T(8,128)S(1)}, f32[96,128]{1,0:T(8,128)S(1)}, f32[96,128]{1,0:T(8,128)S(1)}) custom-call(s32[1,24,128]{2,1,0:T(8,128)} %refs_0_.1, s32[1,24,128]{2,1,0:T(8,128)} %refs_1_.1, f32[1,24,128]{2,1,0:T(8,128)} %refs_2_.2, s32[1,24,128]{2,1,0:T(8,128)} %refs_3_.2, s32[1,24]{1,0:T(1,128)} %bitcast.16, ...), custom_call_target="tpu_custom_call" | custom-call | tf_op jit(solution)/shard_map/pallas_call | solution.py:666
  1.6 3.1 %collective-permute-start = (f32[96,128]{1,0:T(8,128)S(1)}, f32[96,128]{1,0:T(8,128)S(1)}, u32[]{:S(2)}, u32[]{:S(2)}) collective-permute-start(f32[96,128]{1,0:T(8,128)S(1)} %get-tuple-element.30), channel_id=1, source_target_pairs={{0,1},{1,0},{2,3},{3,2},{4,5},{5,4},{6,7},{7,6},{8,9},{9,8},{10,11... | collective-permute-start | bytes 147464 | tf_op jit(solution)/shard_map/ppermute | solution.py:585
  4.7 2.6 %collective-permute-start.1 = (f32[96,128]{1,0:T(8,128)S(1)}, f32[96,128]{1,0:T(8,128)S(1)}, u32[]{:S(2)}, u32[]{:S(2)}) collective-permute-start(f32[96,128]{1,0:T(8,128)S(1)} %get-tuple-element.31), channel_id=1, source_target_pairs={{0,2},{1,3},{2,0},{3,1},{4,6},{5,7},{6,4},{7,5},{8,10},{9,11},{10,... | collective-permute-start | bytes 147464 | tf_op jit(solution)/shard_map/ppermute | solution.py:585
  7.3 2.2 %shard_map.164 = (f32[4,192,128]{2,1,0:T(8,128)S(1)}, bf16[4,512,256]{2,1,0:T(8,128)(2,1)S(1)}, bf16[256,192]{1,0:T(8,128)(2,1)S(1)}, bf16[64,768]{1,0:T(8,128)(...) custom-call(f32[96,128]{1,0:T(8,128)S(1)} %get-tuple-element.29.refs, ...), custom_call_target="tpu_custom_call" | custom-call | flops 200000000 | bytes 2000000 | tf_op jit(solution)/shard_map/pallas_call | solution.py:680
  9.5 1.1 %collective-permute-done.1.refs_2_ = f32[96,128]{1,0:T(8,128)S(1)} collective-permute-done((f32[96,128]{1,0:T(8,128)S(1)}, f32[96,128]{1,0:T(8,128)S(1)}, u32[]{:S(2)}, u32[]{:S(2)}) %collective-permute-start.1) | collective-permute-done | bytes 49184 | tf_op jit(solution)/shard_map/ppermute | solution.py:585
  10.6 2.6 %collective-permute-done.2.refs_3_ = f32[96,128]{1,0:T(8,128)S(1)} collective-permute-done((f32[96,128]{1,0:T(8,128)S(1)}, f32[96,128]{1,0:T(8,128)S(1)}, u32[]{:S(2)}, u32[]{:S(2)}) %collective-permute-start.2) | collective-permute-done | bytes 49184 | tf_op jit(solution)/shard_map/ppermute | solution.py:585
  13.2 7.8 %shard_map.165 = (f32[4,192,128]{2,1,0:T(8,128)S(1)}, f32[384,128]{1,0:T(8,128)S(1)}, f32[4,3,4,128]{3,2,1,0:T(4,128)S(1)}) custom-call(f32[96,128]{1,0:T(8,128)S(1)} %get-tuple-element.29.refs_0_, f32[96,128]{1,0:T(8,128)S(1)} %collective-permute-done.refs_1_, f32[96,128]{1,0:T(8,128)S(1)} %collective-permute-done.1.refs_2_, ...), custom_call_target="tpu_custom_call", output_to_operand_aliasing={{0}: (4, {})} | custom-call | flops 4000000000 | bytes 4000000 | tf_op jit(solution)/shard_map/pallas_call | solution.py:715
  21.0 0.1 collective-permute-start.3
  21.2 1.2 %collective-permute-done.3 = f32[192,128]{1,0:T(8,128)S(1)} collective-permute-done((f32[192,128]{1,0:T(8,128)S(1)}, f32[192,128]{1,0:T(8,128)S(1)}, u32[]{:S(2)}, u32[]{:S(2)}) %collective-permute-start.3) | collective-permute-done | bytes 98336 | tf_op jit(solution)/shard_map/ppermute | solution.py:585
  22.4 2.5 %collective-permute-start.6 = (f32[96,128]{1,0:T(8,128)S(1)}, f32[96,128]{1,0:T(8,128)S(1)}, u32[]{:S(2)}, u32[]{:S(2)}) collective-permute-start(f32[96,128]{1,0:T(8,128)S(1)} %get-tuple-element.53), channel_id=1, source_target_pairs={{0,24},{4,28},{8,16},{12,20},{16,8},{20,12},{24,0},{28,4},{1,25},{... | collective-permute-start | bytes 147464 | tf_op jit(solution)/shard_map/ppermute | solution.py:585
  25.0 0.5 %collective-permute-start.4 = (f32[96,128]{1,0:T(8,128)S(1)}, f32[96,128]{1,0:T(8,128)S(1)}, u32[]{:S(2)}, u32[]{:S(2)}) collective-permute-start(f32[96,128]{1,0:T(8,128)S(1)} %get-tuple-element.53), channel_id=1, source_target_pairs={{0,8},{4,12},{8,0},{12,4},{16,24},{20,28},{24,16},{28,20},{1,9},{5... | collective-permute-start | bytes 147464 | tf_op jit(solution)/shard_map/ppermute | solution.py:585
  25.5 0.5 %collective-permute-start.5 = (f32[96,128]{1,0:T(8,128)S(1)}, f32[96,128]{1,0:T(8,128)S(1)}, u32[]{:S(2)}, u32[]{:S(2)}) collective-permute-start(f32[96,128]{1,0:T(8,128)S(1)} %get-tuple-element.52), channel_id=1, source_target_pairs={{0,16},{4,20},{8,24},{12,28},{16,0},{20,4},{24,8},{28,12},{1,17},{... | collective-permute-start | bytes 147464 | tf_op jit(solution)/shard_map/ppermute | solution.py:585
  26.0 1.7 %collective-permute-done.6 = f32[96,128]{1,0:T(8,128)S(1)} collective-permute-done((f32[96,128]{1,0:T(8,128)S(1)}, f32[96,128]{1,0:T(8,128)S(1)}, u32[]{:S(2)}, u32[]{:S(2)}) %collective-permute-start.6) | collective-permute-done | bytes 49184 | tf_op jit(solution)/shard_map/ppermute | solution.py:585
  27.7 1.9 %collective-permute-done.5 = f32[96,128]{1,0:T(8,128)S(1)} collective-permute-done((f32[96,128]{1,0:T(8,128)S(1)}, f32[96,128]{1,0:T(8,128)S(1)}, u32[]{:S(2)}, u32[]{:S(2)}) %collective-permute-start.5) | collective-permute-done | bytes 49184 | tf_op jit(solution)/shard_map/ppermute | solution.py:585
  29.6 0.8 %collective-permute-start.9 = (f32[108,128]{1,0:T(8,128)S(1)}, f32[108,128]{1,0:T(8,128)S(1)}, u32[]{:S(2)}, u32[]{:S(2)}) collective-permute-start(f32[108,128]{1,0:T(8,128)S(1)} %get-tuple-element.56), channel_id=1, source_target_pairs={{0,3},{1,0},{2,1},{3,2},{4,7},{5,4},{6,5},{7,6},{8,11},{9,8},{10,9... | collective-permute-start | bytes 165896 | tf_op jit(solution)/shard_map/ppermute | solution.py:589
  30.4 1.6 %collective-permute-start.7 = (f32[108,128]{1,0:T(8,128)S(1)}, f32[108,128]{1,0:T(8,128)S(1)}, u32[]{:S(2)}, u32[]{:S(2)}) collective-permute-start(f32[108,128]{1,0:T(8,128)S(1)} %get-tuple-element.54), channel_id=1, source_target_pairs={{0,1},{1,2},{2,3},{3,0},{4,5},{5,6},{6,7},{7,4},{8,9},{9,10},{10,1... | collective-permute-start | bytes 165896 | tf_op jit(solution)/shard_map/ppermute | solution.py:589
  32.1 2.1 %collective-permute-done.9 = f32[108,128]{1,0:T(8,128)S(1)} collective-permute-done((f32[108,128]{1,0:T(8,128)S(1)}, f32[108,128]{1,0:T(8,128)S(1)}, u32[]{:S(2)}, u32[]{:S(2)}) %collective-permute-start.9) | collective-permute-done | bytes 55328 | tf_op jit(solution)/shard_map/ppermute | solution.py:589
  34.2 1.3 %collective-permute-done.8 = f32[108,128]{1,0:T(8,128)S(1)} collective-permute-done((f32[108,128]{1,0:T(8,128)S(1)}, f32[108,128]{1,0:T(8,128)S(1)}, u32[]{:S(2)}, u32[]{:S(2)}) %collective-permute-start.8) | collective-permute-done | bytes 55328 | tf_op jit(solution)/shard_map/ppermute | solution.py:589
  35.5 1.3 %collective-permute-done.7 = f32[108,128]{1,0:T(8,128)S(1)} collective-permute-done((f32[108,128]{1,0:T(8,128)S(1)}, f32[108,128]{1,0:T(8,128)S(1)}, u32[]{:S(2)}, u32[]{:S(2)}) %collective-permute-start.7) | collective-permute-done | bytes 55328 | tf_op jit(solution)/shard_map/ppermute | solution.py:589
  36.8 1.6 %collective-permute-start.10 = (f32[96,128]{1,0:T(8,128)S(1)}, f32[96,128]{1,0:T(8,128)S(1)}, u32[]{:S(2)}, u32[]{:S(2)}) collective-permute-start(f32[96,128]{1,0:T(8,128)S(1)} %slice_add_fusion), channel_id=1, source_target_pairs={{0,8},{4,12},{8,0},{12,4},{16,24},{20,28},{24,16},{28,20},{1,9},{5... | collective-permute-start | bytes 147464 | tf_op jit(solution)/shard_map/ppermute | solution.py:585
  38.4 2.6 %collective-permute-done.10 = f32[96,128]{1,0:T(8,128)S(1)} collective-permute-done((f32[96,128]{1,0:T(8,128)S(1)}, f32[96,128]{1,0:T(8,128)S(1)}, u32[]{:S(2)}, u32[]{:S(2)}) %collective-permute-start.10) | collective-permute-done | bytes 49184 | tf_op jit(solution)/shard_map/ppermute | solution.py:585
  41.0 0.1 collective-permute-start.11
  41.2 1.2 %collective-permute-done.11.refs_1_ = f32[192,128]{1,0:T(8,128)S(1)} collective-permute-done((f32[192,128]{1,0:T(8,128)S(1)}, f32[192,128]{1,0:T(8,128)S(1)}, u32[]{:S(2)}, u32[]{:S(2)}) %collective-permute-start.11) | collective-permute-done | bytes 98336 | tf_op jit(solution)/shard_map/ppermute | solution.py:585
  42.4 1.0 %shard_map.166 = (f32[1,4,1440]{2,1,0:T(4,128)}, f32[3,3,8,32]{3,2,1,0:T(8,128)}, f32[4,4,32,32]{3,2,1,0:T(8,128)}, f32[3,3,32,32]{3,2,1,0:T(8,128)}, f32[3,3,32,64]{3,2,1,0:T(8,128)}, /*index=5*/f32[2,32]{1,0:T(2,128)}) custom-call(f32[192,128]{1,0:T(8,128)S(1)} %maximum_select_fusion.refs_0_, f32[192,128]{1,0:T(8,128)S(1)} %collective-permute-done.11.refs_1_, ...), custom_call_target="tpu_custom_call" | custom-call | tf_op jit(solution)/shard_map/pallas_call | solution.py:760
  (21 shorter events, 0.2 us)
Async XLA Ops:
  1.6 7.9 %collective-permute-start = (f32[96,128]{1,0:T(8,128)S(1)}, f32[96,128]{1,0:T(8,128)S(1)}, u32[]{:S(2)}, u32[]{:S(2)}) collective-permute-start(f32[96,128]{1,0:T(8,128)S(1)} %get-tuple-element.30), channel_id=1, source_target_pairs={{0,1},{1,0},{2,3},{3,2},{4,5},{5,4},{6,7},{7,6},{8,9},{9,8},{10,11... | collective-permute-start | bytes 147464 | tf_op jit(solution)/shard_map/ppermute | solution.py:585
  4.7 5.9 %collective-permute-start.1 = (f32[96,128]{1,0:T(8,128)S(1)}, f32[96,128]{1,0:T(8,128)S(1)}, u32[]{:S(2)}, u32[]{:S(2)}) collective-permute-start(f32[96,128]{1,0:T(8,128)S(1)} %get-tuple-element.31), channel_id=1, source_target_pairs={{0,2},{1,3},{2,0},{3,1},{4,6},{5,7},{6,4},{7,5},{8,10},{9,11},{10,... | collective-permute-start | bytes 147464 | tf_op jit(solution)/shard_map/ppermute | solution.py:585
  7.3 5.9 %collective-permute-start.2 = (f32[96,128]{1,0:T(8,128)S(1)}, f32[96,128]{1,0:T(8,128)S(1)}, u32[]{:S(2)}, u32[]{:S(2)}) collective-permute-start(f32[96,128]{1,0:T(8,128)S(1)} %get-tuple-element.32), channel_id=1, source_target_pairs={{0,3},{1,2},{2,1},{3,0},{4,7},{5,6},{6,5},{7,4},{8,11},{9,10},{10,... | collective-permute-start | bytes 147464 | tf_op jit(solution)/shard_map/ppermute | solution.py:585
  21.0 1.4 %collective-permute-start.3 = (f32[192,128]{1,0:T(8,128)S(1)}, f32[192,128]{1,0:T(8,128)S(1)}, u32[]{:S(2)}, u32[]{:S(2)}) collective-permute-start(f32[192,128]{1,0:T(8,128)S(1)} %constant_dynamic-slice_fusion.6), channel_id=1, source_target_pairs={{0,4},{4,0},{8,12},{12,8},{16,20},{20,16},{24,28},{28,24},{1,5},{5... | collective-permute-start | bytes 294920 | tf_op jit(solution)/shard_map/ppermute | solution.py:585
  22.4 5.3 %collective-permute-start.6 = (f32[96,128]{1,0:T(8,128)S(1)}, f32[96,128]{1,0:T(8,128)S(1)}, u32[]{:S(2)}, u32[]{:S(2)}) collective-permute-start(f32[96,128]{1,0:T(8,128)S(1)} %get-tuple-element.53), channel_id=1, source_target_pairs={{0,24},{4,28},{8,16},{12,20},{16,8},{20,12},{24,0},{28,4},{1,25},{... | collective-permute-start | bytes 147464 | tf_op jit(solution)/shard_map/ppermute | solution.py:585
  25.0 4.6 %collective-permute-start.4 = (f32[96,128]{1,0:T(8,128)S(1)}, f32[96,128]{1,0:T(8,128)S(1)}, u32[]{:S(2)}, u32[]{:S(2)}) collective-permute-start(f32[96,128]{1,0:T(8,128)S(1)} %get-tuple-element.53), channel_id=1, source_target_pairs={{0,8},{4,12},{8,0},{12,4},{16,24},{20,28},{24,16},{28,20},{1,9},{5... | collective-permute-start | bytes 147464 | tf_op jit(solution)/shard_map/ppermute | solution.py:585
  25.5 4.1 %collective-permute-start.5 = (f32[96,128]{1,0:T(8,128)S(1)}, f32[96,128]{1,0:T(8,128)S(1)}, u32[]{:S(2)}, u32[]{:S(2)}) collective-permute-start(f32[96,128]{1,0:T(8,128)S(1)} %get-tuple-element.52), channel_id=1, source_target_pairs={{0,16},{4,20},{8,24},{12,28},{16,0},{20,4},{24,8},{28,12},{1,17},{... | collective-permute-start | bytes 147464 | tf_op jit(solution)/shard_map/ppermute | solution.py:585
  29.6 4.6 %collective-permute-start.9 = (f32[108,128]{1,0:T(8,128)S(1)}, f32[108,128]{1,0:T(8,128)S(1)}, u32[]{:S(2)}, u32[]{:S(2)}) collective-permute-start(f32[108,128]{1,0:T(8,128)S(1)} %get-tuple-element.56), channel_id=1, source_target_pairs={{0,3},{1,0},{2,1},{3,2},{4,7},{5,4},{6,5},{7,6},{8,11},{9,8},{10,9... | collective-permute-start | bytes 165896 | tf_op jit(solution)/shard_map/ppermute | solution.py:589
  30.4 5.1 %collective-permute-start.8 = (f32[108,128]{1,0:T(8,128)S(1)}, f32[108,128]{1,0:T(8,128)S(1)}, u32[]{:S(2)}, u32[]{:S(2)}) collective-permute-start(f32[108,128]{1,0:T(8,128)S(1)} %get-tuple-element.55), channel_id=1, source_target_pairs={{0,2},{1,3},{2,0},{3,1},{4,6},{5,7},{6,4},{7,5},{8,10},{9,11},{10,... | collective-permute-start | bytes 165896 | tf_op jit(solution)/shard_map/ppermute | solution.py:589
  30.4 6.4 %collective-permute-start.7 = (f32[108,128]{1,0:T(8,128)S(1)}, f32[108,128]{1,0:T(8,128)S(1)}, u32[]{:S(2)}, u32[]{:S(2)}) collective-permute-start(f32[108,128]{1,0:T(8,128)S(1)} %get-tuple-element.54), channel_id=1, source_target_pairs={{0,1},{1,2},{2,3},{3,0},{4,5},{5,6},{6,7},{7,4},{8,9},{9,10},{10,1... | collective-permute-start | bytes 165896 | tf_op jit(solution)/shard_map/ppermute | solution.py:589
  36.8 4.2 %collective-permute-start.10 = (f32[96,128]{1,0:T(8,128)S(1)}, f32[96,128]{1,0:T(8,128)S(1)}, u32[]{:S(2)}, u32[]{:S(2)}) collective-permute-start(f32[96,128]{1,0:T(8,128)S(1)} %slice_add_fusion), channel_id=1, source_target_pairs={{0,8},{4,12},{8,0},{12,4},{16,24},{20,28},{24,16},{28,20},{1,9},{5... | collective-permute-start | bytes 147464 | tf_op jit(solution)/shard_map/ppermute | solution.py:585
  41.0 1.4 %collective-permute-start.11 = (f32[192,128]{1,0:T(8,128)S(1)}, f32[192,128]{1,0:T(8,128)S(1)}, u32[]{:S(2)}, u32[]{:S(2)}) collective-permute-start(f32[192,128]{1,0:T(8,128)S(1)} %maximum_select_fusion.refs_0_), channel_id=1, source_target_pairs={{0,4},{4,0},{8,12},{12,8},{16,20},{20,16},{24,28},{28,24},{1,5},{5... | collective-permute-start | bytes 294920 | tf_op jit(solution)/shard_map/ppermute | solution.py:585

commit v3 on v2

--- a/solution.py
+++ b/solution.py
@@ -447,6 +447,11 @@
         for tile in range(own_tiles):
             mean_out[band, tile] = four[:, tile * LANES : (tile + 1) * LANES]
 
+    acc_up[...] = jnp.zeros_like(acc_up)
+    acc_down[...] = jnp.zeros_like(acc_down)
+    acc_mid[...] = jnp.zeros_like(acc_mid)
+    acc_in[...] = jnp.zeros_like(acc_in)
+
     def join_back(index):
         for par in range(2):
             row = 2 * index + par
@@ -464,6 +469,11 @@
 
     looped(coarse // 2, 2 if many else coarse // 2, join_back)
 
+    def weights_up(row):
+        acc_up[...] += dot_lanes(gp4m[pl.ds(row, 3)].reshape(192, half), zj[row + 1])
+
+    looped(rows, 4 if many else rows, weights_up)
+
     def mid_back(group):
         for par in range(2):
             back = dot(wmf[...], zg3[par, pl.ds(4 * group, 6)].reshape(576, half))
@@ -475,6 +485,12 @@
 
     looped(coarse // 8, 1, mid_back)
 
+    def weights_mid(index):
+        for par in range(2):
+            acc_mid[...] += dot_lanes(gp3m[par, pl.ds(index, 3)].reshape(96, half), z2[par, index + 1])
+
+    looped(coarse // 2, 4 if many else coarse // 2, weights_mid)
+
     def down_back(pair):
         back = dot(wbd[...], zg2[pl.ds(2 * pair, 4)].reshape(384, half))
         for out in range(4):
@@ -484,27 +500,18 @@
 
     looped(coarse // 2, 2 if many else coarse // 2, down_back)
 
-    acc_up[...] = jnp.zeros_like(acc_up)
-    acc_down[...] = jnp.zeros_like(acc_down)
-    acc_mid[...] = jnp.zeros_like(acc_mid)
-    acc_in[...] = jnp.zeros_like(acc_in)
-
-    def weights_fine(row):
-        acc_up[...] += dot_lanes(gp4m[pl.ds(row, 3)].reshape(192, half), zj[row + 1])
+    def weights_down(row):
+        acc_down[...] += dot_lanes(
+            gp2m[pl.ds(row, 3)].reshape(96, half),
+            zj[pl.ds(2 * row + 1, 2), 128:256, :].reshape(256, half),
+        )
+
+    looped(coarse, 4 if many else coarse, weights_down)
+
+    def weights_in(row):
         acc_in[...] += dot_lanes(zf[row + 1], gp1m[pl.ds(row, 3)].reshape(192, half))
 
-    looped(rows, 4 if many else rows, weights_fine)
-
-    def weights_coarse(index):
-        for par in range(2):
-            row = 2 * index + par
-            acc_mid[...] += dot_lanes(gp3m[par, pl.ds(index, 3)].reshape(96, half), z2[par, index + 1])
-            acc_down[...] += dot_lanes(
-                gp2m[pl.ds(row, 3)].reshape(96, half),
-                zj[pl.ds(2 * row + 1, 2), 128:256, :].reshape(256, half),
-            )
-
-    looped(coarse // 2, 4 if many else coarse // 2, weights_coarse)
+    looped(rows, 4 if many else rows, weights_in)
 
     up = acc_up[...]
     for step in range(3):

time: 43.6 us -> 43.5 us (level)
  no operation moved by 1% of the time
where the time goes in v3:
time: 43.5 us; the launch traced here: 43.2 us
  waiting for transfers between devices  17.1 us (39%)
  starting transfers between devices  13.4 us (31%)
  Pallas kernels  11.8 us (27%)
  between operations  0.78 us (2%)
    ppermute x9, waiting for transfers between devices, swapped(): return lax.ppermute(values, axis, [(i, i ^ bits) for i in range(count)])  12.3 us
    ppermute x9, starting transfers between devices, swapped(): return lax.ppermute(values, axis, [(i, i ^ bits) for i in range(count)])  10.9 us
    pallas_call x1, Pallas kernels, local(): pl.pallas_call(functools.partial(network_kernel, sizes), out_shape=(shape...  7.69 us
    ppermute x3, waiting for transfers between devices, shifted(): lax.ppermute(values, axis, [(i, (i + shift) % count) for i in range(count)])  4.77 us
    ppermute x3, starting transfers between devices, shifted(): lax.ppermute(values, axis, [(i, (i + shift) % count) for i in range(count)])  2.44 us
    pallas_call x1, Pallas kernels, local(): pl.pallas_call(functools.partial(early_kernel, sizes), out_shape=(shaped(...  2.21 us
    pallas_call x1, Pallas kernels, local(): pl.pallas_call(functools.partial(pack_kernel, sizes), out_shape=(shaped(p...  0.98 us
    pallas_call x1, Pallas kernels, local(): pl.pallas_call(functools.partial(unpack_kernel, (n_band, own, lon_count))...  0.95 us
  transfers between devices with their start and end apart: 12, of which 10 were waited for; matrix products, arithmetic and copies ran while one was open for 0% of the time, Pallas kernels for 5%

profile of v3, /device:TPU:0, one launch (start us, length us, event | category | flops | bytes accessed | tf_op | source)
XLA Modules:
  0.0 43.2 jit_solution(5444537617287348841)
XLA Ops:
  0.6 1.0 %shard_map.163 = (f32[96,128]{1,0:T(8,128)S(1)}, f32[96,128]{1,0:T(8,128)S(1)}, f32[96,128]{1,0:T(8,128)S(1)}, f32[96,128]{1,0:T(8,128)S(1)}) custom-call(s32[1,24,128]{2,1,0:T(8,128)} %refs_0_.1, s32[1,24,128]{2,1,0:T(8,128)} %refs_1_.1, f32[1,24,128]{2,1,0:T(8,128)} %refs_2_.2, s32[1,24,128]{2,1,0:T(8,128)} %refs_3_.2, s32[1,24]{1,0:T(1,128)} %bitcast.16, ...), custom_call_target="tpu_custom_call" | custom-call | tf_op jit(solution)/shard_map/pallas_call | solution.py:673
  1.6 3.1 %collective-permute-start = (f32[96,128]{1,0:T(8,128)S(1)}, f32[96,128]{1,0:T(8,128)S(1)}, u32[]{:S(2)}, u32[]{:S(2)}) collective-permute-start(f32[96,128]{1,0:T(8,128)S(1)} %get-tuple-element.30), channel_id=1, source_target_pairs={{0,1},{1,0},{2,3},{3,2},{4,5},{5,4},{6,7},{7,6},{8,9},{9,8},{10,11... | collective-permute-start | bytes 147464 | tf_op jit(solution)/shard_map/ppermute | solution.py:592
  4.7 2.6 %collective-permute-start.1 = (f32[96,128]{1,0:T(8,128)S(1)}, f32[96,128]{1,0:T(8,128)S(1)}, u32[]{:S(2)}, u32[]{:S(2)}) collective-permute-start(f32[96,128]{1,0:T(8,128)S(1)} %get-tuple-element.31), channel_id=1, source_target_pairs={{0,2},{1,3},{2,0},{3,1},{4,6},{5,7},{6,4},{7,5},{8,10},{9,11},{10,... | collective-permute-start | bytes 147464 | tf_op jit(solution)/shard_map/ppermute | solution.py:592
  7.3 2.2 %shard_map.164 = (f32[4,192,128]{2,1,0:T(8,128)S(1)}, bf16[4,512,256]{2,1,0:T(8,128)(2,1)S(1)}, bf16[256,192]{1,0:T(8,128)(2,1)S(1)}, bf16[64,768]{1,0:T(8,128)(...) custom-call(f32[96,128]{1,0:T(8,128)S(1)} %get-tuple-element.29.refs, ...), custom_call_target="tpu_custom_call" | custom-call | flops 200000000 | bytes 2000000 | tf_op jit(solution)/shard_map/pallas_call | solution.py:687
  9.5 1.1 %collective-permute-done.1.refs_2_ = f32[96,128]{1,0:T(8,128)S(1)} collective-permute-done((f32[96,128]{1,0:T(8,128)S(1)}, f32[96,128]{1,0:T(8,128)S(1)}, u32[]{:S(2)}, u32[]{:S(2)}) %collective-permute-start.1) | collective-permute-done | bytes 49184 | tf_op jit(solution)/shard_map/ppermute | solution.py:592
  10.6 2.6 %collective-permute-done.2.refs_3_ = f32[96,128]{1,0:T(8,128)S(1)} collective-permute-done((f32[96,128]{1,0:T(8,128)S(1)}, f32[96,128]{1,0:T(8,128)S(1)}, u32[]{:S(2)}, u32[]{:S(2)}) %collective-permute-start.2) | collective-permute-done | bytes 49184 | tf_op jit(solution)/shard_map/ppermute | solution.py:592
  13.2 7.7 %shard_map.165 = (f32[4,192,128]{2,1,0:T(8,128)S(1)}, f32[384,128]{1,0:T(8,128)S(1)}, f32[4,3,4,128]{3,2,1,0:T(4,128)S(1)}) custom-call(f32[96,128]{1,0:T(8,128)S(1)} %get-tuple-element.29.refs_0_, f32[96,128]{1,0:T(8,128)S(1)} %collective-permute-done.refs_1_, f32[96,128]{1,0:T(8,128)S(1)} %collective-permute-done.1.refs_2_, ...), custom_call_target="tpu_custom_call", output_to_operand_aliasing={{0}: (4, {})} | custom-call | flops 4000000000 | bytes 4000000 | tf_op jit(solution)/shard_map/pallas_call | solution.py:722
  20.9 0.1 collective-permute-start.3
  21.0 1.2 %collective-permute-done.3 = f32[192,128]{1,0:T(8,128)S(1)} collective-permute-done((f32[192,128]{1,0:T(8,128)S(1)}, f32[192,128]{1,0:T(8,128)S(1)}, u32[]{:S(2)}, u32[]{:S(2)}) %collective-permute-start.3) | collective-permute-done | bytes 98336 | tf_op jit(solution)/shard_map/ppermute | solution.py:592
  22.3 2.5 %collective-permute-start.6 = (f32[96,128]{1,0:T(8,128)S(1)}, f32[96,128]{1,0:T(8,128)S(1)}, u32[]{:S(2)}, u32[]{:S(2)}) collective-permute-start(f32[96,128]{1,0:T(8,128)S(1)} %get-tuple-element.53), channel_id=1, source_target_pairs={{0,24},{4,28},{8,16},{12,20},{16,8},{20,12},{24,0},{28,4},{1,25},{... | collective-permute-start | bytes 147464 | tf_op jit(solution)/shard_map/ppermute | solution.py:592
  24.8 0.5 %collective-permute-start.4 = (f32[96,128]{1,0:T(8,128)S(1)}, f32[96,128]{1,0:T(8,128)S(1)}, u32[]{:S(2)}, u32[]{:S(2)}) collective-permute-start(f32[96,128]{1,0:T(8,128)S(1)} %get-tuple-element.53), channel_id=1, source_target_pairs={{0,8},{4,12},{8,0},{12,4},{16,24},{20,28},{24,16},{28,20},{1,9},{5... | collective-permute-start | bytes 147464 | tf_op jit(solution)/shard_map/ppermute | solution.py:592
  25.4 0.5 %collective-permute-start.5 = (f32[96,128]{1,0:T(8,128)S(1)}, f32[96,128]{1,0:T(8,128)S(1)}, u32[]{:S(2)}, u32[]{:S(2)}) collective-permute-start(f32[96,128]{1,0:T(8,128)S(1)} %get-tuple-element.52), channel_id=1, source_target_pairs={{0,16},{4,20},{8,24},{12,28},{16,0},{20,4},{24,8},{28,12},{1,17},{... | collective-permute-start | bytes 147464 | tf_op jit(solution)/shard_map/ppermute | solution.py:592
  25.9 1.7 %collective-permute-done.6 = f32[96,128]{1,0:T(8,128)S(1)} collective-permute-done((f32[96,128]{1,0:T(8,128)S(1)}, f32[96,128]{1,0:T(8,128)S(1)}, u32[]{:S(2)}, u32[]{:S(2)}) %collective-permute-start.6) | collective-permute-done | bytes 49184 | tf_op jit(solution)/shard_map/ppermute | solution.py:592
  27.6 1.9 %collective-permute-done.5 = f32[96,128]{1,0:T(8,128)S(1)} collective-permute-done((f32[96,128]{1,0:T(8,128)S(1)}, f32[96,128]{1,0:T(8,128)S(1)}, u32[]{:S(2)}, u32[]{:S(2)}) %collective-permute-start.5) | collective-permute-done | bytes 49184 | tf_op jit(solution)/shard_map/ppermute | solution.py:592
  29.5 0.8 %collective-permute-start.9 = (f32[108,128]{1,0:T(8,128)S(1)}, f32[108,128]{1,0:T(8,128)S(1)}, u32[]{:S(2)}, u32[]{:S(2)}) collective-permute-start(f32[108,128]{1,0:T(8,128)S(1)} %get-tuple-element.56), channel_id=1, source_target_pairs={{0,3},{1,0},{2,1},{3,2},{4,7},{5,4},{6,5},{7,6},{8,11},{9,8},{10,9... | collective-permute-start | bytes 165896 | tf_op jit(solution)/shard_map/ppermute | solution.py:596
  30.3 1.6 %collective-permute-start.7 = (f32[108,128]{1,0:T(8,128)S(1)}, f32[108,128]{1,0:T(8,128)S(1)}, u32[]{:S(2)}, u32[]{:S(2)}) collective-permute-start(f32[108,128]{1,0:T(8,128)S(1)} %get-tuple-element.54), channel_id=1, source_target_pairs={{0,1},{1,2},{2,3},{3,0},{4,5},{5,6},{6,7},{7,4},{8,9},{9,10},{10,1... | collective-permute-start | bytes 165896 | tf_op jit(solution)/shard_map/ppermute | solution.py:596
  31.9 2.1 %collective-permute-done.9 = f32[108,128]{1,0:T(8,128)S(1)} collective-permute-done((f32[108,128]{1,0:T(8,128)S(1)}, f32[108,128]{1,0:T(8,128)S(1)}, u32[]{:S(2)}, u32[]{:S(2)}) %collective-permute-start.9) | collective-permute-done | bytes 55328 | tf_op jit(solution)/shard_map/ppermute | solution.py:596
  34.1 1.3 %collective-permute-done.8 = f32[108,128]{1,0:T(8,128)S(1)} collective-permute-done((f32[108,128]{1,0:T(8,128)S(1)}, f32[108,128]{1,0:T(8,128)S(1)}, u32[]{:S(2)}, u32[]{:S(2)}) %collective-permute-start.8) | collective-permute-done | bytes 55328 | tf_op jit(solution)/shard_map/ppermute | solution.py:596
  35.4 1.3 %collective-permute-done.7 = f32[108,128]{1,0:T(8,128)S(1)} collective-permute-done((f32[108,128]{1,0:T(8,128)S(1)}, f32[108,128]{1,0:T(8,128)S(1)}, u32[]{:S(2)}, u32[]{:S(2)}) %collective-permute-start.7) | collective-permute-done | bytes 55328 | tf_op jit(solution)/shard_map/ppermute | solution.py:596
  36.7 1.6 %collective-permute-start.10 = (f32[96,128]{1,0:T(8,128)S(1)}, f32[96,128]{1,0:T(8,128)S(1)}, u32[]{:S(2)}, u32[]{:S(2)}) collective-permute-start(f32[96,128]{1,0:T(8,128)S(1)} %slice_add_fusion), channel_id=1, source_target_pairs={{0,8},{4,12},{8,0},{12,4},{16,24},{20,28},{24,16},{28,20},{1,9},{5... | collective-permute-start | bytes 147464 | tf_op jit(solution)/shard_map/ppermute | solution.py:592
  38.3 2.6 %collective-permute-done.10 = f32[96,128]{1,0:T(8,128)S(1)} collective-permute-done((f32[96,128]{1,0:T(8,128)S(1)}, f32[96,128]{1,0:T(8,128)S(1)}, u32[]{:S(2)}, u32[]{:S(2)}) %collective-permute-start.10) | collective-permute-done | bytes 49184 | tf_op jit(solution)/shard_map/ppermute | solution.py:592
  40.9 0.1 collective-permute-start.11
  41.0 1.2 %collective-permute-done.11.refs_1_ = f32[192,128]{1,0:T(8,128)S(1)} collective-permute-done((f32[192,128]{1,0:T(8,128)S(1)}, f32[192,128]{1,0:T(8,128)S(1)}, u32[]{:S(2)}, u32[]{:S(2)}) %collective-permute-start.11) | collective-permute-done | bytes 98336 | tf_op jit(solution)/shard_map/ppermute | solution.py:592
  42.3 1.0 %shard_map.166 = (f32[1,4,1440]{2,1,0:T(4,128)}, f32[3,3,8,32]{3,2,1,0:T(8,128)}, f32[4,4,32,32]{3,2,1,0:T(8,128)}, f32[3,3,32,32]{3,2,1,0:T(8,128)}, f32[3,3,32,64]{3,2,1,0:T(8,128)}, /*index=5*/f32[2,32]{1,0:T(2,128)}) custom-call(f32[192,128]{1,0:T(8,128)S(1)} %maximum_select_fusion.refs_0_, f32[192,128]{1,0:T(8,128)S(1)} %collective-permute-done.11.refs_1_, ...), custom_call_target="tpu_custom_call" | custom-call | tf_op jit(solution)/shard_map/pallas_call | solution.py:767
  (21 shorter events, 0.2 us)
Async XLA Ops:
  1.6 7.9 %collective-permute-start = (f32[96,128]{1,0:T(8,128)S(1)}, f32[96,128]{1,0:T(8,128)S(1)}, u32[]{:S(2)}, u32[]{:S(2)}) collective-permute-start(f32[96,128]{1,0:T(8,128)S(1)} %get-tuple-element.30), channel_id=1, source_target_pairs={{0,1},{1,0},{2,3},{3,2},{4,5},{5,4},{6,7},{7,6},{8,9},{9,8},{10,11... | collective-permute-start | bytes 147464 | tf_op jit(solution)/shard_map/ppermute | solution.py:592
  4.7 5.9 %collective-permute-start.1 = (f32[96,128]{1,0:T(8,128)S(1)}, f32[96,128]{1,0:T(8,128)S(1)}, u32[]{:S(2)}, u32[]{:S(2)}) collective-permute-start(f32[96,128]{1,0:T(8,128)S(1)} %get-tuple-element.31), channel_id=1, source_target_pairs={{0,2},{1,3},{2,0},{3,1},{4,6},{5,7},{6,4},{7,5},{8,10},{9,11},{10,... | collective-permute-start | bytes 147464 | tf_op jit(solution)/shard_map/ppermute | solution.py:592
  7.3 5.9 %collective-permute-start.2 = (f32[96,128]{1,0:T(8,128)S(1)}, f32[96,128]{1,0:T(8,128)S(1)}, u32[]{:S(2)}, u32[]{:S(2)}) collective-permute-start(f32[96,128]{1,0:T(8,128)S(1)} %get-tuple-element.32), channel_id=1, source_target_pairs={{0,3},{1,2},{2,1},{3,0},{4,7},{5,6},{6,5},{7,4},{8,11},{9,10},{10,... | collective-permute-start | bytes 147464 | tf_op jit(solution)/shard_map/ppermute | solution.py:592
  20.9 1.4 %collective-permute-start.3 = (f32[192,128]{1,0:T(8,128)S(1)}, f32[192,128]{1,0:T(8,128)S(1)}, u32[]{:S(2)}, u32[]{:S(2)}) collective-permute-start(f32[192,128]{1,0:T(8,128)S(1)} %constant_dynamic-slice_fusion.6), channel_id=1, source_target_pairs={{0,4},{4,0},{8,12},{12,8},{16,20},{20,16},{24,28},{28,24},{1,5},{5... | collective-permute-start | bytes 294920 | tf_op jit(solution)/shard_map/ppermute | solution.py:592
  22.3 5.3 %collective-permute-start.6 = (f32[96,128]{1,0:T(8,128)S(1)}, f32[96,128]{1,0:T(8,128)S(1)}, u32[]{:S(2)}, u32[]{:S(2)}) collective-permute-start(f32[96,128]{1,0:T(8,128)S(1)} %get-tuple-element.53), channel_id=1, source_target_pairs={{0,24},{4,28},{8,16},{12,20},{16,8},{20,12},{24,0},{28,4},{1,25},{... | collective-permute-start | bytes 147464 | tf_op jit(solution)/shard_map/ppermute | solution.py:592
  24.8 4.6 %collective-permute-start.4 = (f32[96,128]{1,0:T(8,128)S(1)}, f32[96,128]{1,0:T(8,128)S(1)}, u32[]{:S(2)}, u32[]{:S(2)}) collective-permute-start(f32[96,128]{1,0:T(8,128)S(1)} %get-tuple-element.53), channel_id=1, source_target_pairs={{0,8},{4,12},{8,0},{12,4},{16,24},{20,28},{24,16},{28,20},{1,9},{5... | collective-permute-start | bytes 147464 | tf_op jit(solution)/shard_map/ppermute | solution.py:592
  25.4 4.1 %collective-permute-start.5 = (f32[96,128]{1,0:T(8,128)S(1)}, f32[96,128]{1,0:T(8,128)S(1)}, u32[]{:S(2)}, u32[]{:S(2)}) collective-permute-start(f32[96,128]{1,0:T(8,128)S(1)} %get-tuple-element.52), channel_id=1, source_target_pairs={{0,16},{4,20},{8,24},{12,28},{16,0},{20,4},{24,8},{28,12},{1,17},{... | collective-permute-start | bytes 147464 | tf_op jit(solution)/shard_map/ppermute | solution.py:592
  29.5 4.6 %collective-permute-start.9 = (f32[108,128]{1,0:T(8,128)S(1)}, f32[108,128]{1,0:T(8,128)S(1)}, u32[]{:S(2)}, u32[]{:S(2)}) collective-permute-start(f32[108,128]{1,0:T(8,128)S(1)} %get-tuple-element.56), channel_id=1, source_target_pairs={{0,3},{1,0},{2,1},{3,2},{4,7},{5,4},{6,5},{7,6},{8,11},{9,8},{10,9... | collective-permute-start | bytes 165896 | tf_op jit(solution)/shard_map/ppermute | solution.py:596
  30.3 5.1 %collective-permute-start.8 = (f32[108,128]{1,0:T(8,128)S(1)}, f32[108,128]{1,0:T(8,128)S(1)}, u32[]{:S(2)}, u32[]{:S(2)}) collective-permute-start(f32[108,128]{1,0:T(8,128)S(1)} %get-tuple-element.55), channel_id=1, source_target_pairs={{0,2},{1,3},{2,0},{3,1},{4,6},{5,7},{6,4},{7,5},{8,10},{9,11},{10,... | collective-permute-start | bytes 165896 | tf_op jit(solution)/shard_map/ppermute | solution.py:596
  30.3 6.4 %collective-permute-start.7 = (f32[108,128]{1,0:T(8,128)S(1)}, f32[108,128]{1,0:T(8,128)S(1)}, u32[]{:S(2)}, u32[]{:S(2)}) collective-permute-start(f32[108,128]{1,0:T(8,128)S(1)} %get-tuple-element.54), channel_id=1, source_target_pairs={{0,1},{1,2},{2,3},{3,0},{4,5},{5,6},{6,7},{7,4},{8,9},{9,10},{10,1... | collective-permute-start | bytes 165896 | tf_op jit(solution)/shard_map/ppermute | solution.py:596
  36.7 4.2 %collective-permute-start.10 = (f32[96,128]{1,0:T(8,128)S(1)}, f32[96,128]{1,0:T(8,128)S(1)}, u32[]{:S(2)}, u32[]{:S(2)}) collective-permute-start(f32[96,128]{1,0:T(8,128)S(1)} %slice_add_fusion), channel_id=1, source_target_pairs={{0,8},{4,12},{8,0},{12,4},{16,24},{20,28},{24,16},{28,20},{1,9},{5... | collective-permute-start | bytes 147464 | tf_op jit(solution)/shard_map/ppermute | solution.py:592
  40.9 1.4 %collective-permute-start.11 = (f32[192,128]{1,0:T(8,128)S(1)}, f32[192,128]{1,0:T(8,128)S(1)}, u32[]{:S(2)}, u32[]{:S(2)}) collective-permute-start(f32[192,128]{1,0:T(8,128)S(1)} %maximum_select_fusion.refs_0_), channel_id=1, source_target_pairs={{0,4},{4,0},{8,12},{12,8},{16,20},{20,16},{24,28},{28,24},{1,5},{5... | collective-permute-start | bytes 294920 | tf_op jit(solution)/shard_map/ppermute | solution.py:592

commit v4 on v3

--- a/solution.py
+++ b/solution.py
@@ -146,14 +146,14 @@
 
 def early_kernel(sizes, *refs):
     n_band, n_blocks, own, lon_count = sizes
-    pay = refs[0]
+    pay, w_in, w_head = refs[:3]
     hist, table, w1, wd, wm, wu, wh, wht, wf, wmf, wbd = refs[6:17]
     bands, hi_pos, lo_pos, t1, td, tm, tu, tf, tmf, tbd = refs[17:27]
-    held, sems = refs[27:32], refs[32]
+    held, sems = refs[27:30], refs[30]
     me = lax.axis_index("band")
-    band_copy = pltpu.make_async_copy(pay.at[pl.ds(3 * n_blocks, 8)], bands, sems.at[5])
+    band_copy = pltpu.make_async_copy(pay.at[pl.ds(3 * n_blocks, 8)], bands, sems.at[3])
     band_copy.start()
-    copies = [pltpu.make_async_copy(refs[1 + k], held[k], sems.at[k]) for k in range(5)]
+    copies = [pltpu.make_async_copy(refs[3 + k], held[k], sems.at[k]) for k in range(3)]
     for copy in copies:
         copy.start()
     place_in = iota((4 * LANES, 2 * LANES), 0)
@@ -170,7 +170,7 @@
 
     for copy in copies:
         copy.wait()
-    w_in, w_down, w_mid, w_up, w_head = held
+    w_down, w_mid, w_up = held
     for held in (t1, tm, tu, tf, tmf, tbd):
         held[...] = jnp.zeros_like(held)
     for row in range(3):
@@ -683,7 +683,7 @@
     pays = [packed[0]] + [swapped(packed[k], "band", n_band, k) for k in range(1, n_band)]
 
     hist_shape = (n_band, hist_tiles * 32, LANES)
-    weights = (jnp.transpose(w_in, (0, 1, 3, 2)), w_down, w_mid, w_up, w_head)
+    weights = (w_down, w_mid, w_up)
     early = pl.pallas_call(
         functools.partial(early_kernel, sizes),
         out_shape=(
@@ -699,7 +699,7 @@
             shaped(128, 576),
             shaped(256, 384),
         ),
-        in_specs=[in_vmem] + [in_hbm] * 5,
+        in_specs=[in_vmem] * 3 + [in_hbm] * 3,
         out_specs=(in_vmem,) * 11,
         scratch_shapes=[
             pltpu.SMEM((8, LANES), F32),
@@ -714,10 +714,10 @@
             vmem(384, 256, dtype=F32),
         ]
         + [vmem(*arg.shape) for arg in weights]
-        + [pltpu.SemaphoreType.DMA((6,))],
+        + [pltpu.SemaphoreType.DMA((4,))],
         compiler_params=pltpu.CompilerParams(vmem_limit_bytes=16 * 1024 * 1024),
         cost_estimate=pl.CostEstimate(flops=200_000_000, bytes_accessed=2_000_000, transcendentals=700_000),
-    )(packed[0], *[in_place(arg) for arg in weights])
+    )(packed[0], jnp.transpose(w_in, (0, 1, 3, 2)), w_head, *[in_place(arg) for arg in weights])
 
     _, grads, mean_tiles = pl.pallas_call(
         functools.partial(network_kernel, sizes),

time: 43.5 us -> 43.5 us (level)
  local copies, waits for them, and re-layouts: 0.11 us -> 0.83 us
  waiting for transfers between devices: 17.1 us -> 16.4 us
    unnamed x2 -> x6, local copies, waits for them, and re-layouts: 0.01 us -> 0.73 us
    ppermute x9, waiting for transfers between devices: 12.3 us -> 11.6 us  [swapped(): return lax.ppermute(values, axis, [(i, i ^ bits) for i in range(count)])]
where the time goes in v4:
time: 43.5 us; the launch traced here: 43.3 us
  waiting for transfers between devices  16.4 us (38%)
  starting transfers between devices  13.4 us (31%)
  Pallas kernels  11.8 us (27%)
  local copies, waits for them, and re-layouts  0.83 us (2%)
  between operations  0.78 us (2%)
    ppermute x9, waiting for transfers between devices, swapped(): return lax.ppermute(values, axis, [(i, i ^ bits) for i in range(count)])  11.6 us
    ppermute x9, starting transfers between devices, swapped(): return lax.ppermute(values, axis, [(i, i ^ bits) for i in range(count)])  10.9 us
    pallas_call x1, Pallas kernels, local(): pl.pallas_call(functools.partial(network_kernel, sizes), out_shape=(shape...  7.69 us
    ppermute x3, waiting for transfers between devices, shifted(): lax.ppermute(values, axis, [(i, (i + shift) % count) for i in range(count)])  4.81 us
    ppermute x3, starting transfers between devices, shifted(): lax.ppermute(values, axis, [(i, (i + shift) % count) for i in range(count)])  2.44 us
    pallas_call x1, Pallas kernels, local(): pl.pallas_call(functools.partial(early_kernel, sizes), out_shape=(shaped(...  2.18 us
    pallas_call x1, Pallas kernels, local(): pl.pallas_call(functools.partial(pack_kernel, sizes), out_shape=(shaped(p...  0.98 us
    pallas_call x1, Pallas kernels, local(): pl.pallas_call(functools.partial(unpack_kernel, (n_band, own, lon_count))...  0.95 us
  transfers between devices with their start and end apart: 12, of which 10 were waited for; matrix products, arithmetic and copies ran while one was open for 0% of the time, Pallas kernels for 5%

profile of v4, /device:TPU:0, one launch (start us, length us, event | category | flops | bytes accessed | tf_op | source)
XLA Modules:
  0.0 43.3 jit_solution(2583859600649751196)
XLA Ops:
  0.6 1.0 %shard_map.163 = (f32[96,128]{1,0:T(8,128)S(1)}, f32[96,128]{1,0:T(8,128)S(1)}, f32[96,128]{1,0:T(8,128)S(1)}, f32[96,128]{1,0:T(8,128)S(1)}) custom-call(s32[1,24,128]{2,1,0:T(8,128)} %refs_0_.1, s32[1,24,128]{2,1,0:T(8,128)} %refs_1_.1, f32[1,24,128]{2,1,0:T(8,128)} %refs_2_.2, s32[1,24,128]{2,1,0:T(8,128)} %refs_3_.2, s32[1,24]{1,0:T(1,128)} %bitcast.17, ...), custom_call_target="tpu_custom_call" | custom-call | tf_op jit(solution)/shard_map/pallas_call | solution.py:673
  1.6 3.1 %collective-permute-start = (f32[96,128]{1,0:T(8,128)S(1)}, f32[96,128]{1,0:T(8,128)S(1)}, u32[]{:S(2)}, u32[]{:S(2)}) collective-permute-start(f32[96,128]{1,0:T(8,128)S(1)} %get-tuple-element.30), channel_id=1, source_target_pairs={{0,1},{1,0},{2,3},{3,2},{4,5},{5,4},{6,7},{7,6},{8,9},{9,8},{10,11... | collective-permute-start | bytes 147464 | tf_op jit(solution)/shard_map/ppermute | solution.py:592
  4.7 2.6 %collective-permute-start.1 = (f32[96,128]{1,0:T(8,128)S(1)}, f32[96,128]{1,0:T(8,128)S(1)}, u32[]{:S(2)}, u32[]{:S(2)}) collective-permute-start(f32[96,128]{1,0:T(8,128)S(1)} %get-tuple-element.31), channel_id=1, source_target_pairs={{0,2},{1,3},{2,0},{3,1},{4,6},{5,7},{6,4},{7,5},{8,10},{9,11},{10,... | collective-permute-start | bytes 147464 | tf_op jit(solution)/shard_map/ppermute | solution.py:592
  7.3 0.7 %copy-done = bf16[3,3,32,8]{2,3,1,0:T(8,128)(2,1)S(1)} copy-done((bf16[3,3,32,8]{2,3,1,0:T(8,128)(2,1)S(1)}, bf16[3,3,32,8]{2,3,1,0:T(8,128)(2,1)}, u32[]{:S(2)}) %copy-start) | copy-done | bytes 4632
  8.0 2.2 %shard_map.164 = (f32[4,192,128]{2,1,0:T(8,128)S(1)}, bf16[4,512,256]{2,1,0:T(8,128)(2,1)S(1)}, bf16[256,192]{1,0:T(8,128)(2,1)S(1)}, bf16[64,768]{1,0:T(8,128)(...) custom-call(f32[96,128]{1,0:T(8,128)S(1)} %get-tuple-element.29.refs, ...), custom_call_target="tpu_custom_call" | custom-call | flops 200000000 | bytes 2000000 | tf_op jit(solution)/shard_map/pallas_call | solution.py:687
  10.2 0.4 collective-permute-done.1.refs_2_
  10.6 2.6 %collective-permute-done.2.refs_3_ = f32[96,128]{1,0:T(8,128)S(1)} collective-permute-done((f32[96,128]{1,0:T(8,128)S(1)}, f32[96,128]{1,0:T(8,128)S(1)}, u32[]{:S(2)}, u32[]{:S(2)}) %collective-permute-start.2) | collective-permute-done | bytes 49184 | tf_op jit(solution)/shard_map/ppermute | solution.py:592
  13.2 7.7 %shard_map.165 = (f32[4,192,128]{2,1,0:T(8,128)S(1)}, f32[384,128]{1,0:T(8,128)S(1)}, f32[4,3,4,128]{3,2,1,0:T(4,128)S(1)}) custom-call(f32[96,128]{1,0:T(8,128)S(1)} %get-tuple-element.29.refs_0_, f32[96,128]{1,0:T(8,128)S(1)} %collective-permute-done.refs_1_, f32[96,128]{1,0:T(8,128)S(1)} %collective-permute-done.1.refs_2_, ...), custom_call_target="tpu_custom_call", output_to_operand_aliasing={{0}: (4, {})} | custom-call | flops 4000000000 | bytes 4000000 | tf_op jit(solution)/shard_map/pallas_call | solution.py:722
  21.0 1.2 %collective-permute-done.3 = f32[192,128]{1,0:T(8,128)S(1)} collective-permute-done((f32[192,128]{1,0:T(8,128)S(1)}, f32[192,128]{1,0:T(8,128)S(1)}, u32[]{:S(2)}, u32[]{:S(2)}) %collective-permute-start.3) | collective-permute-done | bytes 98336 | tf_op jit(solution)/shard_map/ppermute | solution.py:592
  22.3 2.5 %collective-permute-start.6 = (f32[96,128]{1,0:T(8,128)S(1)}, f32[96,128]{1,0:T(8,128)S(1)}, u32[]{:S(2)}, u32[]{:S(2)}) collective-permute-start(f32[96,128]{1,0:T(8,128)S(1)} %get-tuple-element.53), channel_id=1, source_target_pairs={{0,24},{4,28},{8,16},{12,20},{16,8},{20,12},{24,0},{28,4},{1,25},{... | collective-permute-start | bytes 147464 | tf_op jit(solution)/shard_map/ppermute | solution.py:592
  24.8 0.5 %collective-permute-start.4 = (f32[96,128]{1,0:T(8,128)S(1)}, f32[96,128]{1,0:T(8,128)S(1)}, u32[]{:S(2)}, u32[]{:S(2)}) collective-permute-start(f32[96,128]{1,0:T(8,128)S(1)} %get-tuple-element.53), channel_id=1, source_target_pairs={{0,8},{4,12},{8,0},{12,4},{16,24},{20,28},{24,16},{28,20},{1,9},{5... | collective-permute-start | bytes 147464 | tf_op jit(solution)/shard_map/ppermute | solution.py:592
  25.4 0.5 %collective-permute-start.5 = (f32[96,128]{1,0:T(8,128)S(1)}, f32[96,128]{1,0:T(8,128)S(1)}, u32[]{:S(2)}, u32[]{:S(2)}) collective-permute-start(f32[96,128]{1,0:T(8,128)S(1)} %get-tuple-element.52), channel_id=1, source_target_pairs={{0,16},{4,20},{8,24},{12,28},{16,0},{20,4},{24,8},{28,12},{1,17},{... | collective-permute-start | bytes 147464 | tf_op jit(solution)/shard_map/ppermute | solution.py:592
  25.9 1.7 %collective-permute-done.6 = f32[96,128]{1,0:T(8,128)S(1)} collective-permute-done((f32[96,128]{1,0:T(8,128)S(1)}, f32[96,128]{1,0:T(8,128)S(1)}, u32[]{:S(2)}, u32[]{:S(2)}) %collective-permute-start.6) | collective-permute-done | bytes 49184 | tf_op jit(solution)/shard_map/ppermute | solution.py:592
  27.6 1.9 %collective-permute-done.5 = f32[96,128]{1,0:T(8,128)S(1)} collective-permute-done((f32[96,128]{1,0:T(8,128)S(1)}, f32[96,128]{1,0:T(8,128)S(1)}, u32[]{:S(2)}, u32[]{:S(2)}) %collective-permute-start.5) | collective-permute-done | bytes 49184 | tf_op jit(solution)/shard_map/ppermute | solution.py:592
  29.5 0.9 %collective-permute-start.9 = (f32[108,128]{1,0:T(8,128)S(1)}, f32[108,128]{1,0:T(8,128)S(1)}, u32[]{:S(2)}, u32[]{:S(2)}) collective-permute-start(f32[108,128]{1,0:T(8,128)S(1)} %get-tuple-element.56), channel_id=1, source_target_pairs={{0,3},{1,0},{2,1},{3,2},{4,7},{5,4},{6,5},{7,6},{8,11},{9,8},{10,9... | collective-permute-start | bytes 165896 | tf_op jit(solution)/shard_map/ppermute | solution.py:596
  30.4 1.5 %collective-permute-start.7 = (f32[108,128]{1,0:T(8,128)S(1)}, f32[108,128]{1,0:T(8,128)S(1)}, u32[]{:S(2)}, u32[]{:S(2)}) collective-permute-start(f32[108,128]{1,0:T(8,128)S(1)} %get-tuple-element.54), channel_id=1, source_target_pairs={{0,1},{1,2},{2,3},{3,0},{4,5},{5,6},{6,7},{7,4},{8,9},{9,10},{10,1... | collective-permute-start | bytes 165896 | tf_op jit(solution)/shard_map/ppermute | solution.py:596
  31.9 2.1 %collective-permute-done.9 = f32[108,128]{1,0:T(8,128)S(1)} collective-permute-done((f32[108,128]{1,0:T(8,128)S(1)}, f32[108,128]{1,0:T(8,128)S(1)}, u32[]{:S(2)}, u32[]{:S(2)}) %collective-permute-start.9) | collective-permute-done | bytes 55328 | tf_op jit(solution)/shard_map/ppermute | solution.py:596
  34.1 1.5 %collective-permute-done.8 = f32[108,128]{1,0:T(8,128)S(1)} collective-permute-done((f32[108,128]{1,0:T(8,128)S(1)}, f32[108,128]{1,0:T(8,128)S(1)}, u32[]{:S(2)}, u32[]{:S(2)}) %collective-permute-start.8) | collective-permute-done | bytes 55328 | tf_op jit(solution)/shard_map/ppermute | solution.py:596
  35.5 1.2 %collective-permute-done.7 = f32[108,128]{1,0:T(8,128)S(1)} collective-permute-done((f32[108,128]{1,0:T(8,128)S(1)}, f32[108,128]{1,0:T(8,128)S(1)}, u32[]{:S(2)}, u32[]{:S(2)}) %collective-permute-start.7) | collective-permute-done | bytes 55328 | tf_op jit(solution)/shard_map/ppermute | solution.py:596
  36.8 1.5 %collective-permute-start.10 = (f32[96,128]{1,0:T(8,128)S(1)}, f32[96,128]{1,0:T(8,128)S(1)}, u32[]{:S(2)}, u32[]{:S(2)}) collective-permute-start(f32[96,128]{1,0:T(8,128)S(1)} %slice_add_fusion), channel_id=1, source_target_pairs={{0,8},{4,12},{8,0},{12,4},{16,24},{20,28},{24,16},{28,20},{1,9},{5... | collective-permute-start | bytes 147464 | tf_op jit(solution)/shard_map/ppermute | solution.py:592
  38.3 2.6 %collective-permute-done.10 = f32[96,128]{1,0:T(8,128)S(1)} collective-permute-done((f32[96,128]{1,0:T(8,128)S(1)}, f32[96,128]{1,0:T(8,128)S(1)}, u32[]{:S(2)}, u32[]{:S(2)}) %collective-permute-start.10) | collective-permute-done | bytes 49184 | tf_op jit(solution)/shard_map/ppermute | solution.py:592
  40.9 0.1 collective-permute-start.11
  41.1 1.2 %collective-permute-done.11.refs_1_ = f32[192,128]{1,0:T(8,128)S(1)} collective-permute-done((f32[192,128]{1,0:T(8,128)S(1)}, f32[192,128]{1,0:T(8,128)S(1)}, u32[]{:S(2)}, u32[]{:S(2)}) %collective-permute-start.11) | collective-permute-done | bytes 98336 | tf_op jit(solution)/shard_map/ppermute | solution.py:592
  42.3 1.0 %shard_map.166 = (f32[1,4,1440]{2,1,0:T(4,128)}, f32[3,3,8,32]{3,2,1,0:T(8,128)}, f32[4,4,32,32]{3,2,1,0:T(8,128)}, f32[3,3,32,32]{3,2,1,0:T(8,128)}, f32[3,3,32,64]{3,2,1,0:T(8,128)}, /*index=5*/f32[2,32]{1,0:T(2,128)}) custom-call(f32[192,128]{1,0:T(8,128)S(1)} %maximum_select_fusion.refs_0_, f32[192,128]{1,0:T(8,128)S(1)} %collective-permute-done.11.refs_1_, ...), custom_call_target="tpu_custom_call" | custom-call | tf_op jit(solution)/shard_map/pallas_call | solution.py:767
  (25 shorter events, 0.3 us)
Async XLA Ops:
  1.6 8.6 %collective-permute-start = (f32[96,128]{1,0:T(8,128)S(1)}, f32[96,128]{1,0:T(8,128)S(1)}, u32[]{:S(2)}, u32[]{:S(2)}) collective-permute-start(f32[96,128]{1,0:T(8,128)S(1)} %get-tuple-element.30), channel_id=1, source_target_pairs={{0,1},{1,0},{2,3},{3,2},{4,5},{5,4},{6,7},{7,6},{8,9},{9,8},{10,11... | collective-permute-start | bytes 147464 | tf_op jit(solution)/shard_map/ppermute | solution.py:592
  4.7 5.9 %collective-permute-start.1 = (f32[96,128]{1,0:T(8,128)S(1)}, f32[96,128]{1,0:T(8,128)S(1)}, u32[]{:S(2)}, u32[]{:S(2)}) collective-permute-start(f32[96,128]{1,0:T(8,128)S(1)} %get-tuple-element.31), channel_id=1, source_target_pairs={{0,2},{1,3},{2,0},{3,1},{4,6},{5,7},{6,4},{7,5},{8,10},{9,11},{10,... | collective-permute-start | bytes 147464 | tf_op jit(solution)/shard_map/ppermute | solution.py:592
  7.3 5.9 %collective-permute-start.2 = (f32[96,128]{1,0:T(8,128)S(1)}, f32[96,128]{1,0:T(8,128)S(1)}, u32[]{:S(2)}, u32[]{:S(2)}) collective-permute-start(f32[96,128]{1,0:T(8,128)S(1)} %get-tuple-element.32), channel_id=1, source_target_pairs={{0,3},{1,2},{2,1},{3,0},{4,7},{5,6},{6,5},{7,4},{8,11},{9,10},{10,... | collective-permute-start | bytes 147464 | tf_op jit(solution)/shard_map/ppermute | solution.py:592
  7.3 0.7 %copy-start = (bf16[3,3,32,8]{2,3,1,0:T(8,128)(2,1)S(1)}, bf16[3,3,32,8]{2,3,1,0:T(8,128)(2,1)}, u32[]{:S(2)}) copy-start(bf16[3,3,32,8]{2,3,1,0:T(8,128)(2,1)} %param.19) | copy-start | bytes 13828
  7.3 0.7 %copy-start.1 = (bf16[2,32]{1,0:T(2,128)(2,1)S(1)}, bf16[2,32]{1,0:T(2,128)(2,1)}, u32[]{:S(2)}) copy-start(bf16[2,32]{1,0:T(2,128)(2,1)} %refs_2_.3) | copy-start | bytes 388
  20.9 1.4 %collective-permute-start.3 = (f32[192,128]{1,0:T(8,128)S(1)}, f32[192,128]{1,0:T(8,128)S(1)}, u32[]{:S(2)}, u32[]{:S(2)}) collective-permute-start(f32[192,128]{1,0:T(8,128)S(1)} %constant_dynamic-slice_fusion.6), channel_id=1, source_target_pairs={{0,4},{4,0},{8,12},{12,8},{16,20},{20,16},{24,28},{28,24},{1,5},{5... | collective-permute-start | bytes 294920 | tf_op jit(solution)/shard_map/ppermute | solution.py:592
  22.3 5.3 %collective-permute-start.6 = (f32[96,128]{1,0:T(8,128)S(1)}, f32[96,128]{1,0:T(8,128)S(1)}, u32[]{:S(2)}, u32[]{:S(2)}) collective-permute-start(f32[96,128]{1,0:T(8,128)S(1)} %get-tuple-element.53), channel_id=1, source_target_pairs={{0,24},{4,28},{8,16},{12,20},{16,8},{20,12},{24,0},{28,4},{1,25},{... | collective-permute-start | bytes 147464 | tf_op jit(solution)/shard_map/ppermute | solution.py:592
  24.8 4.6 %collective-permute-start.4 = (f32[96,128]{1,0:T(8,128)S(1)}, f32[96,128]{1,0:T(8,128)S(1)}, u32[]{:S(2)}, u32[]{:S(2)}) collective-permute-start(f32[96,128]{1,0:T(8,128)S(1)} %get-tuple-element.53), channel_id=1, source_target_pairs={{0,8},{4,12},{8,0},{12,4},{16,24},{20,28},{24,16},{28,20},{1,9},{5... | collective-permute-start | bytes 147464 | tf_op jit(solution)/shard_map/ppermute | solution.py:592
  25.4 4.1 %collective-permute-start.5 = (f32[96,128]{1,0:T(8,128)S(1)}, f32[96,128]{1,0:T(8,128)S(1)}, u32[]{:S(2)}, u32[]{:S(2)}) collective-permute-start(f32[96,128]{1,0:T(8,128)S(1)} %get-tuple-element.52), channel_id=1, source_target_pairs={{0,16},{4,20},{8,24},{12,28},{16,0},{20,4},{24,8},{28,12},{1,17},{... | collective-permute-start | bytes 147464 | tf_op jit(solution)/shard_map/ppermute | solution.py:592
  29.5 4.6 %collective-permute-start.9 = (f32[108,128]{1,0:T(8,128)S(1)}, f32[108,128]{1,0:T(8,128)S(1)}, u32[]{:S(2)}, u32[]{:S(2)}) collective-permute-start(f32[108,128]{1,0:T(8,128)S(1)} %get-tuple-element.56), channel_id=1, source_target_pairs={{0,3},{1,0},{2,1},{3,2},{4,7},{5,4},{6,5},{7,6},{8,11},{9,8},{10,9... | collective-permute-start | bytes 165896 | tf_op jit(solution)/shard_map/ppermute | solution.py:596
  30.4 5.1 %collective-permute-start.8 = (f32[108,128]{1,0:T(8,128)S(1)}, f32[108,128]{1,0:T(8,128)S(1)}, u32[]{:S(2)}, u32[]{:S(2)}) collective-permute-start(f32[108,128]{1,0:T(8,128)S(1)} %get-tuple-element.55), channel_id=1, source_target_pairs={{0,2},{1,3},{2,0},{3,1},{4,6},{5,7},{6,4},{7,5},{8,10},{9,11},{10,... | collective-permute-start | bytes 165896 | tf_op jit(solution)/shard_map/ppermute | solution.py:596
  30.4 6.3 %collective-permute-start.7 = (f32[108,128]{1,0:T(8,128)S(1)}, f32[108,128]{1,0:T(8,128)S(1)}, u32[]{:S(2)}, u32[]{:S(2)}) collective-permute-start(f32[108,128]{1,0:T(8,128)S(1)} %get-tuple-element.54), channel_id=1, source_target_pairs={{0,1},{1,2},{2,3},{3,0},{4,5},{5,6},{6,7},{7,4},{8,9},{9,10},{10,1... | collective-permute-start | bytes 165896 | tf_op jit(solution)/shard_map/ppermute | solution.py:596
  36.8 4.2 %collective-permute-start.10 = (f32[96,128]{1,0:T(8,128)S(1)}, f32[96,128]{1,0:T(8,128)S(1)}, u32[]{:S(2)}, u32[]{:S(2)}) collective-permute-start(f32[96,128]{1,0:T(8,128)S(1)} %slice_add_fusion), channel_id=1, source_target_pairs={{0,8},{4,12},{8,0},{12,4},{16,24},{20,28},{24,16},{28,20},{1,9},{5... | collective-permute-start | bytes 147464 | tf_op jit(solution)/shard_map/ppermute | solution.py:592
  40.9 1.4 %collective-permute-start.11 = (f32[192,128]{1,0:T(8,128)S(1)}, f32[192,128]{1,0:T(8,128)S(1)}, u32[]{:S(2)}, u32[]{:S(2)}) collective-permute-start(f32[192,128]{1,0:T(8,128)S(1)} %maximum_select_fusion.refs_0_), channel_id=1, source_target_pairs={{0,4},{4,0},{8,12},{12,8},{16,20},{20,16},{24,28},{28,24},{1,5},{5... | collective-permute-start | bytes 294920 | tf_op jit(solution)/shard_map/ppermute | solution.py:592
